TPU v7x, 512 devices: a whole 4x4x16 slice. The times are simulated.
512 devices in a mesh: seq: 64 (over y_lo, z, core), chan: 8 (over y_hi, x).
Axes of the slice: x: 4, y: 4 (y_hi: 2, y_lo: 2; y = y_hi * 2 + y_lo), z: 16, core: 2. Of those that a mesh axis runs over, the one named last changes fastest.
Arguments:
- inputs: float32 [768, 131072], P('chan', 'seq'), may hold values from -6 to 6
- cotangent: float32 [768, 131072], P('chan', 'seq'), may hold values from -6 to 6
- kernel: float32 [768, 256, 512], P('chan', 'seq'), may hold values from -6 to 6
- inner_weight: bfloat16 [256, 256], replicated, may hold values from -0.375 to 0.375
- outer_weight: bfloat16 [512, 512], replicated, may hold values from -0.25 to 0.25
- position_diagonal_scaling: float32 [512, 256], P('seq'), may hold values from -4 to 4
- up_weight: bfloat16 [3072, 96], P('chan'), may hold values from -0.625 to 0.625
- down_weight: bfloat16 [768, 384], P('chan'), may hold values from -0.3125 to 0.3125
Outputs:
- grad_inputs: float32 [768, 131072], P('chan', 'seq')
- grad_kernel: float32 [768, 256, 512], P('chan', 'seq')
- grad_up: float32 [3072, 96], P('chan')
- grad_down: float32 [768, 384], P('chan')
- grad_twiddle: float32 [512, 256], P('seq')
All inputs are finite; a program needn't handle non-finite values.
Results may differ from a plain program's by a relative error of at most 0.012.
Values may be sent and summed in bfloat16 or wider, within the bound.
No kernel may reach another device: no remote copies, remote signals or barrier semaphores. Data moves between devices by JAX's collectives and lax.ppermute only.
A program may use at most 64 MiB of HBM per device.

v0:
```python
import math

import jax
import jax.numpy as jnp
from jax import lax
from jax.sharding import PartitionSpec as P

D = 768
HID = 3072
NBLK = 8
INNER = 256
SEQ = 131072


finest_accuracy_setting = lax.Precision.HIGHEST


def gelu_slope(hidden):
    cumulative = 0.5 * (1.0 + lax.erf(hidden * (1.0 / math.sqrt(2.0))))
    density = jnp.exp(-0.5 * hidden * hidden) * (1.0 / math.sqrt(2.0 * math.pi))
    return cumulative + hidden * density


def to_columns(blocked, outer_full):
    return jnp.einsum(
        "pa,cab->cbp",
        outer_full,
        lax.all_to_all(blocked, "seq", split_axis=2, concat_axis=1, tiled=True),
        precision=finest_accuracy_setting,
    )


def to_rows(blocked, middle_full_operator, rotation_rows):
    token_segment = lax.all_to_all(blocked, "seq", split_axis=2, concat_axis=1, tiled=True)
    return (
        token_segment,
        jnp.einsum(
            "wf,xwk->xkf",
            middle_full_operator,
            rotation_rows * token_segment,
            precision=finest_accuracy_setting,
        ),
    )


def regroup(values):
    return lax.all_to_all(values, "chan", split_axis=1, concat_axis=0, tiled=True)


def on_device(
    inputs,
    cotangent,
    kernel,
    inner_weight,
    outer_weight,
    position_diagonal_scaling,
    up_weight,
    down_weight,
):
    middle_full_operator = inner_weight.astype(jnp.float32)
    outer_full = outer_weight.astype(jnp.float32)
    channels, tokens = inputs.shape
    local_rows = position_diagonal_scaling.shape[0]
    block_width = D // NBLK
    block_hidden = HID // NBLK
    slice_rows = block_hidden // NBLK
    rotation_rows = position_diagonal_scaling.T
    blocked = inputs.reshape(channels, local_rows, INNER)
    leading_section = jnp.einsum(
        "pb,cab->cap", middle_full_operator, blocked, precision=finest_accuracy_setting
    )
    spectrum = to_columns(position_diagonal_scaling * leading_section, outer_full)
    yielded_result_array = jnp.einsum(
        "pa,cbp->cba", outer_full, kernel * spectrum, precision=finest_accuracy_setting
    )
    shifted_rows, mixing = to_rows(yielded_result_array, middle_full_operator, rotation_rows)
    mixing = mixing.reshape(channels, tokens)
    gated_full = inputs + inputs * mixing
    gated_low = gated_full.astype(jnp.bfloat16)
    cot_low = cotangent.astype(jnp.bfloat16)
    shared = regroup(gated_low)
    cot_shared = regroup(cot_low)
    up_all, down_all = (
        lax.all_gather(up_weight, "chan", axis=0, tiled=True),
        lax.all_gather(down_weight, "chan", axis=0, tiled=True),
    )
    up_blocks = up_all.reshape(NBLK, block_hidden, block_width)
    shared_blocks = shared.reshape(NBLK, block_width, -1)
    hidden = jnp.einsum(
        "jrc,jct->jrt", up_blocks, shared_blocks, preferred_element_type=jnp.float32
    )
    activation = jax.nn.gelu(hidden, approximate=False).astype(jnp.bfloat16)
    activation = activation.reshape(NBLK, NBLK, slice_rows, -1)
    down_blocks = down_all.reshape(NBLK, block_width, NBLK, slice_rows)
    cot_blocks = cot_shared.reshape(NBLK, block_width, -1)
    full_down = jnp.einsum(
        "pot,jpqt->pojq", cot_blocks, activation, preferred_element_type=jnp.float32
    ).reshape(D, block_hidden)
    grad_act = jnp.einsum(
        "pojq,pot->jpqt", down_blocks, cot_blocks, preferred_element_type=jnp.float32
    ).astype(jnp.bfloat16)
    grad_act = grad_act.reshape(NBLK, block_hidden, -1)
    grad_hidden = (grad_act.astype(jnp.float32) * gelu_slope(hidden)).astype(jnp.bfloat16)
    full_up = jnp.einsum(
        "jrt,jct->jrc", grad_hidden, shared_blocks, preferred_element_type=jnp.float32
    ).reshape(HID, block_width)
    back_shared = jnp.einsum(
        "jrc,jrt->jct", up_blocks, grad_hidden, preferred_element_type=jnp.float32
    ).reshape(D, -1)
    grad_gated = cotangent + lax.all_to_all(
        back_shared, "chan", split_axis=0, concat_axis=1, tiled=True
    )
    grad_up, grad_down = (
        lax.psum_scatter(full_up, "chan", scatter_dimension=0, tiled=True),
        lax.psum_scatter(full_down, "chan", scatter_dimension=0, tiled=True),
    )
    grad_up, grad_down = lax.psum((grad_up, grad_down), "seq")
    grad_scale = 1.0 / math.sqrt(SEQ)
    grad_mix = (grad_gated * inputs).reshape(channels, local_rows, INNER)
    second_factor = jnp.einsum(
        "pb,cab->cap", middle_full_operator, grad_mix, precision=finest_accuracy_setting
    )
    later_product_term = jnp.einsum(
        "xuk,xku->uk", second_factor, shifted_rows, precision=finest_accuracy_setting
    )
    grad_spec = to_columns(position_diagonal_scaling * second_factor, outer_full)
    grad_kernel = grad_spec * spectrum
    sensitivity_yielded_lines = jnp.einsum(
        "pa,cbp->cba", outer_full, kernel * grad_spec, precision=finest_accuracy_setting
    )
    grad_rows, sensitivity_front_operand = to_rows(
        sensitivity_yielded_lines, middle_full_operator, rotation_rows
    )
    early_term = jnp.einsum(
        "ekv,evk->vk", grad_rows, leading_section, precision=finest_accuracy_setting
    )
    grad_twiddle = lax.psum(early_term + later_product_term, "chan") * (1.0 / math.sqrt(D))
    grad_inputs = grad_gated * (1.0 + mixing) + sensitivity_front_operand.reshape(channels, tokens)
    return (grad_inputs, grad_kernel, grad_up * grad_scale, grad_down * grad_scale, grad_twiddle)


def solution(mesh):
    placed = (
        P("chan", "seq"),
        P("chan", "seq"),
        P("chan", "seq", None),
        P(),
        P(),
        P("seq", None),
        P("chan", None),
        P("chan", None),
    )
    return jax.shard_map(
        on_device,
        mesh=mesh,
        in_specs=placed,
        out_specs=(
            P("chan", "seq"),
            P("chan", "seq", None),
            P("chan", None),
            P("chan", None),
            P("seq", None),
        ),
        check_vma=False,
    )
```

profile of v0, /device:TPU:1, one launch (start us, length us, event | category | flops | bytes accessed | tf_op | source)
XLA Modules:
  0.0 898.5 jit_solution(16864442763665151108)
XLA Ops:
  7.2 1.4 copy.154
  8.6 2.4 broadcast_multiply_fusion.1
  11.0 1.4 copy.96
  12.5 18.3 %all-to-all-start.1 = ((f32[96,8,256]{0,1,2:T(8,128)}), f32[96,8,256]{0,1,2:T(8,128)S(1)}, u32[]{:S(2)}, u32[]{:S(2)}) async-start(f32[96,8,256]{0,1,2:T(8,128)} %copy.96), calls=%async_computation.1 | async-start | bytes 2097152 | tf_op jit(solution)/shard_map/all_to_all | solution.py:28
  31.6 49.5 %all-to-all-done.1 = f32[96,8,256]{0,1,2:T(8,128)S(1)} async-done(((f32[96,8,256]{0,1,2:T(8,128)}), f32[96,8,256]{0,1,2:T(8,128)S(1)}, u32[]{:S(2)}, u32[]{:S(2)}) %all-to-all-start.1) | async-done | bytes 786464 | tf_op jit(solution)/shard_map/all_to_all | solution.py:28
  81.1 6.4 all-to-all-start
  87.5 1.8 fusion.30
  92.4 3.4 all-to-all-done
  95.8 12.0 %all-to-all-start.2 = ((f32[96,4,512]{0,1,2:T(4,128)}), f32[96,4,512]{0,1,2:T(4,128)}, u32[]{:S(2)}, u32[]{:S(2)}) async-start(f32[96,4,512]{0,1,2:T(4,128)} %copy.100), calls=%async_computation.2 | async-start | bytes 2097152 | tf_op jit(solution)/shard_map/all_to_all | solution.py:34
  108.7 32.6 %all_gather.6 = bf16[768,384]{1,0:T(8,128)(2,1)} all-gather(bf16[96,384]{1,0:T(8,128)(2,1)S(1)} %copy-done.18), channel_id=1, replica_groups=mesh['seq'=64,'chan'=8] {'chan'}, dimensions={0}, use_global_device_ids=true | all-gather | bytes 663552 | tf_op jit(solution)/shard_map/all_gather | solution.py:85
  141.3 2.5 reshape.78
  143.8 1.6 copy.93
  145.5 31.7 %all_gather.7 = bf16[3072,96]{0,1:T(8,128)(2,1)} all-gather(bf16[384,96]{0,1:T(8,128)(2,1)S(1)} %copy-done.19), channel_id=1, replica_groups=mesh['seq'=64,'chan'=8] {'chan'}, dimensions={0}, use_global_device_ids=true | all-gather | bytes 663552 | tf_op jit(solution)/shard_map/all_gather | solution.py:84
  177.2 3.3 fusion.53
  180.5 1.3 copy.195
  183.3 2.5 copy.103
  185.8 1.6 fusion.59
  189.6 4.3 all-to-all-start.3
  193.8 2.2 convert_bitcast_fusion
  196.1 2.0 copy.94
  198.0 3.5 copy.106
  202.0 11.1 %fusion.8 = (bf16[8,384,256]{1,2,0:T(8,128)(2,1)}, bf16[8,384,256]{1,2,0:T(8,128)(2,1)S(1)}) fusion(f32[8,384,256]{1,2,0:T(8,128)} %copy.106, bf16[12,8,8,384]{3,2,1,0:T(8,128)(2,1)} %bitcast.196, bf16[96,8,256]{2,0,1:T(8,128)(2,1)} %all-to-all-done.3), kind=kOutput, calls=%fused_computation.10 | convolution fusion | flops 209977344 | bytes 7274496 | tf_op jit(solution)/shard_map/jrc,jct->jrt/dot_general | solution.py:89
  213.7 16.2 %all_to_all.120 = f32[8,96,256]{2,1,0:T(8,128)S(1)} all-to-all(f32[8,96,256]{2,1,0:T(8,128)S(1)} %convolution_bitcast_fusion.1), channel_id=1, replica_groups=mesh['seq'=64,'chan'=8] {'chan'}, dimensions={0} | all-to-all | bytes 1572864 | tf_op jit(solution)/shard_map/all_to_all | solution.py:110
  230.8 1.4 broadcast_multiply_fusion
  232.2 1.5 copy.110
  233.7 26.0 %all-to-all-start.5 = ((f32[96,8,256]{0,1,2:T(8,128)}), f32[96,8,256]{0,1,2:T(8,128)}, u32[]{:S(2)}, u32[]{:S(2)}) async-start(f32[96,8,256]{0,1,2:T(8,128)} %copy.110), calls=%async_computation.5 | async-start | bytes 2097152 | tf_op jit(solution)/shard_map/all_to_all | solution.py:28
  259.8 2.6 copy.120
  262.4 3.2 fusion.25
  265.6 3.3 copy.147
  268.8 3.5 reshape.79
  272.4 2.0 convolution_bitcast_fusion
  275.5 34.5 %all-to-all-done.5 = f32[96,8,256]{0,1,2:T(8,128)} async-done(((f32[96,8,256]{0,1,2:T(8,128)}), f32[96,8,256]{0,1,2:T(8,128)}, u32[]{:S(2)}, u32[]{:S(2)}) %all-to-all-start.5) | async-done | bytes 786464 | tf_op jit(solution)/shard_map/all_to_all | solution.py:28
  310.0 4.1 fusion.63
  315.0 1.3 copy.114
  316.3 9.8 %all-to-all-start.6 = ((f32[96,4,512]{0,1,2:T(4,128)}), f32[96,4,512]{0,1,2:T(4,128)}, u32[]{:S(2)}, u32[]{:S(2)}) async-start(f32[96,4,512]{0,1,2:T(4,128)} %copy.114), calls=%async_computation.6 | async-start | bytes 2097152 | tf_op jit(solution)/shard_map/all_to_all | solution.py:34
  326.2 31.9 %reduce-scatter.7.cloned.1.call-done = f32[96,384]{1,0:T(8,128)} async-done(((f32[768,384]{1,0:T(8,128)}), f32[96,384]{1,0:T(8,128)}) %reduce-scatter.7.cloned.1.call-update) | async-done | bytes 147472
  358.1 1.7 copy.146
  359.8 90.0 %reduce-scatter.5.cloned.1.call-done = f32[384,96]{0,1:T(8,128)} async-done(((f32[3072,96]{0,1:T(8,128)}), f32[384,96]{0,1:T(8,128)}) %reduce-scatter.5.cloned.1.call-update) | async-done | bytes 147472 | tf_op jit(solution)/shard_map/reduce_scatter | solution.py:114
  449.8 1.6 copy.141
  451.9 402.3 %all-reduce.3.cloned.1.call-done = (f32[384,96]{0,1:T(8,128)}, f32[96,384]{0,1:T(8,128)}) async-done(((f32[384,96]{0,1:T(8,128)}, f32[96,384]{0,1:T(8,128)}), (f32[384,96]{0,1:T(8,128)}, f32[96,384]{0,1:T(8,128)})) %all-reduce.3.cloned.1.call-update) | async-done | bytes 294928 | tf_op jit(solution)/shard_map/psum | solution.py:117
  855.9 1.6 broadcast_multiply_fusion.3
  857.5 2.5 copy.123
  861.4 1.3 bitcast_multiply_fusion.2
  862.8 1.3 copy.135
  864.1 1.6 multiply_reduce_fusion.1
  865.7 20.1 %psum.23 = f32[8,256]{1,0:T(8,128)S(1)} all-reduce(f32[8,256]{1,0:T(8,128)S(1)} %add.41), channel_id=1, replica_groups=mesh['seq'=64,'chan'=8] {'chan'}, use_global_device_ids=true, to_apply=%region_4.0 | all-reduce | flops 2048 | bytes 16384 | tf_op jit(solution)/shard_map/psum | solution.py:137
  886.4 2.5 copy.117
  888.9 1.6 fusion.55
  (75 shorter events, 18.0 us)
Async XLA Ops:
  7.2 80.3 %copy-start = (bf16[512,512]{1,0:T(8,128)(2,1)S(1)}, bf16[512,512]{1,0:T(8,128)(2,1)}, u32[]{:S(2)}) copy-start(bf16[512,512]{1,0:T(8,128)(2,1)} %param.12) | copy-start | bytes 1572868
  8.6 22.1 %copy-start.2 = (f32[96,2048]{1,0:T(8,128)S(1)}, f32[96,2048]{1,0:T(8,128)}, u32[]{:S(2)}) copy-start(f32[96,2048]{1,0:T(8,128)} %param.9) | copy-start | bytes 2359300
  12.5 77.7 %copy-start.10 = (f32[96,4,512]{2,1,0:T(4,128)S(1)}, f32[96,4,512]{2,1,0:T(4,128)}, u32[]{:S(2)}) copy-start(f32[96,4,512]{2,1,0:T(4,128)} %param.10) | copy-start | bytes 2359300
  12.5 68.7 %all-to-all-start.1 = ((f32[96,8,256]{0,1,2:T(8,128)}), f32[96,8,256]{0,1,2:T(8,128)S(1)}, u32[]{:S(2)}, u32[]{:S(2)}) async-start(f32[96,8,256]{0,1,2:T(8,128)} %copy.96), calls=%async_computation.1 | async-start | bytes 2097152 | tf_op jit(solution)/shard_map/all_to_all | solution.py:28
  81.1 14.7 %all-to-all-start = ((bf16[96,8,256]{2,0,1:T(8,128)(2,1)}), bf16[96,8,256]{2,0,1:T(8,128)(2,1)S(1)}, u32[]{:S(2)}, u32[]{:S(2)}) async-start(bf16[96,8,256]{2,0,1:T(8,128)(2,1)} %bitcast.198), calls=%async_computation | async-start | bytes 786432 | tf_op jit(solution)/shard_map/all_to_all | solution.py:47
  89.3 0.9 copy-start.7
  90.2 17.7 %copy-start.17 = (f32[8,256]{1,0:T(8,128)S(1)}, f32[8,256]{1,0:T(8,128)}, u32[]{:S(2)}) copy-start(f32[8,256]{1,0:T(8,128)} %param.13) | copy-start | bytes 24580
  90.2 18.5 %copy-start.18 = (bf16[96,384]{1,0:T(8,128)(2,1)S(1)}, bf16[96,384]{1,0:T(8,128)(2,1)}, u32[]{:S(2)}) copy-start(bf16[96,384]{1,0:T(8,128)(2,1)} %param.15) | copy-start | bytes 221188
  95.8 84.7 %all-to-all-start.2 = ((f32[96,4,512]{0,1,2:T(4,128)}), f32[96,4,512]{0,1,2:T(4,128)}, u32[]{:S(2)}, u32[]{:S(2)}) async-start(f32[96,4,512]{0,1,2:T(4,128)} %copy.100), calls=%async_computation.2 | async-start | bytes 2097152 | tf_op jit(solution)/shard_map/all_to_all | solution.py:34
  107.9 37.6 %copy-start.19 = (bf16[384,96]{0,1:T(8,128)(2,1)S(1)}, bf16[384,96]{0,1:T(8,128)(2,1)}, u32[]{:S(2)}) copy-start(bf16[384,96]{0,1:T(8,128)(2,1)} %param.14) | copy-start | bytes 221188
  180.5 1.5 copy-start.15
  182.0 6.7 copy-start.1
  187.7 1.0 copy-start.3
  189.6 12.5 %all-to-all-start.3 = ((bf16[96,8,256]{2,0,1:T(8,128)(2,1)}), bf16[96,8,256]{2,0,1:T(8,128)(2,1)}, u32[]{:S(2)}, u32[]{:S(2)}) async-start(bf16[96,8,256]{2,0,1:T(8,128)(2,1)} %bitcast.199), calls=%async_computation.3 | async-start | bytes 786432 | tf_op jit(solution)/shard_map/all_to_all | solution.py:47
  202.0 11.1 %copy-start.12 = (bf16[3072,96]{0,1:T(8,128)(2,1)S(1)}, bf16[3072,96]{0,1:T(8,128)(2,1)}, u32[]{:S(2)}) copy-start(bf16[3072,96]{0,1:T(8,128)(2,1)} %all_gather.7) | copy-start | bytes 1769476
  213.1 17.0 %copy-start.9 = (bf16[8,384,256]{1,2,0:T(8,128)(2,1)}, bf16[8,384,256]{1,2,0:T(8,128)(2,1)S(1)}, u32[]{:S(2)}) copy-start(bf16[8,384,256]{1,2,0:T(8,128)(2,1)S(1)} %get-tuple-element.28) | copy-start | bytes 4718596
  229.9 0.9 copy-start.13
  230.0 2.2 copy-start.5
  233.7 76.2 %all-to-all-start.5 = ((f32[96,8,256]{0,1,2:T(8,128)}), f32[96,8,256]{0,1,2:T(8,128)}, u32[]{:S(2)}, u32[]{:S(2)}) async-start(f32[96,8,256]{0,1,2:T(8,128)} %copy.110), calls=%async_computation.5 | async-start | bytes 2097152 | tf_op jit(solution)/shard_map/all_to_all | solution.py:28
  259.7 98.4 %reduce-scatter.7.cloned.1.call-start = ((), (), s32[]{:S(2)}) async-start(), calls=%async_computation.10 | async-start | bytes 1327104
  272.3 37.7 %copy-start.8 = (f32[96,4,512]{2,0,1:T(8,128)S(1)}, f32[96,4,512]{2,0,1:T(8,128)}, u32[]{:S(2)}) copy-start(f32[96,4,512]{2,0,1:T(8,128)} %copy-done.7) | copy-start | bytes 2359300
  272.3 177.5 %reduce-scatter.5.cloned.1.call-start = ((), (), s32[]{:S(2)}) async-start(), calls=%async_computation.9 | async-start | bytes 1327104 | tf_op jit(solution)/shard_map/reduce_scatter | solution.py:114
  310.0 4.1 copy-start.11
  316.3 543.7 %all-to-all-start.6 = ((f32[96,4,512]{0,1,2:T(4,128)}), f32[96,4,512]{0,1,2:T(4,128)}, u32[]{:S(2)}, u32[]{:S(2)}) async-start(f32[96,4,512]{0,1,2:T(4,128)} %copy.114), calls=%async_computation.6 | async-start | bytes 2097152 | tf_op jit(solution)/shard_map/all_to_all | solution.py:34
  326.2 528.0 %all-reduce.3.cloned.1.call-start = ((), (), s32[]{:S(2)}) async-start(), calls=%async_computation.11 | async-start | bytes 688128 | tf_op jit(solution)/shard_map/psum | solution.py:117
  855.1 6.3 copy-start.16
  862.8 26.2 %copy-start.14 = (bf16[256,256]{1,0:T(8,128)(2,1)S(1)}, bf16[256,256]{1,0:T(8,128)(2,1)}, u32[]{:S(2)}) copy-start(bf16[256,256]{1,0:T(8,128)(2,1)} %param.11) | copy-start | bytes 393220
  864.1 26.7 %copy-start.4 = (f32[12,8,8,256]{3,1,2,0:T(8,128)S(1)}, f32[12,8,8,256]{3,1,2,0:T(8,128)}, u32[]{:S(2)}) copy-start(f32[12,8,8,256]{3,1,2,0:T(8,128)} %copy-done.3) | copy-start | bytes 2359300
  864.1 26.7 %copy-start.6 = (f32[8,12,8,256]{3,2,0,1:T(8,128)S(1)}, f32[8,12,8,256]{3,2,0,1:T(8,128)}, u32[]{:S(2)}) copy-start(f32[8,12,8,256]{3,2,0,1:T(8,128)} %copy-done.5) | copy-start | bytes 2359300
Sparse Core Ops, SparseCore 0:
  272.4 85.6 reduce-scatter.6
  363.4 86.4 reduce-scatter.4
  453.4 400.7 all-reduce.2
where the time goes:
time: 903 us; the launch traced here: 898 us
  waiting for transfers between devices  612 us (68%)
  blocking collectives  101 us (11%)
  starting transfers between devices  76.9 us (9%)
  local copies, waits for them, and re-layouts  48.6 us (5%)
  matrix products  35 us (4%)
  between operations  14.1 us (2%)
  other arithmetic  11.3 us (1%)
    psum x1, waiting for transfers between devices, on_device(): grad_up, grad_down = lax.psum((grad_up, grad_down), 'seq')  402 us
    reduce_scatter x1, waiting for transfers between devices, on_device(): lax.psum_scatter(full_up, 'chan', scatter_dimension=0, tiled=True)  90 us
    all_to_all x2, waiting for transfers between devices, to_columns(): lax.all_to_all(blocked, 'seq', split_axis=2, concat_axis=1, tiled=True)  84 us
    all_to_all x2, starting transfers between devices, to_columns(): lax.all_to_all(blocked, 'seq', split_axis=2, concat_axis=1, tiled=True)  44.3 us
    all_gather x1, blocking collectives, on_device(): lax.all_gather(down_weight, 'chan', axis=0, tiled=True)  32.6 us
    unnamed x4, waiting for transfers between devices  31.9 us
    all_gather x1, blocking collectives, on_device(): lax.all_gather(up_weight, 'chan', axis=0, tiled=True)  31.7 us
    all_to_all x2, starting transfers between devices, to_rows(): lax.all_to_all(blocked, 'seq', split_axis=2, concat_axis=1, tiled=True)  21.9 us
  transfers between devices with their start and end apart: 9, of which 7 were waited for; matrix products, arithmetic and copies ran while one was open for 6% of the time, Pallas kernels for 0%

commit v1 on v0

v1 whole, which is shorter than its diff:
```python
import functools
import math

import jax
import jax.numpy as jnp
from jax import lax
from jax.experimental import pallas as pl
from jax.experimental.pallas import tpu as pltpu
from jax.sharding import PartitionSpec as P

D = 768
HID = 3072
NBLK = 8
OUTER = 512
INNER = 256
SEQ = 131072
BW = D // NBLK
HB = HID // NBLK
SLICE = HB // NBLK
NSEQ = 64
ROWS = OUTER // NSEQ
COLS = INNER // NSEQ
LANES = COLS * BW
TOK = ROWS * INNER
LANE_TILE = 128

f32 = jnp.float32
bf16 = jnp.bfloat16
NT = (((1,), (1,)), ((), ()))
NN = (((1,), (0,)), ((), ()))


def dot(lhs, rhs, dims=NN):
    return lax.dot_general(lhs, rhs, dims, preferred_element_type=f32)


def call(kernel, outs, *operands, flops=0, scratch=(), trans=0):
    shapes = [jax.ShapeDtypeStruct(shape, dtype) for shape, dtype in outs]
    nbytes = sum(math.prod(o.shape) * o.dtype.itemsize for o in list(operands) + shapes)
    return pl.pallas_call(
        kernel,
        out_shape=shapes,
        in_specs=[pl.BlockSpec(memory_space=pltpu.VMEM)] * len(operands),
        out_specs=[pl.BlockSpec(memory_space=pltpu.VMEM)] * len(shapes),
        scratch_shapes=list(scratch),
        cost_estimate=pl.CostEstimate(flops=flops, bytes_accessed=nbytes, transcendentals=trans),
        compiler_params=pltpu.CompilerParams(vmem_limit_bytes=40 * 1024 * 1024),
    )(*operands)


def token_columns(a):
    return slice(a * INNER, (a + 1) * INNER)


def to_message(value, a, turned, stage):
    turned[:, :BW] = value.T
    parts = [turned[pl.ds(b, NSEQ, stride=COLS), :][:, :BW] for b in range(COLS)]
    row = jnp.concatenate(parts, axis=1)
    for k in range(LANES // LANE_TILE):
        stage[k, pl.ds(a, NSEQ, stride=ROWS), :] = row[:, k * LANE_TILE : (k + 1) * LANE_TILE]


def from_message(a, turned, stage):
    row = jnp.concatenate(
        [stage[k, pl.ds(a, NSEQ, stride=ROWS), :] for k in range(LANES // LANE_TILE)], axis=1
    )
    for b in range(COLS):
        turned[pl.ds(b, NSEQ, stride=COLS), :] = jnp.concatenate(
            [row[:, b * BW : (b + 1) * BW], jnp.zeros((NSEQ, LANE_TILE - BW), f32)], axis=1
        )
    return turned[...].T[:BW]


def pack(stage, send_ref):
    for k in range(LANES // LANE_TILE):
        send_ref[:, k * LANE_TILE : (k + 1) * LANE_TILE] = stage[k].astype(bf16)


def unpack(recv_ref, stage):
    for k in range(LANES // LANE_TILE):
        stage[k] = recv_ref[:, k * LANE_TILE : (k + 1) * LANE_TILE].astype(f32)


STAGE = pltpu.VMEM((LANES // LANE_TILE, OUTER, LANE_TILE), f32)
TURNED = pltpu.VMEM((INNER, LANE_TILE), f32)


def rows_in(x_ref, w_ref, tw_ref, send_ref, first_ref, turned, stage):
    w = w_ref[...]
    for a in range(ROWS):
        cols = token_columns(a)
        first = dot(x_ref[:, cols].astype(bf16), w, NT)
        first_ref[:, cols] = first.astype(bf16)
        to_message(first * tw_ref[a : a + 1, :], a, turned, stage)
    pack(stage, send_ref)


def columns(recv_ref, outer_ref, outer_t_ref, kernel_ref, send_ref, spec_ref):
    spec = dot(outer_ref[...], recv_ref[...])
    spec_ref[...] = spec.astype(spec_ref.dtype)
    scaled = (kernel_ref[...].astype(f32) * spec).astype(bf16)
    send_ref[...] = dot(outer_t_ref[...], scaled).astype(bf16)


def mlp(
    recv_ref,
    x_ref,
    cot_ref,
    grad_act_ref,
    w_ref,
    tw_ref,
    up_ref,
    up_t_ref,
    send_ref,
    back_ref,
    low_ref,
    act_ref,
    grad_hidden_ref,
    grad_mix_ref,
    direct_ref,
    turned,
    stage,
    turned_out,
    stage_out,
):
    unpack(recv_ref, stage)
    w = w_ref[...]
    up = up_ref[...]
    up_t = up_t_ref[...]
    for a in range(ROWS):
        cols = token_columns(a)
        twiddle = tw_ref[a : a + 1, :]
        back = from_message(a, turned, stage)
        back_ref[:, cols] = back.astype(bf16)
        mixing = dot((back * twiddle).astype(bf16), w)
        x = x_ref[:, cols]
        low = (x + x * mixing).astype(bf16)
        low_ref[:, cols] = low
        hidden = dot(up, low)
        cumulative = 0.5 * (1.0 + lax.erf(hidden * (1.0 / math.sqrt(2.0))))
        density = jnp.exp(-0.5 * hidden * hidden) * (1.0 / math.sqrt(2.0 * math.pi))
        act_ref[:, cols] = (hidden * cumulative).astype(bf16)
        slope = cumulative + hidden * density
        grad_hidden = (grad_act_ref[:, cols].astype(f32) * slope).astype(bf16)
        grad_hidden_ref[:, cols] = grad_hidden
        grad_gated = cot_ref[:, cols] + dot(up_t, grad_hidden)
        direct_ref[:, cols] = grad_gated * (1.0 + mixing)
        grad_mix = (grad_gated * x).astype(bf16)
        grad_mix_ref[:, cols] = grad_mix
        second = dot(grad_mix, w, NT)
        to_message(second * twiddle, a, turned_out, stage_out)
    pack(stage_out, send_ref)


def hidden_cotangent(shared_ref, out_ref):
    for p in range(NBLK):
        down = shared_ref[p, :, TOK : TOK + LANE_TILE].astype(f32).T[:SLICE].astype(bf16)
        out_ref[p * SLICE : (p + 1) * SLICE, :] = dot(down, shared_ref[p, :, :TOK]).astype(bf16)


def weight_grads(
    grad_hidden_ref, low_ref, act_ref, shared_ref, grad_mix_ref, back_ref, w_ref, up_ref, down_ref, later_ref
):
    zeros = jnp.zeros((HB, LANE_TILE - BW), f32)
    up_ref[...] = jnp.concatenate([dot(grad_hidden_ref[...], low_ref[...], NT), zeros], axis=1).astype(bf16)
    for p in range(NBLK):
        rows = slice(p * SLICE, (p + 1) * SLICE)
        part = dot(act_ref[rows, :], shared_ref[p, :, :TOK], NT)
        down_ref[rows, :] = jnp.concatenate([part, zeros[:SLICE]], axis=1).astype(bf16)
    w = w_ref[...]
    for a in range(ROWS):
        cols = token_columns(a)
        second = dot(grad_mix_ref[:, cols], w, NT)
        later_ref[a : a + 1, :] = jnp.sum(second * back_ref[:, cols].astype(f32), axis=0, keepdims=True)


def rows_out(recv_ref, w_ref, tw_ref, first_ref, direct_ref, later_ref, out_ref, twiddle_ref, turned, stage):
    unpack(recv_ref, stage)
    w = w_ref[...]
    for a in range(ROWS):
        cols = token_columns(a)
        grad_back = from_message(a, turned, stage)
        early = jnp.sum(grad_back * first_ref[:, cols].astype(f32), axis=0, keepdims=True)
        twiddle_ref[a : a + 1, :] = early + later_ref[a : a + 1, :]
        out_ref[:, cols] = direct_ref[:, cols] + dot((grad_back * tw_ref[a : a + 1, :]).astype(bf16), w)


def exchange(values):
    return lax.all_to_all(
        values.reshape(NSEQ, ROWS, LANES), "seq", split_axis=0, concat_axis=0, tiled=True
    ).reshape(OUTER, LANES)


def to_all(value, axis, size):
    copies = jnp.broadcast_to(value[None], (size,) + value.shape)
    return lax.all_to_all(copies, axis, split_axis=0, concat_axis=0, tiled=True)


def on_device(inputs, cotangent, kernel, inner_weight, outer_weight, twiddle, up_weight, down_weight):
    mix_flops = 2 * BW * TOK * INNER
    col_flops = 4 * OUTER * OUTER * LANES
    mlp_flops = 2 * HB * BW * TOK

    send, first = call(
        rows_in,
        [((OUTER, LANES), bf16), ((BW, TOK), bf16)],
        inputs,
        inner_weight,
        twiddle,
        flops=mix_flops,
        scratch=[TURNED, STAGE],
    )

    cotangent_late, down_late, send = lax.optimization_barrier((cotangent, down_weight, send))
    down_parts = down_late.reshape(BW, NBLK, SLICE).transpose(1, 0, 2)
    down_parts = jnp.pad(down_parts, ((0, 0), (0, 0), (0, LANE_TILE - SLICE)))
    cot_parts = jnp.broadcast_to(cotangent_late.astype(bf16)[None], (NBLK, BW, TOK))
    shared = lax.all_to_all(
        jnp.concatenate([cot_parts, down_parts], axis=2), "chan", split_axis=0, concat_axis=0, tiled=True
    )

    kernel_t = kernel.astype(bf16).transpose(2, 1, 0).reshape(OUTER, LANES)
    outer_t = outer_weight.T
    up_t = up_weight.T

    recv = exchange(send)
    send, spectrum = call(
        columns,
        [((OUTER, LANES), bf16), ((OUTER, LANES), bf16)],
        recv,
        outer_weight,
        outer_t,
        kernel_t,
        flops=col_flops,
    )
    recv = exchange(send)
    (grad_act,) = call(hidden_cotangent, [((HB, TOK), bf16)], shared, flops=mlp_flops)
    send, back, low, act, grad_hidden, grad_mix, direct = call(
        mlp,
        [
            ((OUTER, LANES), bf16),
            ((BW, TOK), bf16),
            ((BW, TOK), bf16),
            ((HB, TOK), bf16),
            ((HB, TOK), bf16),
            ((BW, TOK), bf16),
            ((BW, TOK), f32),
        ],
        recv,
        inputs,
        cotangent,
        grad_act,
        inner_weight,
        twiddle,
        up_weight,
        up_t,
        flops=2 * mix_flops + 2 * mlp_flops,
        trans=2 * HB * TOK,
        scratch=[TURNED, STAGE, TURNED, STAGE],
    )
    recv = exchange(send)

    up_part, down_part, later = call(
        weight_grads,
        [((HB, LANE_TILE), bf16), ((HB, LANE_TILE), bf16), ((ROWS, INNER), f32)],
        grad_hidden,
        low,
        act,
        shared,
        grad_mix,
        back,
        inner_weight,
        flops=2 * mlp_flops + mix_flops,
    )
    down_part = lax.all_to_all(
        down_part.reshape(NBLK, SLICE, LANE_TILE), "chan", split_axis=0, concat_axis=0, tiled=True
    ).reshape(HB, LANE_TILE)
    share = 16
    grads = jnp.concatenate(
        [up_part, down_part, jnp.zeros((NSEQ * share - 2 * HB, LANE_TILE), bf16)], axis=0
    ).reshape(NSEQ, share, LANE_TILE)
    grads = lax.all_to_all(grads, "seq", split_axis=0, concat_axis=0, tiled=True)
    grads = jnp.sum(grads.astype(f32), axis=0) * (1.0 / math.sqrt(SEQ))
    grads = to_all(grads.astype(bf16), "seq", NSEQ).reshape(NSEQ * share, LANE_TILE).astype(f32)
    grad_up = grads[:HB, :BW]
    grad_down = grads[HB : 2 * HB, :BW].T

    send, grad_spec = call(
        columns,
        [((OUTER, LANES), bf16), ((OUTER, LANES), f32)],
        recv,
        outer_weight,
        outer_t,
        kernel_t,
        flops=col_flops,
    )
    recv = exchange(send)
    grad_kernel = (grad_spec * spectrum.astype(f32)).reshape(OUTER, COLS, BW).transpose(2, 1, 0)

    grad_inputs, grad_twiddle = call(
        rows_out,
        [((BW, TOK), f32), ((ROWS, INNER), f32)],
        recv,
        inner_weight,
        twiddle,
        first,
        direct,
        later,
        flops=mix_flops,
        scratch=[TURNED, STAGE],
    )
    grad_twiddle = jnp.sum(to_all(grad_twiddle, "chan", NBLK), axis=0) * (1.0 / math.sqrt(D))
    return grad_inputs, grad_kernel, grad_up, grad_down, grad_twiddle


def solution(mesh):
    placed = (
        P("chan", "seq"),
        P("chan", "seq"),
        P("chan", "seq", None),
        P(),
        P(),
        P("seq", None),
        P("chan", None),
        P("chan", None),
    )
    return jax.shard_map(
        on_device,
        mesh=mesh,
        in_specs=placed,
        out_specs=(
            P("chan", "seq"),
            P("chan", "seq", None),
            P("chan", None),
            P("chan", None),
            P("seq", None),
        ),
        check_vma=False,
    )
```

time: 903 us -> 302 us (0.33)
  waiting for transfers between devices: 612 us -> 158 us
  blocking collectives: 101 us -> 28 us
  matrix products: 35 us -> 0 us
  local copies, waits for them, and re-layouts: 48.6 us -> 32 us
  starting transfers between devices: 76.9 us -> 61 us
  Pallas kernels: 0 us -> 14 us
  between operations: 14.1 us -> 0.92 us
    psum x1 -> x0, waiting for transfers between devices: 402 us -> none  [on_device(): grad_up, grad_down = lax.psum((grad_up, grad_down), 'seq')]
    reduce_scatter x1 -> x0, waiting for transfers between devices: 90 us -> none  [on_device(): lax.psum_scatter(full_up, 'chan', scatter_dimension=0, tiled=True)]
    all_to_all x6 -> x8, waiting for transfers between devices: 87.8 us -> 158 us  [the longest x4 97.4 us: exchange(): lax.all_to_all(values.reshape(NSEQ, ROWS, LANES), 'seq', split_axis=0, co...]
    all_gather x2 -> x0, blocking collectives: 64.4 us -> none  [the longest x1 32.6 us: on_device(): lax.all_gather(down_weight, 'chan', axis=0, tiled=True)]
    unnamed x4 -> x0, waiting for transfers between devices: 31.9 us -> none
    dot_general x12 -> x0, matrix products: 31.7 us -> none  [the longest x1 11.1 us: on_device(): jnp.einsum('jrc,jct->jrt', up_blocks, shared_blocks, preferred_element_ty...]
    psum x1 -> x0, blocking collectives: 20.1 us -> none  [on_device(): lax.psum(early_term + later_product_term, 'chan') * (1.0 / math.sqrt(D))]
    all_to_all x6 -> x8, starting transfers between devices: 76.8 us -> 61 us  [the longest x4 32.3 us: exchange(): lax.all_to_all(values.reshape(NSEQ, ROWS, LANES), 'seq', split_axis=0, co...]
  transfers between devices with their start and end apart: 9 -> 8, of which waited for: 7 -> 8; matrix products, arithmetic and copies ran while one was open for 6% -> 6% of each run, Pallas kernels for 0% -> 1%
where the time goes in v1:
time: 302 us; the launch traced here: 300 us
  waiting for transfers between devices  158 us (52%)
  starting transfers between devices  61 us (20%)
  local copies, waits for them, and re-layouts  32 us (11%)
  blocking collectives  28 us (9%)
  Pallas kernels  14 us (5%)
  other arithmetic  5.96 us (2%)
    all_to_all x4, waiting for transfers between devices, exchange(): lax.all_to_all(values.reshape(NSEQ, ROWS, LANES), 'seq', split_axis=0, co...  97.4 us
    all_to_all x4, starting transfers between devices, exchange(): lax.all_to_all(values.reshape(NSEQ, ROWS, LANES), 'seq', split_axis=0, co...  32.3 us
    all_to_all x1, waiting for transfers between devices, on_device(): lax.all_to_all(jnp.concatenate([cot_parts, down_parts], axis=2), 'chan',...  29.1 us
    all_to_all x1, blocking collectives, on_device(): lax.all_to_all(grads, 'seq', split_axis=0, concat_axis=0, tiled=True)  28 us
    unnamed x64, local copies, waits for them, and re-layouts  25.7 us
    all_to_all x2, waiting for transfers between devices, to_all(): return lax.all_to_all(copies, axis, split_axis=0, concat_axis=0, tiled=True)  24.7 us
    all_to_all x1, starting transfers between devices, on_device(): lax.all_to_all(down_part.reshape(NBLK, SLICE, LANE_TILE), 'chan', split_a...  14.3 us
    pallas_call x7, Pallas kernels, call(): pl.pallas_call(kernel, out_shape=shapes, in_specs=[pl.BlockSpec(memory_sp...  14 us
  transfers between devices with their start and end apart: 8, of which 8 were waited for; matrix products, arithmetic and copies ran while one was open for 6% of the time, Pallas kernels for 1%

profile of v1, /device:TPU:1, one launch (start us, length us, event | category | flops | bytes accessed | tf_op | source)
XLA Modules:
  0.0 300.0 jit_solution(12707917992901827231)
XLA Ops:
  0.6 1.1 copy-done.8
  1.8 0.9 copy-done.11
  3.4 1.7 shard_map.119
  5.8 18.2 %all-to-all-start = ((bf16[64,8,384]{2,1,0:T(8,128)(2,1)}), bf16[64,8,384]{2,1,0:T(8,128)(2,1)S(1)}, u32[]{:S(2)}, u32[]{:S(2)}) async-start(bf16[64,8,384]{2,1,0:T(8,128)(2,1)} %bitcast), calls=%async_computation | async-start | bytes 786432 | tf_op jit(solution)/shard_map/all_to_all | solution.py:189
  24.0 1.2 convert_element_type.28
  25.1 1.0 copy.31
  26.7 2.0 fusion.1
  28.7 22.5 %all-to-all-done = bf16[64,8,384]{2,1,0:T(8,128)(2,1)S(1)} async-done(((bf16[64,8,384]{2,1,0:T(8,128)(2,1)}), bf16[64,8,384]{2,1,0:T(8,128)(2,1)S(1)}, u32[]{:S(2)}, u32[]{:S(2)}) %all-to-all-start) | async-done | bytes 393248 | tf_op jit(solution)/shard_map/all_to_all | solution.py:189
  52.0 6.4 %all-to-all-start.2 = ((bf16[8,96,2176]{2,1,0:T(8,128)(2,1)}), bf16[8,96,2176]{2,1,0:T(8,128)(2,1)S(1)}, u32[]{:S(2)}, u32[]{:S(2)}) async-start(bf16[8,96,2176]{2,1,0:T(8,128)(2,1)} %fusion.1), calls=%async_computation.2 | async-start | bytes 6684672 | tf_op jit(solution)/shard_map/all_to_all | solution.py:218
  58.3 2.1 copy.40
  60.5 1.9 copy.30.kernel_ref
  62.4 2.0 copy.28
  64.5 1.0 copy-done.2
  65.5 1.0 copy-done.4
  66.5 1.0 copy-done.6
  67.5 1.0 copy-done.14
  68.5 0.8 shard_map.120
  70.1 0.8 copy-done.21
  70.8 29.1 %all-to-all-done.2.shared_ref = bf16[8,96,2176]{2,1,0:T(8,128)(2,1)S(1)} async-done(((bf16[8,96,2176]{2,1,0:T(8,128)(2,1)}), bf16[8,96,2176]{2,1,0:T(8,128)(2,1)S(1)}, u32[]{:S(2)}, u32[]{:S(2)}) %all-to-all-start.2) | async-done | bytes 3342368 | tf_op jit(solution)/shard_map/all_to_all | solution.py:218
  100.0 5.5 %all-to-all-start.1 = ((bf16[64,8,384]{2,1,0:T(8,128)(2,1)}), bf16[64,8,384]{2,1,0:T(8,128)(2,1)}, u32[]{:S(2)}, u32[]{:S(2)}) async-start(bf16[64,8,384]{2,1,0:T(8,128)(2,1)} %bitcast.32), calls=%async_computation.1 | async-start | bytes 786432 | tf_op jit(solution)/shard_map/all_to_all | solution.py:189
  106.8 1.2 copy-done
  108.0 24.6 %all-to-all-done.1 = bf16[64,8,384]{2,1,0:T(8,128)(2,1)} async-done(((bf16[64,8,384]{2,1,0:T(8,128)(2,1)}), bf16[64,8,384]{2,1,0:T(8,128)(2,1)}, u32[]{:S(2)}, u32[]{:S(2)}) %all-to-all-start.1) | async-done | bytes 393248 | tf_op jit(solution)/shard_map/all_to_all | solution.py:189
  132.6 1.4 copy-done.1
  134.0 1.1 copy-done.9
  135.2 1.1 copy-done.10
  136.3 0.9 copy-done.23
  137.2 5.8 %shard_map.122 = (bf16[512,384]{1,0:T(8,128)(2,1)S(1)}, bf16[96,2048]{1,0:T(8,128)(2,1)S(1)}, bf16[96,2048]{1,0:T(8,128)(2,1)S(1)}, bf16[384,2048]{1,0:T(8,128)(...) custom-call(bf16[512,384]{1,0:T(8,128)(2,1)} %bitcast.6.recv_ref, ...), custom_call_target="tpu_custom_call" | custom-call | flops 503316480 | bytes 9330688 | tf_op jit(solution)/shard_map/pallas_call | solution.py:40
  143.0 1.8 shard_map.124
  146.1 14.3 %all-to-all-start.5 = ((bf16[8,48,128]{2,1,0:T(8,128)(2,1)}), bf16[8,48,128]{2,1,0:T(8,128)(2,1)S(1)}, u32[]{:S(2)}, u32[]{:S(2)}) async-start(bf16[8,48,128]{2,1,0:T(8,128)(2,1)} %bitcast.34), calls=%async_computation.5 | async-start | bytes 196608 | tf_op jit(solution)/shard_map/all_to_all | solution.py:275
  160.4 6.9 %all-to-all-done.5 = bf16[8,48,128]{2,1,0:T(8,128)(2,1)S(1)} async-done(((bf16[8,48,128]{2,1,0:T(8,128)(2,1)}), bf16[8,48,128]{2,1,0:T(8,128)(2,1)S(1)}, u32[]{:S(2)}, u32[]{:S(2)}) %all-to-all-start.5) | async-done | bytes 98336 | tf_op jit(solution)/shard_map/all_to_all | solution.py:275
  167.3 1.1 maximum_maximum_fusion
  168.4 28.0 %all_to_all.45 = bf16[64,16,128]{2,1,0:T(8,128)(2,1)S(1)} all-to-all(bf16[64,16,128]{2,1,0:T(8,128)(2,1)S(1)} %bitcast.37), channel_id=1, replica_groups=mesh['seq'=64,'chan'=8] {'seq'}, dimensions={0} | all-to-all | bytes 524288 | tf_op jit(solution)/shard_map/all_to_all | solution.py:282
  196.4 4.4 %all-to-all-start.3 = ((bf16[64,8,384]{2,1,0:T(8,128)(2,1)}), bf16[64,8,384]{2,1,0:T(8,128)(2,1)S(1)}, u32[]{:S(2)}, u32[]{:S(2)}) async-start(bf16[64,8,384]{2,1,0:T(8,128)(2,1)} %bitcast.31), calls=%async_computation.3 | async-start | bytes 786432 | tf_op jit(solution)/shard_map/all_to_all | solution.py:189
  200.9 27.0 %all-to-all-done.3 = bf16[64,8,384]{2,1,0:T(8,128)(2,1)S(1)} async-done(((bf16[64,8,384]{2,1,0:T(8,128)(2,1)}), bf16[64,8,384]{2,1,0:T(8,128)(2,1)S(1)}, u32[]{:S(2)}, u32[]{:S(2)}) %all-to-all-start.3) | async-done | bytes 393248 | tf_op jit(solution)/shard_map/all_to_all | solution.py:189
  228.6 4.7 %all-to-all-start.7 = ((bf16[64,16,128]{2,1,0:T(8,128)(2,1)}), bf16[64,16,128]{2,1,0:T(8,128)(2,1)S(1)}, u32[]{:S(2)}, u32[]{:S(2)}) async-start(bf16[64,16,128]{2,1,0:T(8,128)(2,1)} %broadcast_in_dim.10), calls=%async_computation.7 | async-start | bytes 524288 | tf_op jit(solution)/shard_map/all_to_all | solution.py:196
  233.3 1.0 copy-done.7
  234.3 1.5 shard_map.123
  235.8 19.7 %all-to-all-done.7 = bf16[64,16,128]{2,1,0:T(8,128)(2,1)S(1)} async-done(((bf16[64,16,128]{2,1,0:T(8,128)(2,1)}), bf16[64,16,128]{2,1,0:T(8,128)(2,1)S(1)}, u32[]{:S(2)}, u32[]{:S(2)}) %all-to-all-start.7) | async-done | bytes 262176 | tf_op jit(solution)/shard_map/all_to_all | solution.py:196
  255.6 4.3 %all-to-all-start.4 = ((bf16[64,8,384]{2,1,0:T(8,128)(2,1)}), bf16[64,8,384]{2,1,0:T(8,128)(2,1)S(1)}, u32[]{:S(2)}, u32[]{:S(2)}) async-start(bf16[64,8,384]{2,1,0:T(8,128)(2,1)} %bitcast.12), calls=%async_computation.4 | async-start | bytes 786432 | tf_op jit(solution)/shard_map/all_to_all | solution.py:189
  259.9 0.9 convert_multiply_fusion
  260.8 1.4 copy.35
  262.3 1.4 copy.36
  263.7 23.3 %all-to-all-done.4 = bf16[64,8,384]{2,1,0:T(8,128)(2,1)S(1)} async-done(((bf16[64,8,384]{2,1,0:T(8,128)(2,1)}), bf16[64,8,384]{2,1,0:T(8,128)(2,1)S(1)}, u32[]{:S(2)}, u32[]{:S(2)}) %all-to-all-start.4) | async-done | bytes 393248 | tf_op jit(solution)/shard_map/all_to_all | solution.py:189
  287.0 1.8 shard_map.125
  289.4 3.3 %all-to-all-start.8 = ((f32[8,8,256]{2,1,0:T(8,128)}), f32[8,8,256]{2,1,0:T(8,128)S(1)}, u32[]{:S(2)}, u32[]{:S(2)}) async-start(f32[8,8,256]{2,1,0:T(8,128)} %broadcast_in_dim.11), calls=%async_computation.8 | async-start | bytes 131072 | tf_op jit(solution)/shard_map/all_to_all | solution.py:196
  292.8 0.8 copy.37
  293.6 0.8 copy.38
  294.4 5.0 %all-to-all-done.8 = f32[8,8,256]{2,1,0:T(8,128)S(1)} async-done(((f32[8,8,256]{2,1,0:T(8,128)}), f32[8,8,256]{2,1,0:T(8,128)S(1)}, u32[]{:S(2)}, u32[]{:S(2)}) %all-to-all-start.8) | async-done | bytes 65568 | tf_op jit(solution)/shard_map/all_to_all | solution.py:196
  (59 shorter events, 8.3 us)
Async XLA Ops:
  0.6 1.1 copy-start.8
  1.8 0.9 copy-start.11
  2.7 0.7 copy-start.27
  5.1 0.7 copy-start.19
  5.8 45.4 %all-to-all-start = ((bf16[64,8,384]{2,1,0:T(8,128)(2,1)}), bf16[64,8,384]{2,1,0:T(8,128)(2,1)S(1)}, u32[]{:S(2)}, u32[]{:S(2)}) async-start(bf16[64,8,384]{2,1,0:T(8,128)(2,1)} %bitcast), calls=%async_computation | async-start | bytes 786432 | tf_op jit(solution)/shard_map/all_to_all | solution.py:189
  51.2 0.7 copy-start.13
  52.0 48.0 %all-to-all-start.2 = ((bf16[8,96,2176]{2,1,0:T(8,128)(2,1)}), bf16[8,96,2176]{2,1,0:T(8,128)(2,1)S(1)}, u32[]{:S(2)}, u32[]{:S(2)}) async-start(bf16[8,96,2176]{2,1,0:T(8,128)(2,1)} %fusion.1), calls=%async_computation.2 | async-start | bytes 6684672 | tf_op jit(solution)/shard_map/all_to_all | solution.py:218
  58.3 47.1 %copy-start.24 = (bf16[384,96]{0,1:T(8,128)(2,1)S(1)}, bf16[384,96]{0,1:T(8,128)(2,1)}, u32[]{:S(2)}) copy-start(bf16[384,96]{0,1:T(8,128)(2,1)} %param.14) | copy-start | bytes 221188
  64.4 1.0 copy-start.2
  65.5 1.0 copy-start.4
  66.5 1.0 copy-start.6
  67.5 1.0 copy-start.14
  69.3 0.7 copy-start.18
  70.1 0.8 copy-start.21
  70.8 61.8 %copy-start.12 = (bf16[256,256]{1,0:T(8,128)(2,1)S(1)}, bf16[256,256]{1,0:T(8,128)(2,1)}, u32[]{:S(2)}) copy-start(bf16[256,256]{1,0:T(8,128)(2,1)} %w_ref.7) | copy-start | bytes 393220
  70.8 61.8 %copy-start.28 = (f32[8,256]{1,0:T(8,128)S(1)}, f32[8,256]{1,0:T(8,128)}, u32[]{:S(2)}) copy-start(f32[8,256]{1,0:T(8,128)} %tw_ref.5) | copy-start | bytes 24580
  100.0 32.6 %all-to-all-start.1 = ((bf16[64,8,384]{2,1,0:T(8,128)(2,1)}), bf16[64,8,384]{2,1,0:T(8,128)(2,1)}, u32[]{:S(2)}, u32[]{:S(2)}) async-start(bf16[64,8,384]{2,1,0:T(8,128)(2,1)} %bitcast.32), calls=%async_computation.1 | async-start | bytes 786432 | tf_op jit(solution)/shard_map/all_to_all | solution.py:189
  106.8 1.2 copy-start
  132.6 1.4 copy-start.1
  134.0 1.1 copy-start.9
  135.2 1.1 copy-start.10
  136.3 0.9 copy-start.23
  143.0 1.8 copy-start.15
  143.0 1.8 copy-start.17
  144.8 0.6 copy-start.25
  145.5 0.6 copy-start.26
  146.1 87.2 %copy-start.3 = (bf16[512,512]{1,0:T(8,128)(2,1)S(1)}, bf16[512,512]{1,0:T(8,128)(2,1)}, u32[]{:S(2)}) copy-start(bf16[512,512]{1,0:T(8,128)(2,1)} %outer_ref.3) | copy-start | bytes 1572868
  146.1 87.2 %copy-start.5 = (bf16[512,512]{0,1:T(8,128)(2,1)S(1)}, bf16[512,512]{0,1:T(8,128)(2,1)}, u32[]{:S(2)}) copy-start(bf16[512,512]{0,1:T(8,128)(2,1)} %copy.28) | copy-start | bytes 1572868
  146.1 113.8 %copy-start.22 = (bf16[512,384]{1,0:T(8,128)(2,1)S(1)}, bf16[512,384]{1,0:T(8,128)(2,1)}, u32[]{:S(2)}) copy-start(bf16[512,384]{1,0:T(8,128)(2,1)} %copy-done.21) | copy-start | bytes 1179652
  146.1 21.2 %all-to-all-start.5 = ((bf16[8,48,128]{2,1,0:T(8,128)(2,1)}), bf16[8,48,128]{2,1,0:T(8,128)(2,1)S(1)}, u32[]{:S(2)}, u32[]{:S(2)}) async-start(bf16[8,48,128]{2,1,0:T(8,128)(2,1)} %bitcast.34), calls=%async_computation.5 | async-start | bytes 196608 | tf_op jit(solution)/shard_map/all_to_all | solution.py:275
  196.4 31.5 %all-to-all-start.3 = ((bf16[64,8,384]{2,1,0:T(8,128)(2,1)}), bf16[64,8,384]{2,1,0:T(8,128)(2,1)S(1)}, u32[]{:S(2)}, u32[]{:S(2)}) async-start(bf16[64,8,384]{2,1,0:T(8,128)(2,1)} %bitcast.31), calls=%async_computation.3 | async-start | bytes 786432 | tf_op jit(solution)/shard_map/all_to_all | solution.py:189
  228.6 26.9 %all-to-all-start.7 = ((bf16[64,16,128]{2,1,0:T(8,128)(2,1)}), bf16[64,16,128]{2,1,0:T(8,128)(2,1)S(1)}, u32[]{:S(2)}, u32[]{:S(2)}) async-start(bf16[64,16,128]{2,1,0:T(8,128)(2,1)} %broadcast_in_dim.10), calls=%async_computation.7 | async-start | bytes 524288 | tf_op jit(solution)/shard_map/all_to_all | solution.py:196
  233.3 1.0 copy-start.7
  255.6 31.4 %copy-start.16 = (f32[96,2048]{1,0:T(8,128)S(1)}, f32[96,2048]{1,0:T(8,128)}, u32[]{:S(2)}) copy-start(f32[96,2048]{1,0:T(8,128)} %copy-done.15) | copy-start | bytes 2359300
  255.6 31.4 %copy-start.20 = (bf16[96,2048]{1,0:T(8,128)(2,1)S(1)}, bf16[96,2048]{1,0:T(8,128)(2,1)}, u32[]{:S(2)}) copy-start(bf16[96,2048]{1,0:T(8,128)(2,1)} %copy-done.19) | copy-start | bytes 1179652
  255.6 31.4 %all-to-all-start.4 = ((bf16[64,8,384]{2,1,0:T(8,128)(2,1)}), bf16[64,8,384]{2,1,0:T(8,128)(2,1)S(1)}, u32[]{:S(2)}, u32[]{:S(2)}) async-start(bf16[64,8,384]{2,1,0:T(8,128)(2,1)} %bitcast.12), calls=%async_computation.4 | async-start | bytes 786432 | tf_op jit(solution)/shard_map/all_to_all | solution.py:189
  289.4 10.0 %all-to-all-start.8 = ((f32[8,8,256]{2,1,0:T(8,128)}), f32[8,8,256]{2,1,0:T(8,128)S(1)}, u32[]{:S(2)}, u32[]{:S(2)}) async-start(f32[8,8,256]{2,1,0:T(8,128)} %broadcast_in_dim.11), calls=%async_computation.8 | async-start | bytes 131072 | tf_op jit(solution)/shard_map/all_to_all | solution.py:196

commit v2 on v1

v2 whole, which is shorter than its diff:
```python
import functools
import math

import jax
import jax.numpy as jnp
from jax import lax
from jax.experimental import pallas as pl
from jax.experimental.pallas import tpu as pltpu
from jax.sharding import PartitionSpec as P

D = 768
HID = 3072
NBLK = 8
OUTER = 512
INNER = 256
SEQ = 131072
BW = D // NBLK
HB = HID // NBLK
SLICE = HB // NBLK
NSEQ = 64
ROWS = OUTER // NSEQ
COLS = INNER // NSEQ
LANES = COLS * BW
TOK = ROWS * INNER
LANE_TILE = 128
WIDE = LANES + 2 * LANE_TILE

f32 = jnp.float32
bf16 = jnp.bfloat16
NT = (((1,), (1,)), ((), ()))
NN = (((1,), (0,)), ((), ()))


def dot(lhs, rhs, dims=NN):
    return lax.dot_general(lhs, rhs, dims, preferred_element_type=f32)


class Stacked:
    def __init__(self, parts, shape, places):
        self.parts, self.shape, self.places = parts, shape, places
        self.dtype = parts[0].dtype


def call(body, outs, *operands, flops=0, scratch=(), trans=0):
    shapes = [jax.ShapeDtypeStruct(shape, dtype) for shape, dtype in outs]
    nbytes = sum(math.prod(o.shape) * o.dtype.itemsize for o in list(operands) + shapes)
    arrays = []
    for operand in operands:
        arrays += operand.parts if isinstance(operand, Stacked) else [operand]
    n_in, n_out = len(operands), len(shapes)

    def kernel(*refs):
        sources, targets, refs = refs[: len(arrays)], refs[len(arrays) : len(arrays) + n_out], refs[len(arrays) + n_out :]
        held, built, refs = refs[:n_in], refs[n_in : n_in + n_out], refs[n_in + n_out :]
        in_sems, out_sems, refs = refs[0], refs[1], refs[2:]
        loads, taken = [], 0
        for operand, ref in zip(operands, held):
            if isinstance(operand, Stacked):
                places = operand.places(ref)
            else:
                places = [ref]
            copies = []
            for place in places:
                copies.append(pltpu.make_async_copy(sources[taken], place, in_sems.at[taken]))
                copies[-1].start()
                taken += 1
            loads.append(copies)

        def ready(i):
            while loads[i]:
                loads[i].pop().wait()
            return held[i]

        stores = []

        class Out:
            def __init__(self, i):
                self.i, self.ref, self.parts = i, built[i], 0

            def store(self, *index):
                source = built[self.i].at[index] if index else built[self.i]
                target = targets[self.i].at[index] if index else targets[self.i]
                copy = pltpu.make_async_copy(source, target, out_sems.at[self.i, self.parts])
                self.parts += 1
                copy.start()
                stores.append(copy)

        out = [Out(i) for i in range(n_out)]
        body([functools.partial(ready, i) for i in range(n_in)], out, *refs)
        for i in range(n_in):
            ready(i)
        for o in out:
            if not o.parts:
                o.store()
        for copy in stores:
            copy.wait()

    return pl.pallas_call(
        kernel,
        out_shape=shapes,
        in_specs=[pl.BlockSpec(memory_space=pltpu.HBM)] * len(arrays),
        out_specs=[pl.BlockSpec(memory_space=pltpu.HBM)] * n_out,
        scratch_shapes=[pltpu.VMEM(o.shape, o.dtype) for o in list(operands) + shapes]
        + [pltpu.SemaphoreType.DMA((len(arrays),)), pltpu.SemaphoreType.DMA((n_out, ROWS))]
        + list(scratch),
        cost_estimate=pl.CostEstimate(flops=flops, bytes_accessed=nbytes, transcendentals=trans),
        compiler_params=pltpu.CompilerParams(vmem_limit_bytes=60 * 1024 * 1024),
    )(*arrays)


def token_columns(a):
    return slice(a * INNER, (a + 1) * INNER)


def to_message(value, a, turned, stage):
    turned[:, :BW] = value.T
    parts = [turned[pl.ds(b, NSEQ, stride=COLS), :][:, :BW] for b in range(COLS)]
    row = jnp.concatenate(parts, axis=1)
    for k in range(LANES // LANE_TILE):
        stage[k, pl.ds(a, NSEQ, stride=ROWS), :] = row[:, k * LANE_TILE : (k + 1) * LANE_TILE]


def from_message(a, turned, stage):
    row = jnp.concatenate(
        [stage[k, pl.ds(a, NSEQ, stride=ROWS), :] for k in range(LANES // LANE_TILE)], axis=1
    )
    for b in range(COLS):
        turned[pl.ds(b, NSEQ, stride=COLS), :] = jnp.concatenate(
            [row[:, b * BW : (b + 1) * BW], jnp.zeros((NSEQ, LANE_TILE - BW), f32)], axis=1
        )
    return turned[...].T[:BW]


def pack(stage, send_ref):
    for k in range(LANES // LANE_TILE):
        send_ref[:, k * LANE_TILE : (k + 1) * LANE_TILE] = stage[k].astype(bf16)


def unpack(recv_ref, stage):
    for k in range(LANES // LANE_TILE):
        stage[k] = recv_ref[:, k * LANE_TILE : (k + 1) * LANE_TILE].astype(f32)


STAGE = pltpu.VMEM((LANES // LANE_TILE, OUTER, LANE_TILE), f32)
TURNED = pltpu.VMEM((INNER, LANE_TILE), f32)


def rows_in(ins, outs, turned, stage):
    x, w, twiddle = ins
    send, first_out = outs
    for a in range(ROWS):
        cols = token_columns(a)
        first = dot(x()[:, cols].astype(bf16), w()[...], NT)
        first_out.ref[:, cols] = first.astype(bf16)
        to_message(first * twiddle()[a : a + 1, :], a, turned, stage)
    first_out.store()
    pack(stage, send.ref)


def columns(ins, outs):
    recv, outer, kernel, outer_t = ins
    send, spec_out = outs
    spec = dot(outer()[...], recv()[:, :LANES])
    spec_out.ref[...] = spec.astype(spec_out.ref.dtype)
    spec_out.store()
    scaled = (kernel()[...].astype(f32) * spec).astype(bf16)
    send.ref[:, :LANES] = dot(outer_t()[...], scaled).astype(bf16)
    if recv().shape[1] == WIDE:
        parts = recv()[:, LANES:].astype(f32).reshape(NSEQ, ROWS, WIDE - LANES)
        total = jnp.sum(parts, axis=0, keepdims=True)
        send.ref[:, LANES:] = (
            jnp.broadcast_to(total, parts.shape).reshape(OUTER, WIDE - LANES).astype(bf16)
        )


def mlp(ins, outs, turned, stage, turned_out, stage_out, down_t, down_own, grad_up, grad_down):
    recv, w, twiddle, x_in, up, shared, up_t, cot = ins
    send, later, direct = outs
    me = lax.axis_index("chan")
    unpack(recv(), stage)
    for a in range(ROWS):
        cols = token_columns(a)
        scale = twiddle()[a : a + 1, :]
        back = from_message(a, turned, stage)
        mixing = dot((back * scale).astype(bf16), w()[...])
        x = x_in()[:, cols]
        low = (x + x * mixing).astype(bf16)
        hidden = dot(up()[...], low)
        cumulative = 0.5 * (1.0 + lax.erf(hidden * (1.0 / math.sqrt(2.0))))
        density = jnp.exp(-0.5 * hidden * hidden) * (1.0 / math.sqrt(2.0 * math.pi))
        act = (hidden * cumulative).astype(bf16)
        slope = cumulative + hidden * density
        if a == 0:
            for p in range(NBLK):
                down_t[...] = shared()[p, :, TOK:].astype(f32).T
                own = pl.ds(pl.multiple_of(me * SLICE, SLICE), SLICE)
                down_own[p * SLICE : (p + 1) * SLICE, :] = down_t[own, :].astype(bf16)
        grad_act, down_part = [], []
        for p in range(NBLK):
            rows = slice(p * SLICE, (p + 1) * SLICE)
            cot_low = shared()[p, :, cols]
            grad_act.append(dot(down_own[rows, :], cot_low).astype(bf16))
            down_part.append(dot(act[rows], cot_low, NT))
        grad_act = jnp.concatenate(grad_act, axis=0).astype(f32)
        down_part = jnp.concatenate(down_part, axis=0)
        grad_hidden = (grad_act * slope).astype(bf16)
        up_part = dot(grad_hidden, low, NT)
        if a == 0:
            grad_up[...] = up_part
            grad_down[...] = down_part
        else:
            grad_up[...] += up_part
            grad_down[...] += down_part
        grad_gated = cot()[:, cols] + dot(up_t()[...], grad_hidden)
        direct.ref[:, cols] = grad_gated * (1.0 + mixing)
        direct.store(slice(None), cols)
        grad_mix = (grad_gated * x).astype(bf16)
        second = dot(grad_mix, w()[...], NT)
        later.ref[a : a + 1, :] = jnp.sum(second * back, axis=0, keepdims=True)
        to_message(second * scale, a, turned_out, stage_out)
    pack(stage_out, send.ref)
    zeros = jnp.zeros((HB, LANE_TILE - BW), f32)
    for start, total in ((LANES, grad_up), (LANES + LANE_TILE, grad_down)):
        send.ref[:HB, start : start + LANE_TILE] = jnp.concatenate([total[...], zeros], axis=1).astype(bf16)
    send.ref[HB:, LANES:] = jnp.zeros((OUTER - HB, WIDE - LANES), bf16)


def gather_over_chan(block):
    across, left, right, far = (lax.ppermute(block, "chan", step_to(step)) for step in ((1, 0), (0, 1), (0, 3), (1, 2)))
    half = BW // 2

    def onward():
        return (
            lax.ppermute(across, "chan", step_to((0, 1))),
            lax.ppermute(across, "chan", step_to((0, 3))),
            lax.ppermute(left[:half], "chan", step_to((0, 1))),
            lax.ppermute(right[half:], "chan", step_to((0, 3))),
        )

    return (across, left, right, far), onward


def block_places(ref):
    me = lax.axis_index("chan")
    half = BW // 2

    def at(dy, dx):
        return ref.at[(me // 4 + dy) % 2 * 4 + (me % 4 + dx) % 4]

    opposite = at(0, 2)
    return [
        at(0, 0),
        at(1, 0),
        at(0, 3),
        at(0, 1),
        at(1, 2),
        at(1, 3),
        at(1, 1),
        opposite.at[pl.ds(0, half)],
        opposite.at[pl.ds(half, half)],
    ]


def twiddle_terms(ins, outs, turned, stage):
    recv, first, later, twiddle = ins
    shared, grad_back_out, grad_up = outs
    grad_up.ref[...] = recv()[:HB, LANES : LANES + BW].astype(f32) * (1.0 / math.sqrt(SEQ))
    grad_up.store()
    unpack(recv(), stage)
    terms = []
    for a in range(ROWS):
        cols = token_columns(a)
        grad_back = from_message(a, turned, stage)
        terms.append(
            jnp.sum(grad_back * first()[:, cols].astype(f32), axis=0, keepdims=True) + later()[a : a + 1, :]
        )
        grad_back_out.ref[:, cols] = (grad_back * twiddle()[a : a + 1, :]).astype(bf16)
    grad_back_out.store()
    terms = jnp.concatenate(terms, axis=0)
    terms = jnp.concatenate([terms[:, :LANE_TILE], terms[:, LANE_TILE:]], axis=0).astype(bf16)
    for p in range(NBLK):
        shared.ref[p, :SLICE, :] = recv()[p * SLICE : (p + 1) * SLICE, LANES + LANE_TILE :]
        shared.ref[p, SLICE:, :] = terms


def rows_out(ins, outs):
    grad_back, w, direct = ins
    (out,) = outs
    for a in range(ROWS):
        cols = token_columns(a)
        out.ref[:, cols] = direct()[:, cols] + dot(grad_back()[:, cols], w()[...])
        out.store(slice(None), cols)


def finish(ins, outs):
    (shared,) = ins
    grad_down, grad_twiddle = outs
    terms = jnp.sum(shared()[:, SLICE:, :].astype(f32), axis=0) * (1.0 / math.sqrt(D))
    grad_twiddle.ref[:, :LANE_TILE] = terms[:ROWS]
    grad_twiddle.ref[:, LANE_TILE:] = terms[ROWS:]
    down = jnp.concatenate([shared()[j, :SLICE, :].astype(f32) for j in range(NBLK)], axis=0)
    grad_down.ref[...] = down.T[:BW] * (1.0 / math.sqrt(SEQ))


def exchange(values):
    return lax.all_to_all(
        values.reshape(NSEQ, ROWS, -1), "seq", split_axis=0, concat_axis=0, tiled=True
    ).reshape(values.shape)


def step_to(step):
    dy, dx = step
    return [(y * 4 + x, (y + dy) % 2 * 4 + (x + dx) % 4) for y in range(2) for x in range(4)]


def on_device(inputs, cotangent, kernel, inner_weight, outer_weight, twiddle, up_weight, down_weight):
    mix_flops = 2 * BW * TOK * INNER
    col_flops = 4 * OUTER * OUTER * LANES
    mlp_flops = 2 * HB * BW * TOK
    send, first = call(
        rows_in,
        [((OUTER, LANES), bf16), ((BW, TOK), bf16)],
        inputs,
        inner_weight,
        twiddle,
        flops=mix_flops,
        scratch=[TURNED, STAGE],
    )

    cotangent_late, down_late, send = lax.optimization_barrier((cotangent, down_weight, send))
    block = jnp.concatenate([cotangent_late.astype(bf16), down_late], axis=1)
    straight, onward = gather_over_chan(block)
    shared = (block,) + straight + onward()
    shared = Stacked(shared, (NBLK, BW, TOK + HB), block_places)

    kernel_t = kernel.astype(bf16).transpose(2, 1, 0).reshape(OUTER, LANES)
    outer_t = outer_weight.T
    up_t = up_weight.T

    recv, *straight = lax.optimization_barrier((exchange(send),) + straight)
    send, spectrum = call(
        columns,
        [((OUTER, LANES), bf16), ((OUTER, LANES), bf16)],
        recv,
        outer_weight,
        kernel_t,
        outer_t,
        flops=col_flops,
    )
    recv = exchange(send)
    send, later, direct = call(
        mlp,
        [((OUTER, WIDE), bf16), ((ROWS, INNER), f32), ((BW, TOK), f32)],
        recv,
        inner_weight,
        twiddle,
        inputs,
        up_weight,
        shared,
        up_t,
        cotangent,
        flops=2 * mix_flops + 5 * mlp_flops,
        trans=2 * HB * TOK,
        scratch=[
            TURNED,
            STAGE,
            TURNED,
            STAGE,
            pltpu.VMEM((HB, BW), f32),
            pltpu.VMEM((HB, BW), bf16),
            pltpu.VMEM((HB, BW), f32),
            pltpu.VMEM((HB, BW), f32),
        ],
    )
    recv = exchange(send)

    send, grad_spec = call(
        columns,
        [((OUTER, WIDE), bf16), ((OUTER, LANES), f32)],
        recv,
        outer_weight,
        kernel_t,
        outer_t,
        flops=col_flops,
    )
    recv = exchange(send)
    grad_kernel = (grad_spec * spectrum.astype(f32)).reshape(OUTER, COLS, BW).transpose(2, 1, 0)

    shared, grad_back, grad_up = call(
        twiddle_terms,
        [((NBLK, SLICE + 2 * ROWS, LANE_TILE), bf16), ((BW, TOK), bf16), ((HB, BW), f32)],
        recv,
        first,
        later,
        twiddle,
        scratch=[TURNED, STAGE],
    )
    shared = lax.all_to_all(shared, "chan", split_axis=0, concat_axis=0, tiled=True)
    (grad_inputs,) = call(
        rows_out, [((BW, TOK), f32)], grad_back, inner_weight, direct, flops=mix_flops
    )
    grad_down, grad_twiddle = call(finish, [((BW, HB), f32), ((ROWS, INNER), f32)], shared)
    return grad_inputs, grad_kernel, grad_up, grad_down, grad_twiddle


def solution(mesh):
    placed = (
        P("chan", "seq"),
        P("chan", "seq"),
        P("chan", "seq", None),
        P(),
        P(),
        P("seq", None),
        P("chan", None),
        P("chan", None),
    )
    return jax.shard_map(
        on_device,
        mesh=mesh,
        in_specs=placed,
        out_specs=(
            P("chan", "seq"),
            P("chan", "seq", None),
            P("chan", None),
            P("chan", None),
            P("seq", None),
        ),
        check_vma=False,
    )
```

time: 302 us -> 222 us (0.74)
  waiting for transfers between devices: 158 us -> 30.5 us
  blocking collectives: 28 us -> 91.7 us
  local copies, waits for them, and re-layouts: 32 us -> 8.5 us
  Pallas kernels: 14 us -> 26.3 us
  other arithmetic: 5.96 us -> 0.14 us
    all_to_all x8 -> x3, waiting for transfers between devices: 158 us -> 4.9 us  [the longest x2 3.02 us: exchange(): lax.all_to_all(values.reshape(NSEQ, ROWS, -1), 'seq', split_axis=0, conca...]
    all_to_all x1 -> x2, blocking collectives: 28 us -> 91.7 us  [exchange(): lax.all_to_all(values.reshape(NSEQ, ROWS, -1), 'seq', split_axis=0, conca...]
    ppermute x0 -> x8, starting transfers between devices: none -> 27.5 us  [the longest x4 14.5 us: gather_over_chan(): lax.ppermute(block, 'chan', step_to(step))]
    all_to_all x8 -> x3, starting transfers between devices: 61 us -> 34.2 us  [the longest x2 30.7 us: exchange(): lax.all_to_all(values.reshape(NSEQ, ROWS, -1), 'seq', split_axis=0, conca...]
    ppermute x0 -> x8, waiting for transfers between devices: none -> 25.6 us  [the longest x4 15.2 us: gather_over_chan(): lax.ppermute(block, 'chan', step_to(step))]
    unnamed x64 -> x43, local copies, waits for them, and re-layouts: 25.7 us -> 7.26 us
    pallas_call x7, Pallas kernels: 14 us -> 26.3 us  [call(): pl.pallas_call(kernel, out_shape=shapes, in_specs=[pl.BlockSpec(memory_sp...]
    concatenate x2 -> x1, other arithmetic: 3.09 us -> 0.03 us  [on_device(): block = jnp.concatenate([cotangent_late.astype(bf16), down_late], axis=1)]
  transfers between devices with their start and end apart: 8 -> 11, of which waited for: 8 -> 7; matrix products, arithmetic and copies ran while one was open for 6% -> 3% of each run, Pallas kernels for 1% -> 1%
where the time goes in v2:
time: 222 us; the launch traced here: 220 us
  blocking collectives  91.7 us (41%)
  starting transfers between devices  61.7 us (28%)
  waiting for transfers between devices  30.5 us (14%)
  Pallas kernels  26.3 us (12%)
  local copies, waits for them, and re-layouts  8.5 us (4%)
    all_to_all x2, blocking collectives, exchange(): lax.all_to_all(values.reshape(NSEQ, ROWS, -1), 'seq', split_axis=0, conca...  91.7 us
    all_to_all x2, starting transfers between devices, exchange(): lax.all_to_all(values.reshape(NSEQ, ROWS, -1), 'seq', split_axis=0, conca...  30.7 us
    pallas_call x7, Pallas kernels, call(): pl.pallas_call(kernel, out_shape=shapes, in_specs=[pl.BlockSpec(memory_sp...  26.3 us
    ppermute x4, waiting for transfers between devices, gather_over_chan(): lax.ppermute(block, 'chan', step_to(step))  15.2 us
    ppermute x4, starting transfers between devices, gather_over_chan(): lax.ppermute(block, 'chan', step_to(step))  14.5 us
    unnamed x43, local copies, waits for them, and re-layouts  7.26 us
    ppermute x1, waiting for transfers between devices, onward(): lax.ppermute(right[half:], 'chan', step_to((0, 3)))  5.38 us
    ppermute x1, waiting for transfers between devices, onward(): lax.ppermute(left[:half], 'chan', step_to((0, 1)))  5 us
  transfers between devices with their start and end apart: 11, of which 7 were waited for; matrix products, arithmetic and copies ran while one was open for 3% of the time, Pallas kernels for 1%

profile of v2, /device:TPU:1, one launch (start us, length us, event | category | flops | bytes accessed | tf_op | source)
XLA Modules:
  0.0 220.0 jit_solution(12298503395275450373)
XLA Ops:
  0.6 0.0 copy-start.1
  0.6 3.2 %shard_map.119 = (bf16[512,384]{1,0:T(8,128)(2,1)}, bf16[96,2048]{1,0:T(8,128)(2,1)}) custom-call(f32[96,2048]{1,0:T(8,128)} %refs_3_.2, bf16[256,256]{1,0:T(8,128)(2,1)} %refs_1_.9, f32[8,256]{1,0:T(8,128)} %refs_3_.3), custom_call_target="tpu_custom_call" | custom-call | flops 100663296 | bytes 1712128 | tf_op jit(solution)/shard_map/pallas_call | solution.py:98
  3.8 18.2 %all-to-all-start = ((bf16[64,8,384]{2,1,0:T(8,128)(2,1)}), bf16[64,8,384]{2,1,0:T(8,128)(2,1)S(1)}, u32[]{:S(2)}, u32[]{:S(2)}) async-start(bf16[64,8,384]{2,1,0:T(8,128)(2,1)} %bitcast.26), calls=%async_computation | async-start | bytes 786432 | tf_op jit(solution)/shard_map/all_to_all | solution.py:306
  22.0 0.0 copy-start.18
  22.0 0.0 copy-start.7
  22.1 0.8 copy-done.18
  23.0 0.0 copy-start.2
  23.0 7.0 %collective-permute-start.3 = (bf16[96,2432]{1,0:T(8,128)(2,1)S(1)}, bf16[96,2432]{1,0:T(8,128)(2,1)S(1)}, u32[]{:S(2)}, u32[]{:S(2)}) collective-permute-start(bf16[96,2432]{1,0:T(8,128)(2,1)S(1)} %pad_maximum_fusion.refs_5_), channel_id=1, source_target_pairs={{0,6},{1,7},{2,4},{3,5},{4,2},{5,3},{6,0},{7,1},{8,14},{9,15},{10,... | collective-permute-start | bytes 1400840 | tf_op jit(solution)/shard_map/ppermute | solution.py:229
  30.0 2.8 %collective-permute-start.2 = (bf16[96,2432]{1,0:T(8,128)(2,1)S(1)}, bf16[96,2432]{1,0:T(8,128)(2,1)S(1)}, u32[]{:S(2)}, u32[]{:S(2)}) collective-permute-start(bf16[96,2432]{1,0:T(8,128)(2,1)S(1)} %pad_maximum_fusion.refs_5_), channel_id=1, source_target_pairs={{0,3},{1,0},{2,1},{3,2},{4,7},{5,4},{6,5},{7,6},{8,11},{9,8},{10,9... | collective-permute-start | bytes 1400840 | tf_op jit(solution)/shard_map/ppermute | solution.py:229
  32.7 2.5 %collective-permute-start.1 = (bf16[96,2432]{1,0:T(8,128)(2,1)S(1)}, bf16[96,2432]{1,0:T(8,128)(2,1)S(1)}, u32[]{:S(2)}, u32[]{:S(2)}) collective-permute-start(bf16[96,2432]{1,0:T(8,128)(2,1)S(1)} %pad_maximum_fusion.refs_5_), channel_id=1, source_target_pairs={{0,1},{1,2},{2,3},{3,0},{4,5},{5,6},{6,7},{7,4},{8,9},{9,10},{10,1... | collective-permute-start | bytes 1400840 | tf_op jit(solution)/shard_map/ppermute | solution.py:229
  35.3 2.3 %collective-permute-start = (bf16[96,2432]{1,0:T(8,128)(2,1)S(1)}, bf16[96,2432]{1,0:T(8,128)(2,1)}, u32[]{:S(2)}, u32[]{:S(2)}) collective-permute-start(bf16[96,2432]{1,0:T(8,128)(2,1)S(1)} %pad_maximum_fusion.refs_5_), channel_id=1, source_target_pairs={{0,4},{1,5},{2,6},{3,7},{4,0},{5,1},{6,2},{7,3},{8,12},{9,13},{10,... | collective-permute-start | bytes 1400840 | tf_op jit(solution)/shard_map/ppermute | solution.py:229
  37.5 0.2 copy.27
  37.8 0.0 copy-start
  37.8 0.9 copy.20.refs_2_
  38.7 0.1 copy-done
  38.8 1.0 copy.19
  39.8 3.3 %collective-permute-done.3.refs_9_ = bf16[96,2432]{1,0:T(8,128)(2,1)S(1)} collective-permute-done((bf16[96,2432]{1,0:T(8,128)(2,1)S(1)}, bf16[96,2432]{1,0:T(8,128)(2,1)S(1)}, u32[]{:S(2)}, u32[]{:S(2)}) %collective-permute-start.3) | collective-permute-done | bytes 466976 | tf_op jit(solution)/shard_map/ppermute | solution.py:229
  43.1 8.9 %collective-permute-done.2.refs_8_ = bf16[96,2432]{1,0:T(8,128)(2,1)S(1)} collective-permute-done((bf16[96,2432]{1,0:T(8,128)(2,1)S(1)}, bf16[96,2432]{1,0:T(8,128)(2,1)S(1)}, u32[]{:S(2)}, u32[]{:S(2)}) %collective-permute-start.2) | collective-permute-done | bytes 466976 | tf_op jit(solution)/shard_map/ppermute | solution.py:229
  52.1 3.0 %collective-permute-done.refs_6_ = bf16[96,2432]{1,0:T(8,128)(2,1)} collective-permute-done((bf16[96,2432]{1,0:T(8,128)(2,1)S(1)}, bf16[96,2432]{1,0:T(8,128)(2,1)}, u32[]{:S(2)}, u32[]{:S(2)}) %collective-permute-start) | collective-permute-done | bytes 466976 | tf_op jit(solution)/shard_map/ppermute | solution.py:229
  55.0 0.0 all-to-all-done
  55.1 0.7 copy-done.4
  55.8 3.1 %shard_map.120 = (bf16[512,384]{1,0:T(8,128)(2,1)}, bf16[512,384]{1,0:T(8,128)(2,1)}) custom-call(bf16[512,384]{1,0:T(8,128)(2,1)} %bitcast.22, bf16[512,512]{1,0:T(8,128)(2,1)} %refs_1_.8, bf16[512,384]{1,0:T(8,128)(2,1)} %copy.20.refs_2_, bf16[512,512]{1,0:T(8,128)(2,1)} %bitcast.16), custom_call_target="tpu_custom_call" | custom-call | flops 402653184 | bytes 2621440 | tf_op jit(solution)/shard_map/pallas_call | solution.py:98
  58.9 12.5 %all-to-all-start.1 = ((bf16[64,8,384]{2,1,0:T(8,128)(2,1)}), bf16[64,8,384]{2,1,0:T(8,128)(2,1)S(1)}, u32[]{:S(2)}, u32[]{:S(2)}) async-start(bf16[64,8,384]{2,1,0:T(8,128)(2,1)} %bitcast.27), calls=%async_computation.1 | async-start | bytes 786432 | tf_op jit(solution)/shard_map/all_to_all | solution.py:306
  71.4 4.4 %collective-permute-start.5 = (bf16[96,2432]{1,0:T(8,128)(2,1)}, bf16[96,2432]{1,0:T(8,128)(2,1)S(1)}, u32[]{:S(2)}, u32[]{:S(2)}) collective-permute-start(bf16[96,2432]{1,0:T(8,128)(2,1)} %collective-permute-done.refs_6_), channel_id=1, source_target_pairs={{0,3},{1,0},{2,1},{3,2},{4,7},{5,4},{6,5},{7,6},{8,11},{9,8},{10,9... | collective-permute-start | bytes 1400840 | tf_op jit(solution)/shard_map/ppermute | solution.py:235
  75.8 1.9 collective-permute-start.4
  77.8 0.0 copy-start.14
  77.8 4.7 %collective-permute-start.7 = (bf16[48,2432]{1,0:T(8,128)(2,1)S(1)}, bf16[48,2432]{1,0:T(8,128)(2,1)S(1)}, u32[]{:S(2)}, u32[]{:S(2)}) collective-permute-start(bf16[48,2432]{1,0:T(8,128)(2,1)S(1)} %slice.9), channel_id=1, source_target_pairs={{0,3},{1,0},{2,1},{3,2},{4,7},{5,4},{6,5},{7,6},{8,11},{9,8},{10,9... | collective-permute-start | bytes 700424 | tf_op jit(solution)/shard_map/ppermute | solution.py:237
  82.5 1.9 collective-permute-start.6
  84.5 0.8 copy.21.refs_4_
  85.2 5.4 %collective-permute-done.7.refs_13_ = bf16[48,2432]{1,0:T(8,128)(2,1)S(1)} collective-permute-done((bf16[48,2432]{1,0:T(8,128)(2,1)S(1)}, bf16[48,2432]{1,0:T(8,128)(2,1)S(1)}, u32[]{:S(2)}, u32[]{:S(2)}) %collective-permute-start.7) | collective-permute-done | bytes 233504 | tf_op jit(solution)/shard_map/ppermute | solution.py:237
  90.6 5.0 %collective-permute-done.6.refs_12_ = bf16[48,2432]{1,0:T(8,128)(2,1)S(1)} collective-permute-done((bf16[48,2432]{1,0:T(8,128)(2,1)S(1)}, bf16[48,2432]{1,0:T(8,128)(2,1)S(1)}, u32[]{:S(2)}, u32[]{:S(2)}) %collective-permute-start.6) | collective-permute-done | bytes 233504 | tf_op jit(solution)/shard_map/ppermute | solution.py:236
  95.6 3.0 %all-to-all-done.1 = bf16[64,8,384]{2,1,0:T(8,128)(2,1)S(1)} async-done(((bf16[64,8,384]{2,1,0:T(8,128)(2,1)}), bf16[64,8,384]{2,1,0:T(8,128)(2,1)S(1)}, u32[]{:S(2)}, u32[]{:S(2)}) %all-to-all-start.1) | async-done | bytes 393248 | tf_op jit(solution)/shard_map/all_to_all | solution.py:306
  98.7 0.7 copy-done.3
  99.4 9.4 %shard_map.121 = (bf16[512,640]{1,0:T(8,128)(2,1)}, f32[8,256]{1,0:T(8,128)}, f32[96,2048]{1,0:T(8,128)}) custom-call(bf16[512,384]{1,0:T(8,128)(2,1)} %bitcast.21, bf16[256,256]{1,0:T(8,128)(2,1)} %refs_1_.9, f32[8,256]{1,0:T(8,128)} %refs_3_.3, f32[96,2048]{1,0:T(8,128)} %refs_3_.2, bf16[384,96]{1,0:T(8,128)(2,1)} %copy.21.refs_4_, ...), custom_call_target="tpu_custom_call" | custom-call | flops 956301312 | bytes 7438336 | tf_op jit(solution)/shard_map/pallas_call | solution.py:98
  108.8 48.5 %all_to_all.25 = bf16[64,8,640]{2,1,0:T(8,128)(2,1)} all-to-all(bf16[64,8,640]{2,1,0:T(8,128)(2,1)} %bitcast.24), channel_id=1, replica_groups=mesh['seq'=64,'chan'=8] {'seq'}, dimensions={0} | all-to-all | bytes 1310720 | tf_op jit(solution)/shard_map/all_to_all | solution.py:306
  157.3 3.3 %shard_map.122 = (bf16[512,640]{1,0:T(8,128)(2,1)}, f32[512,384]{1,0:T(8,128)}) custom-call(bf16[512,640]{1,0:T(8,128)(2,1)} %bitcast.20, bf16[512,512]{1,0:T(8,128)(2,1)} %refs_1_.8, bf16[512,384]{1,0:T(8,128)(2,1)} %copy.20.refs_2_, bf16[512,512]{1,0:T(8,128)(2,1)} %bitcast.17), custom_call_target="tpu_custom_call" | custom-call | flops 402653184 | bytes 3538944 | tf_op jit(solution)/shard_map/pallas_call | solution.py:98
  160.5 43.3 %all_to_all.26 = bf16[64,8,640]{2,1,0:T(8,128)(2,1)} all-to-all(bf16[64,8,640]{2,1,0:T(8,128)(2,1)} %bitcast.25), channel_id=1, replica_groups=mesh['seq'=64,'chan'=8] {'seq'}, dimensions={0} | all-to-all | bytes 1310720 | tf_op jit(solution)/shard_map/all_to_all | solution.py:306
  203.8 3.1 %shard_map.123 = (bf16[8,64,128]{2,1,0:T(8,128)(2,1)}, bf16[96,2048]{1,0:T(8,128)(2,1)}, f32[384,96]{1,0:T(8,128)}) custom-call(bf16[512,640]{1,0:T(8,128)(2,1)} %bitcast.19, bf16[96,2048]{1,0:T(8,128)(2,1)} %get-tuple-element.31.refs_1_, f32[8,256]{1,0:T(8,128)} %get-tuple-element.32.refs_2_, f32[8,256]{1,0:T(8,128)} %refs_3_.3), custom_call_target="tpu_custom_call" | custom-call | bytes 1736704 | tf_op jit(solution)/shard_map/pallas_call | solution.py:98
  206.9 3.6 %all-to-all-start.4 = ((bf16[8,64,128]{2,1,0:T(8,128)(2,1)}), bf16[8,64,128]{2,1,0:T(8,128)(2,1)S(1)}, u32[]{:S(2)}, u32[]{:S(2)}) async-start(bf16[8,64,128]{2,1,0:T(8,128)(2,1)} %get-tuple-element.38), calls=%async_computation.4 | async-start | bytes 262144 | tf_op jit(solution)/shard_map/all_to_all | solution.py:398
  210.5 0.1 convert_multiply_fusion
  210.6 0.3 copy.23
  210.9 0.0 copy-start.17
  210.9 1.4 copy.24
  212.3 0.8 copy.25
  213.0 2.5 %shard_map.124 = f32[96,2048]{1,0:T(8,128)} custom-call(bf16[96,2048]{1,0:T(8,128)(2,1)} %get-tuple-element.33.refs_0_, bf16[256,256]{1,0:T(8,128)(2,1)} %refs_1_.9, f32[96,2048]{1,0:T(8,128)} %get-tuple-element.34.refs_2_), custom_call_target="tpu_custom_call" | custom-call | flops 100663296 | bytes 2097152 | tf_op jit(solution)/shard_map/pallas_call | solution.py:98
  215.6 1.9 all-to-all-done.4.refs_0_
  217.4 0.6 copy-done.9
  218.1 1.8 shard_map.125
  (33 shorter events, 0.2 us)
Async XLA Ops:
  0.6 21.4 %copy-start.1 = (f32[96,2048]{1,0:T(8,128)S(1)}, f32[96,2048]{1,0:T(8,128)}, u32[]{:S(2)}) copy-start(f32[96,2048]{1,0:T(8,128)} %refs_15_.1) | copy-start | bytes 2359300
  3.8 51.2 %all-to-all-start = ((bf16[64,8,384]{2,1,0:T(8,128)(2,1)}), bf16[64,8,384]{2,1,0:T(8,128)(2,1)S(1)}, u32[]{:S(2)}, u32[]{:S(2)}) async-start(bf16[64,8,384]{2,1,0:T(8,128)(2,1)} %bitcast.26), calls=%async_computation | async-start | bytes 786432 | tf_op jit(solution)/shard_map/all_to_all | solution.py:306
  22.0 0.9 copy-start.18
  22.0 15.5 %copy-start.7 = (f32[96,4,512]{2,1,0:T(4,128)S(1)}, f32[96,4,512]{2,1,0:T(4,128)}, u32[]{:S(2)}) copy-start(f32[96,4,512]{2,1,0:T(4,128)} %param.10) | copy-start | bytes 2359300
  23.0 14.8 %copy-start.2 = (bf16[96,2432]{1,0:T(8,128)(2,1)}, bf16[96,2432]{1,0:T(8,128)(2,1)S(1)}, u32[]{:S(2)}) copy-start(bf16[96,2432]{1,0:T(8,128)(2,1)S(1)} %pad_maximum_fusion.refs_5_) | copy-start | bytes 1400836
  23.0 20.2 %collective-permute-start.3 = (bf16[96,2432]{1,0:T(8,128)(2,1)S(1)}, bf16[96,2432]{1,0:T(8,128)(2,1)S(1)}, u32[]{:S(2)}, u32[]{:S(2)}) collective-permute-start(bf16[96,2432]{1,0:T(8,128)(2,1)S(1)} %pad_maximum_fusion.refs_5_), channel_id=1, source_target_pairs={{0,6},{1,7},{2,4},{3,5},{4,2},{5,3},{6,0},{7,1},{8,14},{9,15},{10,... | collective-permute-start | bytes 1400840 | tf_op jit(solution)/shard_map/ppermute | solution.py:229
  30.0 22.1 %collective-permute-start.2 = (bf16[96,2432]{1,0:T(8,128)(2,1)S(1)}, bf16[96,2432]{1,0:T(8,128)(2,1)S(1)}, u32[]{:S(2)}, u32[]{:S(2)}) collective-permute-start(bf16[96,2432]{1,0:T(8,128)(2,1)S(1)} %pad_maximum_fusion.refs_5_), channel_id=1, source_target_pairs={{0,3},{1,0},{2,1},{3,2},{4,7},{5,4},{6,5},{7,6},{8,11},{9,8},{10,9... | collective-permute-start | bytes 1400840 | tf_op jit(solution)/shard_map/ppermute | solution.py:229
  32.7 19.3 %collective-permute-start.1 = (bf16[96,2432]{1,0:T(8,128)(2,1)S(1)}, bf16[96,2432]{1,0:T(8,128)(2,1)S(1)}, u32[]{:S(2)}, u32[]{:S(2)}) collective-permute-start(bf16[96,2432]{1,0:T(8,128)(2,1)S(1)} %pad_maximum_fusion.refs_5_), channel_id=1, source_target_pairs={{0,1},{1,2},{2,3},{3,0},{4,5},{5,6},{6,7},{7,4},{8,9},{9,10},{10,1... | collective-permute-start | bytes 1400840 | tf_op jit(solution)/shard_map/ppermute | solution.py:229
  35.3 19.8 %collective-permute-start = (bf16[96,2432]{1,0:T(8,128)(2,1)S(1)}, bf16[96,2432]{1,0:T(8,128)(2,1)}, u32[]{:S(2)}, u32[]{:S(2)}) collective-permute-start(bf16[96,2432]{1,0:T(8,128)(2,1)S(1)} %pad_maximum_fusion.refs_5_), channel_id=1, source_target_pairs={{0,4},{1,5},{2,6},{3,7},{4,0},{5,1},{6,2},{7,3},{8,12},{9,13},{10,... | collective-permute-start | bytes 1400840 | tf_op jit(solution)/shard_map/ppermute | solution.py:229
  37.8 1.0 copy-start
  43.1 34.6 %copy-start.10 = (bf16[96,2432]{1,0:T(8,128)(2,1)}, bf16[96,2432]{1,0:T(8,128)(2,1)S(1)}, u32[]{:S(2)}) copy-start(bf16[96,2432]{1,0:T(8,128)(2,1)S(1)} %collective-permute-done.3.refs_9_) | copy-start | bytes 1400836
  52.1 25.7 %copy-start.5 = (bf16[96,2432]{1,0:T(8,128)(2,1)}, bf16[96,2432]{1,0:T(8,128)(2,1)S(1)}, u32[]{:S(2)}) copy-start(bf16[96,2432]{1,0:T(8,128)(2,1)S(1)} %collective-permute-done.2.refs_8_) | copy-start | bytes 1400836
  52.1 30.5 %copy-start.6 = (bf16[96,2432]{1,0:T(8,128)(2,1)}, bf16[96,2432]{1,0:T(8,128)(2,1)S(1)}, u32[]{:S(2)}) copy-start(bf16[96,2432]{1,0:T(8,128)(2,1)S(1)} %collective-permute-done.1.refs_7_) | copy-start | bytes 1400836
  55.1 0.7 copy-start.4
  58.9 39.8 %all-to-all-start.1 = ((bf16[64,8,384]{2,1,0:T(8,128)(2,1)}), bf16[64,8,384]{2,1,0:T(8,128)(2,1)S(1)}, u32[]{:S(2)}, u32[]{:S(2)}) async-start(bf16[64,8,384]{2,1,0:T(8,128)(2,1)} %bitcast.27), calls=%async_computation.1 | async-start | bytes 786432 | tf_op jit(solution)/shard_map/all_to_all | solution.py:306
  71.4 24.2 %collective-permute-start.5 = (bf16[96,2432]{1,0:T(8,128)(2,1)}, bf16[96,2432]{1,0:T(8,128)(2,1)S(1)}, u32[]{:S(2)}, u32[]{:S(2)}) collective-permute-start(bf16[96,2432]{1,0:T(8,128)(2,1)} %collective-permute-done.refs_6_), channel_id=1, source_target_pairs={{0,3},{1,0},{2,1},{3,2},{4,7},{5,4},{6,5},{7,6},{8,11},{9,8},{10,9... | collective-permute-start | bytes 1400840 | tf_op jit(solution)/shard_map/ppermute | solution.py:235
  75.8 19.8 %collective-permute-start.4 = (bf16[96,2432]{1,0:T(8,128)(2,1)}, bf16[96,2432]{1,0:T(8,128)(2,1)S(1)}, u32[]{:S(2)}, u32[]{:S(2)}) collective-permute-start(bf16[96,2432]{1,0:T(8,128)(2,1)} %collective-permute-done.refs_6_), channel_id=1, source_target_pairs={{0,1},{1,2},{2,3},{3,0},{4,5},{5,6},{6,7},{7,4},{8,9},{9,10},{10,1... | collective-permute-start | bytes 1400840 | tf_op jit(solution)/shard_map/ppermute | solution.py:234
  77.8 6.7 %copy-start.14 = (bf16[384,96]{0,1:T(8,128)(2,1)S(1)}, bf16[384,96]{0,1:T(8,128)(2,1)}, u32[]{:S(2)}) copy-start(bf16[384,96]{0,1:T(8,128)(2,1)} %param.14) | copy-start | bytes 221188
  77.8 12.8 %collective-permute-start.7 = (bf16[48,2432]{1,0:T(8,128)(2,1)S(1)}, bf16[48,2432]{1,0:T(8,128)(2,1)S(1)}, u32[]{:S(2)}, u32[]{:S(2)}) collective-permute-start(bf16[48,2432]{1,0:T(8,128)(2,1)S(1)} %slice.9), channel_id=1, source_target_pairs={{0,3},{1,0},{2,1},{3,2},{4,7},{5,4},{6,5},{7,6},{8,11},{9,8},{10,9... | collective-permute-start | bytes 700424 | tf_op jit(solution)/shard_map/ppermute | solution.py:237
  82.5 13.1 %collective-permute-start.6 = (bf16[48,2432]{1,0:T(8,128)(2,1)S(1)}, bf16[48,2432]{1,0:T(8,128)(2,1)S(1)}, u32[]{:S(2)}, u32[]{:S(2)}) collective-permute-start(bf16[48,2432]{1,0:T(8,128)(2,1)S(1)} %slice.8), channel_id=1, source_target_pairs={{0,1},{1,2},{2,3},{3,0},{4,5},{5,6},{6,7},{7,4},{8,9},{9,10},{10,1... | collective-permute-start | bytes 700424 | tf_op jit(solution)/shard_map/ppermute | solution.py:236
  90.6 8.1 %copy-start.15 = (bf16[48,2432]{1,0:T(8,128)(2,1)}, bf16[48,2432]{1,0:T(8,128)(2,1)S(1)}, u32[]{:S(2)}) copy-start(bf16[48,2432]{1,0:T(8,128)(2,1)S(1)} %collective-permute-done.7.refs_13_) | copy-start | bytes 700420
  95.6 3.1 %copy-start.16 = (bf16[48,2432]{1,0:T(8,128)(2,1)}, bf16[48,2432]{1,0:T(8,128)(2,1)S(1)}, u32[]{:S(2)}) copy-start(bf16[48,2432]{1,0:T(8,128)(2,1)S(1)} %collective-permute-done.6.refs_12_) | copy-start | bytes 700420
  95.6 3.0 %copy-start.11 = (bf16[96,2432]{1,0:T(8,128)(2,1)}, bf16[96,2432]{1,0:T(8,128)(2,1)S(1)}, u32[]{:S(2)}) copy-start(bf16[96,2432]{1,0:T(8,128)(2,1)S(1)} %collective-permute-done.5.refs_11_) | copy-start | bytes 1400836
  95.6 3.0 %copy-start.12 = (bf16[96,2432]{1,0:T(8,128)(2,1)}, bf16[96,2432]{1,0:T(8,128)(2,1)S(1)}, u32[]{:S(2)}) copy-start(bf16[96,2432]{1,0:T(8,128)(2,1)S(1)} %collective-permute-done.4.refs_10_) | copy-start | bytes 1400836
  98.7 0.8 copy-start.3
  203.8 6.7 %copy-start.8 = (f32[512,384]{1,0:T(8,128)S(1)}, f32[512,384]{1,0:T(8,128)}, u32[]{:S(2)}) copy-start(f32[512,384]{1,0:T(8,128)} %get-tuple-element.35) | copy-start | bytes 2359300
  203.8 6.7 %copy-start.13 = (bf16[512,384]{1,0:T(8,128)(2,1)S(1)}, bf16[512,384]{1,0:T(8,128)(2,1)}, u32[]{:S(2)}) copy-start(bf16[512,384]{1,0:T(8,128)(2,1)} %get-tuple-element.36) | copy-start | bytes 1179652
  206.9 10.5 %all-to-all-start.4 = ((bf16[8,64,128]{2,1,0:T(8,128)(2,1)}), bf16[8,64,128]{2,1,0:T(8,128)(2,1)S(1)}, u32[]{:S(2)}, u32[]{:S(2)}) async-start(bf16[8,64,128]{2,1,0:T(8,128)(2,1)} %get-tuple-element.38), calls=%async_computation.4 | async-start | bytes 262144 | tf_op jit(solution)/shard_map/all_to_all | solution.py:398
  210.9 1.4 copy-start.17
  217.4 0.6 copy-start.9

commit v3 on v2

--- a/solution.py
+++ b/solution.py
@@ -46,24 +46,30 @@
     nbytes = sum(math.prod(o.shape) * o.dtype.itemsize for o in list(operands) + shapes)
     arrays = []
     for operand in operands:
-        arrays += operand.parts if isinstance(operand, Stacked) else [operand]
+        arrays += list(operand.parts) if isinstance(operand, Stacked) else [operand]
     n_in, n_out = len(operands), len(shapes)
 
     def kernel(*refs):
         sources, targets, refs = refs[: len(arrays)], refs[len(arrays) : len(arrays) + n_out], refs[len(arrays) + n_out :]
         held, built, refs = refs[:n_in], refs[n_in : n_in + n_out], refs[n_in + n_out :]
         in_sems, out_sems, refs = refs[0], refs[1], refs[2:]
-        loads, taken = [], 0
+        loads, taken, n_copies = [], 0, 0
         for operand, ref in zip(operands, held):
             if isinstance(operand, Stacked):
-                places = operand.places(ref)
+                moves = [
+                    (source.at[pl.ds(start, rows)], place)
+                    for source, places in zip(sources[taken:], operand.places(ref))
+                    for start, rows, place in places
+                ]
+                taken += len(operand.parts)
             else:
-                places = [ref]
+                moves = [(sources[taken], ref)]
+                taken += 1
             copies = []
-            for place in places:
-                copies.append(pltpu.make_async_copy(sources[taken], place, in_sems.at[taken]))
+            for source, place in moves:
+                copies.append(pltpu.make_async_copy(source, place, in_sems.at[n_copies]))
                 copies[-1].start()
-                taken += 1
+                n_copies += 1
             loads.append(copies)
 
         def ready(i):
@@ -101,7 +107,7 @@
         in_specs=[pl.BlockSpec(memory_space=pltpu.HBM)] * len(arrays),
         out_specs=[pl.BlockSpec(memory_space=pltpu.HBM)] * n_out,
         scratch_shapes=[pltpu.VMEM(o.shape, o.dtype) for o in list(operands) + shapes]
-        + [pltpu.SemaphoreType.DMA((len(arrays),)), pltpu.SemaphoreType.DMA((n_out, ROWS))]
+        + [pltpu.SemaphoreType.DMA((2 * len(arrays),)), pltpu.SemaphoreType.DMA((n_out, ROWS))]
         + list(scratch),
         cost_estimate=pl.CostEstimate(flops=flops, bytes_accessed=nbytes, transcendentals=trans),
         compiler_params=pltpu.CompilerParams(vmem_limit_bytes=60 * 1024 * 1024),
@@ -226,18 +232,12 @@
 
 
 def gather_over_chan(block):
-    across, left, right, far = (lax.ppermute(block, "chan", step_to(step)) for step in ((1, 0), (0, 1), (0, 3), (1, 2)))
+    straight = [lax.ppermute(block, "chan", step_to(step)) for step in ((1, 0), (0, 1), (0, 3), (1, 2))]
+    across, left, right, far = lax.optimization_barrier(straight)
     half = BW // 2
-
-    def onward():
-        return (
-            lax.ppermute(across, "chan", step_to((0, 1))),
-            lax.ppermute(across, "chan", step_to((0, 3))),
-            lax.ppermute(left[:half], "chan", step_to((0, 1))),
-            lax.ppermute(right[half:], "chan", step_to((0, 3))),
-        )
-
-    return (across, left, right, far), onward
+    onward_left = lax.ppermute(jnp.concatenate([across, left[:half]]), "chan", step_to((0, 1)))
+    onward_right = lax.ppermute(jnp.concatenate([across, right[half:]]), "chan", step_to((0, 3)))
+    return block, across, left, right, far, onward_left, onward_right
 
 
 def block_places(ref):
@@ -247,17 +247,14 @@
     def at(dy, dx):
         return ref.at[(me // 4 + dy) % 2 * 4 + (me % 4 + dx) % 4]
 
-    opposite = at(0, 2)
     return [
-        at(0, 0),
-        at(1, 0),
-        at(0, 3),
-        at(0, 1),
-        at(1, 2),
-        at(1, 3),
-        at(1, 1),
-        opposite.at[pl.ds(0, half)],
-        opposite.at[pl.ds(half, half)],
+        [(0, BW, at(0, 0))],
+        [(0, BW, at(1, 0))],
+        [(0, BW, at(0, 3))],
+        [(0, BW, at(0, 1))],
+        [(0, BW, at(1, 2))],
+        [(0, BW, at(1, 3)), (BW, half, at(0, 2).at[pl.ds(0, half)])],
+        [(0, BW, at(1, 1)), (BW, half, at(0, 2).at[pl.ds(half, half)])],
     ]
 
 
@@ -329,15 +326,13 @@
 
     cotangent_late, down_late, send = lax.optimization_barrier((cotangent, down_weight, send))
     block = jnp.concatenate([cotangent_late.astype(bf16), down_late], axis=1)
-    straight, onward = gather_over_chan(block)
-    shared = (block,) + straight + onward()
-    shared = Stacked(shared, (NBLK, BW, TOK + HB), block_places)
+    shared = Stacked(gather_over_chan(block), (NBLK, BW, TOK + HB), block_places)
 
     kernel_t = kernel.astype(bf16).transpose(2, 1, 0).reshape(OUTER, LANES)
     outer_t = outer_weight.T
     up_t = up_weight.T
 
-    recv, *straight = lax.optimization_barrier((exchange(send),) + straight)
+    recv = exchange(send)
     send, spectrum = call(
         columns,
         [((OUTER, LANES), bf16), ((OUTER, LANES), bf16)],

time: 222 us -> 210 us (0.946)
  starting transfers between devices: 61.7 us -> 48.3 us
    ppermute x4, waiting for transfers between devices: 15.2 us -> 0.01 us  [gather_over_chan(): lax.ppermute(block, 'chan', step_to(step))]
    all_to_all x2, waiting for transfers between devices: 3.02 us -> 12.1 us  [exchange(): lax.all_to_all(values.reshape(NSEQ, ROWS, -1), 'seq', split_axis=0, conca...]
    all_to_all x2, starting transfers between devices: 30.7 us -> 23.4 us  [exchange(): lax.all_to_all(values.reshape(NSEQ, ROWS, -1), 'seq', split_axis=0, conca...]
    ppermute x4 -> x2, starting transfers between devices: 12.9 us -> 6.3 us  [the longest x1 4.37 us: gather_over_chan(): lax.ppermute(jnp.concatenate([across, right[half:]]), 'chan', step_to((0,...]
    ppermute x4 -> x2, waiting for transfers between devices: 10.4 us -> 16.9 us  [the longest x1 12.2 us: gather_over_chan(): lax.ppermute(jnp.concatenate([across, right[half:]]), 'chan', step_to((0,...]
    unnamed x43 -> x39, local copies, waits for them, and re-layouts: 7.26 us -> 6.45 us
  transfers between devices with their start and end apart: 11 -> 9, of which waited for: 7 -> 5; matrix products, arithmetic and copies ran while one was open for 3% -> 3% of each run, Pallas kernels for 1% -> 3%
where the time goes in v3:
time: 210 us; the launch traced here: 209 us
  blocking collectives  92.7 us (44%)
  starting transfers between devices  48.3 us (23%)
  waiting for transfers between devices  30.8 us (15%)
  Pallas kernels  26.6 us (13%)
  local copies, waits for them, and re-layouts  7.68 us (4%)
    all_to_all x2, blocking collectives, exchange(): lax.all_to_all(values.reshape(NSEQ, ROWS, -1), 'seq', split_axis=0, conca...  92.7 us
    pallas_call x7, Pallas kernels, call(): pl.pallas_call(kernel, out_shape=shapes, in_specs=[pl.BlockSpec(memory_sp...  26.6 us
    all_to_all x2, starting transfers between devices, exchange(): lax.all_to_all(values.reshape(NSEQ, ROWS, -1), 'seq', split_axis=0, conca...  23.4 us
    ppermute x4, starting transfers between devices, gather_over_chan(): lax.ppermute(block, 'chan', step_to(step))  14.7 us
    ppermute x1, waiting for transfers between devices, gather_over_chan(): lax.ppermute(jnp.concatenate([across, right[half:]]), 'chan', step_to((0,...  12.2 us
    all_to_all x2, waiting for transfers between devices, exchange(): lax.all_to_all(values.reshape(NSEQ, ROWS, -1), 'seq', split_axis=0, conca...  12.1 us
    unnamed x39, local copies, waits for them, and re-layouts  6.45 us
    ppermute x1, waiting for transfers between devices, gather_over_chan(): lax.ppermute(jnp.concatenate([across, left[:half]]), 'chan', step_to((0,...  4.68 us
  transfers between devices with their start and end apart: 9, of which 5 were waited for; matrix products, arithmetic and copies ran while one was open for 3% of the time, Pallas kernels for 3%

profile of v3, /device:TPU:1, one launch (start us, length us, event | category | flops | bytes accessed | tf_op | source)
XLA Modules:
  0.0 208.5 jit_solution(9698542668190822127)
XLA Ops:
  0.6 0.0 copy-start.1
  0.6 3.2 %shard_map.119 = (bf16[512,384]{1,0:T(8,128)(2,1)}, bf16[96,2048]{1,0:T(8,128)(2,1)}) custom-call(f32[96,2048]{1,0:T(8,128)} %refs_3_.2, bf16[256,256]{1,0:T(8,128)(2,1)} %refs_1_.9, f32[8,256]{1,0:T(8,128)} %refs_3_.3), custom_call_target="tpu_custom_call" | custom-call | flops 100663296 | bytes 1712128 | tf_op jit(solution)/shard_map/pallas_call | solution.py:104
  3.9 0.0 copy-start.16
  3.9 18.3 %all-to-all-start = ((bf16[64,8,384]{2,1,0:T(8,128)(2,1)}), bf16[64,8,384]{2,1,0:T(8,128)(2,1)S(1)}, u32[]{:S(2)}, u32[]{:S(2)}) async-start(bf16[64,8,384]{2,1,0:T(8,128)(2,1)} %bitcast.27), calls=%async_computation | async-start | bytes 786432 | tf_op jit(solution)/shard_map/all_to_all | solution.py:303
  22.2 0.0 copy-done.1
  22.2 0.0 copy-start.8
  22.3 0.0 copy-start
  22.3 7.1 %collective-permute-start.3 = (bf16[96,2432]{1,0:T(8,128)(2,1)S(1)}, bf16[96,2432]{1,0:T(8,128)(2,1)}, u32[]{:S(2)}, u32[]{:S(2)}) collective-permute-start(bf16[96,2432]{1,0:T(8,128)(2,1)S(1)} %pad_maximum_fusion.2.refs_5_), channel_id=1, source_target_pairs={{0,6},{1,7},{2,4},{3,5},{4,2},{5,3},{6,0},{7,1},{8,14},{9,15},{10,... | collective-permute-start | bytes 1400840 | tf_op jit(solution)/shard_map/ppermute | solution.py:235
  29.5 2.8 %collective-permute-start.2 = (bf16[96,2432]{1,0:T(8,128)(2,1)S(1)}, bf16[96,2432]{1,0:T(8,128)(2,1)S(1)}, u32[]{:S(2)}, u32[]{:S(2)}) collective-permute-start(bf16[96,2432]{1,0:T(8,128)(2,1)S(1)} %pad_maximum_fusion.2.refs_5_), channel_id=1, source_target_pairs={{0,3},{1,0},{2,1},{3,2},{4,7},{5,4},{6,5},{7,6},{8,11},{9,8},{10,9... | collective-permute-start | bytes 1400840 | tf_op jit(solution)/shard_map/ppermute | solution.py:235
  32.2 2.5 %collective-permute-start.1 = (bf16[96,2432]{1,0:T(8,128)(2,1)S(1)}, bf16[96,2432]{1,0:T(8,128)(2,1)S(1)}, u32[]{:S(2)}, u32[]{:S(2)}) collective-permute-start(bf16[96,2432]{1,0:T(8,128)(2,1)S(1)} %pad_maximum_fusion.2.refs_5_), channel_id=1, source_target_pairs={{0,1},{1,2},{2,3},{3,0},{4,5},{5,6},{6,7},{7,4},{8,9},{9,10},{10,1... | collective-permute-start | bytes 1400840 | tf_op jit(solution)/shard_map/ppermute | solution.py:235
  34.8 2.3 %collective-permute-start = (bf16[96,2432]{1,0:T(8,128)(2,1)S(1)}, bf16[96,2432]{1,0:T(8,128)(2,1)S(1)}, u32[]{:S(2)}, u32[]{:S(2)}) collective-permute-start(bf16[96,2432]{1,0:T(8,128)(2,1)S(1)} %pad_maximum_fusion.2.refs_5_), channel_id=1, source_target_pairs={{0,4},{1,5},{2,6},{3,7},{4,0},{5,1},{6,2},{7,3},{8,12},{9,13},{10,... | collective-permute-start | bytes 1400840 | tf_op jit(solution)/shard_map/ppermute | solution.py:235
  37.0 0.2 copy.27
  37.3 0.9 copy.20.refs_2_
  38.2 1.0 copy.19
  39.2 10.2 %all-to-all-done = bf16[64,8,384]{2,1,0:T(8,128)(2,1)S(1)} async-done(((bf16[64,8,384]{2,1,0:T(8,128)(2,1)}), bf16[64,8,384]{2,1,0:T(8,128)(2,1)S(1)}, u32[]{:S(2)}, u32[]{:S(2)}) %all-to-all-start) | async-done | bytes 393248 | tf_op jit(solution)/shard_map/all_to_all | solution.py:303
  49.4 0.7 copy-done.5
  50.2 3.1 %shard_map.120 = (bf16[512,384]{1,0:T(8,128)(2,1)}, bf16[512,384]{1,0:T(8,128)(2,1)}) custom-call(bf16[512,384]{1,0:T(8,128)(2,1)} %bitcast.22, bf16[512,512]{1,0:T(8,128)(2,1)} %refs_1_.8, bf16[512,384]{1,0:T(8,128)(2,1)} %copy.20.refs_2_, bf16[512,512]{1,0:T(8,128)(2,1)} %bitcast.16), custom_call_target="tpu_custom_call" | custom-call | flops 402653184 | bytes 2621440 | tf_op jit(solution)/shard_map/pallas_call | solution.py:104
  53.3 5.1 %all-to-all-start.1 = ((bf16[64,8,384]{2,1,0:T(8,128)(2,1)}), bf16[64,8,384]{2,1,0:T(8,128)(2,1)S(1)}, u32[]{:S(2)}, u32[]{:S(2)}) async-start(bf16[64,8,384]{2,1,0:T(8,128)(2,1)} %bitcast.26), calls=%async_computation.1 | async-start | bytes 786432 | tf_op jit(solution)/shard_map/all_to_all | solution.py:303
  58.4 0.0 collective-permute-done.3.refs_9_
  58.4 0.0 collective-permute-done.2.refs_8_
  58.5 0.0 collective-permute-done.1.refs_7_
  58.5 0.0 collective-permute-done.refs_6_
  58.5 0.0 copy-start.3
  58.6 0.0 copy-start.14
  58.6 1.2 pad_maximum_fusion
  59.7 0.1 copy-done.3
  59.8 4.4 %collective-permute-start.5 = (bf16[144,2432]{1,0:T(8,128)(2,1)}, bf16[144,2432]{1,0:T(8,128)(2,1)S(1)}, u32[]{:S(2)}, u32[]{:S(2)}) collective-permute-start(bf16[144,2432]{1,0:T(8,128)(2,1)} %get-tuple-element.57), channel_id=1, source_target_pairs={{0,3},{1,0},{2,1},{3,2},{4,7},{5,4},{6,5},{7,6},{8,11},{9,8},{10,9... | collective-permute-start | bytes 2101256 | tf_op jit(solution)/shard_map/ppermute | solution.py:239
  64.2 1.9 collective-permute-start.4
  66.1 0.8 copy.21.refs_4_
  66.9 12.2 %collective-permute-done.5.refs_11_ = bf16[144,2432]{1,0:T(8,128)(2,1)S(1)} collective-permute-done((bf16[144,2432]{1,0:T(8,128)(2,1)}, bf16[144,2432]{1,0:T(8,128)(2,1)S(1)}, u32[]{:S(2)}, u32[]{:S(2)}) %collective-permute-start.5) | collective-permute-done | bytes 700448 | tf_op jit(solution)/shard_map/ppermute | solution.py:239
  79.1 4.7 %collective-permute-done.4.refs_10_ = bf16[144,2432]{1,0:T(8,128)(2,1)S(1)} collective-permute-done((bf16[144,2432]{1,0:T(8,128)(2,1)S(1)}, bf16[144,2432]{1,0:T(8,128)(2,1)S(1)}, u32[]{:S(2)}, u32[]{:S(2)}) %collective-permute-start.4) | collective-permute-done | bytes 700448 | tf_op jit(solution)/shard_map/ppermute | solution.py:238
  83.8 1.9 all-to-all-done.1
  85.7 0.7 copy-done.4
  86.4 9.5 %shard_map.121 = (bf16[512,640]{1,0:T(8,128)(2,1)}, f32[8,256]{1,0:T(8,128)}, f32[96,2048]{1,0:T(8,128)}) custom-call(bf16[512,384]{1,0:T(8,128)(2,1)} %bitcast.21, bf16[256,256]{1,0:T(8,128)(2,1)} %refs_1_.9, f32[8,256]{1,0:T(8,128)} %refs_3_.3, f32[96,2048]{1,0:T(8,128)} %refs_3_.2, bf16[384,96]{1,0:T(8,128)(2,1)} %copy.21.refs_4_, ...), custom_call_target="tpu_custom_call" | custom-call | flops 956301312 | bytes 7438336 | tf_op jit(solution)/shard_map/pallas_call | solution.py:104
  95.9 49.4 %all_to_all.25 = bf16[64,8,640]{2,1,0:T(8,128)(2,1)} all-to-all(bf16[64,8,640]{2,1,0:T(8,128)(2,1)} %bitcast.24), channel_id=1, replica_groups=mesh['seq'=64,'chan'=8] {'seq'}, dimensions={0} | all-to-all | bytes 1310720 | tf_op jit(solution)/shard_map/all_to_all | solution.py:303
  145.3 3.3 %shard_map.122 = (bf16[512,640]{1,0:T(8,128)(2,1)}, f32[512,384]{1,0:T(8,128)}) custom-call(bf16[512,640]{1,0:T(8,128)(2,1)} %bitcast.20, bf16[512,512]{1,0:T(8,128)(2,1)} %refs_1_.8, bf16[512,384]{1,0:T(8,128)(2,1)} %copy.20.refs_2_, bf16[512,512]{1,0:T(8,128)(2,1)} %bitcast.17), custom_call_target="tpu_custom_call" | custom-call | flops 402653184 | bytes 3538944 | tf_op jit(solution)/shard_map/pallas_call | solution.py:104
  148.7 43.3 %all_to_all.26 = bf16[64,8,640]{2,1,0:T(8,128)(2,1)} all-to-all(bf16[64,8,640]{2,1,0:T(8,128)(2,1)} %bitcast.25), channel_id=1, replica_groups=mesh['seq'=64,'chan'=8] {'seq'}, dimensions={0} | all-to-all | bytes 1310720 | tf_op jit(solution)/shard_map/all_to_all | solution.py:303
  191.9 3.1 %shard_map.123 = (bf16[8,64,128]{2,1,0:T(8,128)(2,1)}, bf16[96,2048]{1,0:T(8,128)(2,1)}, f32[384,96]{1,0:T(8,128)}) custom-call(bf16[512,640]{1,0:T(8,128)(2,1)} %bitcast.19, bf16[96,2048]{1,0:T(8,128)(2,1)} %get-tuple-element.37.refs_1_, f32[8,256]{1,0:T(8,128)} %get-tuple-element.38.refs_2_, f32[8,256]{1,0:T(8,128)} %refs_3_.3), custom_call_target="tpu_custom_call" | custom-call | bytes 1736704 | tf_op jit(solution)/shard_map/pallas_call | solution.py:104
  195.1 3.9 %all-to-all-start.4 = ((bf16[8,64,128]{2,1,0:T(8,128)(2,1)}), bf16[8,64,128]{2,1,0:T(8,128)(2,1)S(1)}, u32[]{:S(2)}, u32[]{:S(2)}) async-start(bf16[8,64,128]{2,1,0:T(8,128)(2,1)} %get-tuple-element.44), calls=%async_computation.4 | async-start | bytes 262144 | tf_op jit(solution)/shard_map/all_to_all | solution.py:393
  199.0 0.1 convert_multiply_fusion
  199.1 0.3 copy.23
  199.3 0.0 copy-start.15
  199.3 1.4 copy.24
  200.7 0.8 copy.25
  201.5 2.5 %shard_map.124 = f32[96,2048]{1,0:T(8,128)} custom-call(bf16[96,2048]{1,0:T(8,128)(2,1)} %get-tuple-element.39.refs_0_, bf16[256,256]{1,0:T(8,128)(2,1)} %refs_1_.9, f32[96,2048]{1,0:T(8,128)} %get-tuple-element.40.refs_2_), custom_call_target="tpu_custom_call" | custom-call | flops 100663296 | bytes 2097152 | tf_op jit(solution)/shard_map/pallas_call | solution.py:104
  204.1 1.9 all-to-all-done.4.refs_0_
  205.9 0.6 copy-done.12
  206.5 1.8 shard_map.125
  (26 shorter events, 0.2 us)
Async XLA Ops:
  0.6 21.6 %copy-start.1 = (f32[96,2048]{1,0:T(8,128)S(1)}, f32[96,2048]{1,0:T(8,128)}, u32[]{:S(2)}) copy-start(f32[96,2048]{1,0:T(8,128)} %refs_13_.1) | copy-start | bytes 2359300
  3.9 18.4 %copy-start.16 = (bf16[96,384]{1,0:T(8,128)(2,1)S(1)}, bf16[96,384]{1,0:T(8,128)(2,1)}, u32[]{:S(2)}) copy-start(bf16[96,384]{1,0:T(8,128)(2,1)} %param.15) | copy-start | bytes 221188
  3.9 45.6 %all-to-all-start = ((bf16[64,8,384]{2,1,0:T(8,128)(2,1)}), bf16[64,8,384]{2,1,0:T(8,128)(2,1)S(1)}, u32[]{:S(2)}, u32[]{:S(2)}) async-start(bf16[64,8,384]{2,1,0:T(8,128)(2,1)} %bitcast.27), calls=%async_computation | async-start | bytes 786432 | tf_op jit(solution)/shard_map/all_to_all | solution.py:303
  22.2 14.8 %copy-start.8 = (f32[96,4,512]{2,1,0:T(4,128)S(1)}, f32[96,4,512]{2,1,0:T(4,128)}, u32[]{:S(2)}) copy-start(f32[96,4,512]{2,1,0:T(4,128)} %param.10) | copy-start | bytes 2359300
  22.3 15.9 %copy-start.2 = (bf16[96,2432]{1,0:T(8,128)(2,1)}, bf16[96,2432]{1,0:T(8,128)(2,1)S(1)}, u32[]{:S(2)}) copy-start(bf16[96,2432]{1,0:T(8,128)(2,1)S(1)} %pad_maximum_fusion.2.refs_5_) | copy-start | bytes 1400836
  22.3 15.9 %copy-start = (bf16[512,512]{1,0:T(8,128)(2,1)S(1)}, bf16[512,512]{1,0:T(8,128)(2,1)}, u32[]{:S(2)}) copy-start(bf16[512,512]{1,0:T(8,128)(2,1)} %refs_1_.8) | copy-start | bytes 1572868
  22.3 36.1 %collective-permute-start.3 = (bf16[96,2432]{1,0:T(8,128)(2,1)S(1)}, bf16[96,2432]{1,0:T(8,128)(2,1)}, u32[]{:S(2)}, u32[]{:S(2)}) collective-permute-start(bf16[96,2432]{1,0:T(8,128)(2,1)S(1)} %pad_maximum_fusion.2.refs_5_), channel_id=1, source_target_pairs={{0,6},{1,7},{2,4},{3,5},{4,2},{5,3},{6,0},{7,1},{8,14},{9,15},{10,... | collective-permute-start | bytes 1400840 | tf_op jit(solution)/shard_map/ppermute | solution.py:235
  29.5 29.0 %collective-permute-start.2 = (bf16[96,2432]{1,0:T(8,128)(2,1)S(1)}, bf16[96,2432]{1,0:T(8,128)(2,1)S(1)}, u32[]{:S(2)}, u32[]{:S(2)}) collective-permute-start(bf16[96,2432]{1,0:T(8,128)(2,1)S(1)} %pad_maximum_fusion.2.refs_5_), channel_id=1, source_target_pairs={{0,3},{1,0},{2,1},{3,2},{4,7},{5,4},{6,5},{7,6},{8,11},{9,8},{10,9... | collective-permute-start | bytes 1400840 | tf_op jit(solution)/shard_map/ppermute | solution.py:235
  32.2 26.2 %collective-permute-start.1 = (bf16[96,2432]{1,0:T(8,128)(2,1)S(1)}, bf16[96,2432]{1,0:T(8,128)(2,1)S(1)}, u32[]{:S(2)}, u32[]{:S(2)}) collective-permute-start(bf16[96,2432]{1,0:T(8,128)(2,1)S(1)} %pad_maximum_fusion.2.refs_5_), channel_id=1, source_target_pairs={{0,1},{1,2},{2,3},{3,0},{4,5},{5,6},{6,7},{7,4},{8,9},{9,10},{10,1... | collective-permute-start | bytes 1400840 | tf_op jit(solution)/shard_map/ppermute | solution.py:235
  34.8 23.7 %collective-permute-start = (bf16[96,2432]{1,0:T(8,128)(2,1)S(1)}, bf16[96,2432]{1,0:T(8,128)(2,1)S(1)}, u32[]{:S(2)}, u32[]{:S(2)}) collective-permute-start(bf16[96,2432]{1,0:T(8,128)(2,1)S(1)} %pad_maximum_fusion.2.refs_5_), channel_id=1, source_target_pairs={{0,4},{1,5},{2,6},{3,7},{4,0},{5,1},{6,2},{7,3},{8,12},{9,13},{10,... | collective-permute-start | bytes 1400840 | tf_op jit(solution)/shard_map/ppermute | solution.py:235
  49.4 0.7 copy-start.5
  53.3 32.3 %all-to-all-start.1 = ((bf16[64,8,384]{2,1,0:T(8,128)(2,1)}), bf16[64,8,384]{2,1,0:T(8,128)(2,1)S(1)}, u32[]{:S(2)}, u32[]{:S(2)}) async-start(bf16[64,8,384]{2,1,0:T(8,128)(2,1)} %bitcast.26), calls=%async_computation.1 | async-start | bytes 786432 | tf_op jit(solution)/shard_map/all_to_all | solution.py:303
  58.4 1.3 copy-start.6
  58.5 1.3 copy-start.7
  58.5 1.3 copy-start.3
  58.6 7.6 %copy-start.14 = (bf16[384,96]{0,1:T(8,128)(2,1)S(1)}, bf16[384,96]{0,1:T(8,128)(2,1)}, u32[]{:S(2)}) copy-start(bf16[384,96]{0,1:T(8,128)(2,1)} %param.14) | copy-start | bytes 221188
  59.8 19.3 %collective-permute-start.5 = (bf16[144,2432]{1,0:T(8,128)(2,1)}, bf16[144,2432]{1,0:T(8,128)(2,1)S(1)}, u32[]{:S(2)}, u32[]{:S(2)}) collective-permute-start(bf16[144,2432]{1,0:T(8,128)(2,1)} %get-tuple-element.57), channel_id=1, source_target_pairs={{0,3},{1,0},{2,1},{3,2},{4,7},{5,4},{6,5},{7,6},{8,11},{9,8},{10,9... | collective-permute-start | bytes 2101256 | tf_op jit(solution)/shard_map/ppermute | solution.py:239
  64.2 19.6 %collective-permute-start.4 = (bf16[144,2432]{1,0:T(8,128)(2,1)S(1)}, bf16[144,2432]{1,0:T(8,128)(2,1)S(1)}, u32[]{:S(2)}, u32[]{:S(2)}) collective-permute-start(bf16[144,2432]{1,0:T(8,128)(2,1)S(1)} %get-tuple-element.58), channel_id=1, source_target_pairs={{0,1},{1,2},{2,3},{3,0},{4,5},{5,6},{6,7},{7,4},{8,9},{9,10},{10,1... | collective-permute-start | bytes 2101256 | tf_op jit(solution)/shard_map/ppermute | solution.py:238
  79.1 6.6 %copy-start.10 = (bf16[144,2432]{1,0:T(8,128)(2,1)}, bf16[144,2432]{1,0:T(8,128)(2,1)S(1)}, u32[]{:S(2)}) copy-start(bf16[144,2432]{1,0:T(8,128)(2,1)S(1)} %collective-permute-done.5.refs_11_) | copy-start | bytes 2101252
  83.8 1.9 copy-start.11
  85.7 0.7 copy-start.4
  191.9 7.1 %copy-start.9 = (f32[512,384]{1,0:T(8,128)S(1)}, f32[512,384]{1,0:T(8,128)}, u32[]{:S(2)}) copy-start(f32[512,384]{1,0:T(8,128)} %get-tuple-element.41) | copy-start | bytes 2359300
  191.9 7.1 %copy-start.13 = (bf16[512,384]{1,0:T(8,128)(2,1)S(1)}, bf16[512,384]{1,0:T(8,128)(2,1)}, u32[]{:S(2)}) copy-start(bf16[512,384]{1,0:T(8,128)(2,1)} %get-tuple-element.42) | copy-start | bytes 1179652
  195.1 10.8 %all-to-all-start.4 = ((bf16[8,64,128]{2,1,0:T(8,128)(2,1)}), bf16[8,64,128]{2,1,0:T(8,128)(2,1)S(1)}, u32[]{:S(2)}, u32[]{:S(2)}) async-start(bf16[8,64,128]{2,1,0:T(8,128)(2,1)} %get-tuple-element.44), calls=%async_computation.4 | async-start | bytes 262144 | tf_op jit(solution)/shard_map/all_to_all | solution.py:393
  199.3 1.4 copy-start.15
  205.9 0.6 copy-start.12

commit v4 on v3

--- a/solution.py
+++ b/solution.py
@@ -23,7 +23,9 @@
 LANES = COLS * BW
 TOK = ROWS * INNER
 LANE_TILE = 128
-WIDE = LANES + 2 * LANE_TILE
+MIXED = ROWS // 2 * LANES
+PIECES = 2 * HB // (2 * NSEQ)
+WIDE = MIXED + (PIECES * BW + LANE_TILE - 1) // LANE_TILE * LANE_TILE
 
 f32 = jnp.float32
 bf16 = jnp.bfloat16
@@ -123,12 +125,12 @@
     parts = [turned[pl.ds(b, NSEQ, stride=COLS), :][:, :BW] for b in range(COLS)]
     row = jnp.concatenate(parts, axis=1)
     for k in range(LANES // LANE_TILE):
-        stage[k, pl.ds(a, NSEQ, stride=ROWS), :] = row[:, k * LANE_TILE : (k + 1) * LANE_TILE]
+        stage[k, :, a, :] = row[:, k * LANE_TILE : (k + 1) * LANE_TILE]
 
 
 def from_message(a, turned, stage):
     row = jnp.concatenate(
-        [stage[k, pl.ds(a, NSEQ, stride=ROWS), :] for k in range(LANES // LANE_TILE)], axis=1
+        [stage[k, :, a, :] for k in range(LANES // LANE_TILE)], axis=1
     )
     for b in range(COLS):
         turned[pl.ds(b, NSEQ, stride=COLS), :] = jnp.concatenate(
@@ -137,17 +139,36 @@
     return turned[...].T[:BW]
 
 
+def lane_tile(k):
+    return slice(k * LANE_TILE, (k + 1) * LANE_TILE)
+
+
 def pack(stage, send_ref):
     for k in range(LANES // LANE_TILE):
-        send_ref[:, k * LANE_TILE : (k + 1) * LANE_TILE] = stage[k].astype(bf16)
+        send_ref[:, lane_tile(k)] = stage[k].reshape(OUTER, LANE_TILE).astype(bf16)
 
 
 def unpack(recv_ref, stage):
     for k in range(LANES // LANE_TILE):
-        stage[k] = recv_ref[:, k * LANE_TILE : (k + 1) * LANE_TILE].astype(f32)
-
-
-STAGE = pltpu.VMEM((LANES // LANE_TILE, OUTER, LANE_TILE), f32)
+        stage[k] = recv_ref[:, lane_tile(k)].astype(f32).reshape(NSEQ, ROWS, LANE_TILE)
+
+
+def pairs():
+    tiles = LANES // LANE_TILE
+    return [(h * tiles + k, slice(2 * h, 2 * h + 2), k) for h in range(ROWS // 2) for k in range(tiles)]
+
+
+def pack_wide(stage, send_ref):
+    for tile, rows, k in pairs():
+        send_ref[:, :, lane_tile(tile)] = stage[k, :, rows, :].astype(bf16)
+
+
+def unpack_wide(recv_ref, stage):
+    for tile, rows, k in pairs():
+        stage[k, :, rows, :] = recv_ref[:, :, lane_tile(tile)].astype(f32)
+
+
+STAGE = pltpu.VMEM((LANES // LANE_TILE, NSEQ, ROWS, LANE_TILE), f32)
 TURNED = pltpu.VMEM((INNER, LANE_TILE), f32)
 
 
@@ -166,17 +187,29 @@
 def columns(ins, outs):
     recv, outer, kernel, outer_t = ins
     send, spec_out = outs
-    spec = dot(outer()[...], recv()[:, :LANES])
-    spec_out.ref[...] = spec.astype(spec_out.ref.dtype)
+    spec = dot(outer()[...], recv()[...])
+    spec_out.ref[...] = spec.astype(bf16)
     spec_out.store()
     scaled = (kernel()[...].astype(f32) * spec).astype(bf16)
-    send.ref[:, :LANES] = dot(outer_t()[...], scaled).astype(bf16)
-    if recv().shape[1] == WIDE:
-        parts = recv()[:, LANES:].astype(f32).reshape(NSEQ, ROWS, WIDE - LANES)
-        total = jnp.sum(parts, axis=0, keepdims=True)
-        send.ref[:, LANES:] = (
-            jnp.broadcast_to(total, parts.shape).reshape(OUTER, WIDE - LANES).astype(bf16)
-        )
+    send.ref[...] = dot(outer_t()[...], scaled).astype(bf16)
+
+
+def columns_wide(ins, outs, stage):
+    recv, outer, kernel, outer_t = ins
+    send, spec_out = outs
+    unpack_wide(recv(), stage)
+    tiles = LANES // LANE_TILE
+    rows = jnp.concatenate([stage[k].reshape(OUTER, LANE_TILE).astype(bf16) for k in range(tiles)], axis=1)
+    spec = dot(outer()[...], rows)
+    spec_out.ref[...] = spec
+    spec_out.store()
+    total = jnp.sum(recv()[:, :, MIXED:].astype(f32), axis=0, keepdims=True)
+    send.ref[:, :, MIXED:] = jnp.broadcast_to(total, (NSEQ, 2, WIDE - MIXED)).astype(bf16)
+    scaled = (kernel()[...].astype(f32) * spec).astype(bf16)
+    back = dot(outer_t()[...], scaled)
+    for k in range(tiles):
+        stage[k] = back[:, lane_tile(k)].reshape(NSEQ, ROWS, LANE_TILE)
+    pack_wide(stage, send.ref)
 
 
 def mlp(ins, outs, turned, stage, turned_out, stage_out, down_t, down_own, grad_up, grad_down):
@@ -224,11 +257,12 @@
         second = dot(grad_mix, w()[...], NT)
         later.ref[a : a + 1, :] = jnp.sum(second * back, axis=0, keepdims=True)
         to_message(second * scale, a, turned_out, stage_out)
-    pack(stage_out, send.ref)
-    zeros = jnp.zeros((HB, LANE_TILE - BW), f32)
-    for start, total in ((LANES, grad_up), (LANES + LANE_TILE, grad_down)):
-        send.ref[:HB, start : start + LANE_TILE] = jnp.concatenate([total[...], zeros], axis=1).astype(bf16)
-    send.ref[HB:, LANES:] = jnp.zeros((OUTER - HB, WIDE - LANES), bf16)
+    pack_wide(stage_out, send.ref)
+    grads = jnp.concatenate([grad_up[...], grad_down[...]], axis=0)
+    pieces = [grads[i * 2 * NSEQ : (i + 1) * 2 * NSEQ] for i in range(PIECES)]
+    pieces.append(jnp.zeros((2 * NSEQ, WIDE - MIXED - PIECES * BW), f32))
+    grads = jnp.concatenate(pieces, axis=1).reshape(NSEQ, 2, WIDE - MIXED)
+    send.ref[:, :, MIXED:] = grads.astype(bf16)
 
 
 def gather_over_chan(block):
@@ -261,9 +295,7 @@
 def twiddle_terms(ins, outs, turned, stage):
     recv, first, later, twiddle = ins
     shared, grad_back_out, grad_up = outs
-    grad_up.ref[...] = recv()[:HB, LANES : LANES + BW].astype(f32) * (1.0 / math.sqrt(SEQ))
-    grad_up.store()
-    unpack(recv(), stage)
+    unpack_wide(recv(), stage)
     terms = []
     for a in range(ROWS):
         cols = token_columns(a)
@@ -275,8 +307,13 @@
     grad_back_out.store()
     terms = jnp.concatenate(terms, axis=0)
     terms = jnp.concatenate([terms[:, :LANE_TILE], terms[:, LANE_TILE:]], axis=0).astype(bf16)
+    grads = recv()[:, :, MIXED:].astype(f32).reshape(2 * NSEQ, WIDE - MIXED)
+    grads = jnp.concatenate([grads[:, i * BW : (i + 1) * BW] for i in range(PIECES)], axis=0)
+    grad_up.ref[...] = grads[:HB] * (1.0 / math.sqrt(SEQ))
+    zeros = jnp.zeros((SLICE, LANE_TILE - BW), f32)
     for p in range(NBLK):
-        shared.ref[p, :SLICE, :] = recv()[p * SLICE : (p + 1) * SLICE, LANES + LANE_TILE :]
+        rows = slice(HB + p * SLICE, HB + (p + 1) * SLICE)
+        shared.ref[p, :SLICE, :] = jnp.concatenate([grads[rows], zeros], axis=1).astype(bf16)
         shared.ref[p, SLICE:, :] = terms
 
 
@@ -301,7 +338,7 @@
 
 def exchange(values):
     return lax.all_to_all(
-        values.reshape(NSEQ, ROWS, -1), "seq", split_axis=0, concat_axis=0, tiled=True
+        values.reshape(NSEQ, -1, values.shape[-1]), "seq", split_axis=0, concat_axis=0, tiled=True
     ).reshape(values.shape)
 
 
@@ -345,7 +382,7 @@
     recv = exchange(send)
     send, later, direct = call(
         mlp,
-        [((OUTER, WIDE), bf16), ((ROWS, INNER), f32), ((BW, TOK), f32)],
+        [((NSEQ, 2, WIDE), bf16), ((ROWS, INNER), f32), ((BW, TOK), f32)],
         recv,
         inner_weight,
         twiddle,
@@ -370,13 +407,14 @@
     recv = exchange(send)
 
     send, grad_spec = call(
-        columns,
-        [((OUTER, WIDE), bf16), ((OUTER, LANES), f32)],
+        columns_wide,
+        [((NSEQ, 2, WIDE), bf16), ((OUTER, LANES), f32)],
         recv,
         outer_weight,
         kernel_t,
         outer_t,
         flops=col_flops,
+        scratch=[STAGE],
     )
     recv = exchange(send)
     grad_kernel = (grad_spec * spectrum.astype(f32)).reshape(OUTER, COLS, BW).transpose(2, 1, 0)

time: 210 us -> 204 us (0.971)
  blocking collectives: 92.7 us -> 85.3 us
    all_to_all x2, blocking collectives: 92.7 us -> 85.3 us  [exchange(): lax.all_to_all(values.reshape(NSEQ, -1, values.shape[-1]), 'seq', split_a...]
where the time goes in v4:
time: 204 us; the launch traced here: 203 us
  blocking collectives  85.3 us (42%)
  starting transfers between devices  48.2 us (24%)
  waiting for transfers between devices  31.1 us (15%)
  Pallas kernels  28.1 us (14%)
  local copies, waits for them, and re-layouts  7.63 us (4%)
    all_to_all x2, blocking collectives, exchange(): lax.all_to_all(values.reshape(NSEQ, -1, values.shape[-1]), 'seq', split_a...  85.3 us
    pallas_call x7, Pallas kernels, call(): pl.pallas_call(kernel, out_shape=shapes, in_specs=[pl.BlockSpec(memory_sp...  28.1 us
    all_to_all x2, starting transfers between devices, exchange(): lax.all_to_all(values.reshape(NSEQ, -1, values.shape[-1]), 'seq', split_a...  23.4 us
    ppermute x4, starting transfers between devices, gather_over_chan(): lax.ppermute(block, 'chan', step_to(step))  14.7 us
    ppermute x1, waiting for transfers between devices, gather_over_chan(): lax.ppermute(jnp.concatenate([across, right[half:]]), 'chan', step_to((0,...  12.2 us
    all_to_all x2, waiting for transfers between devices, exchange(): lax.all_to_all(values.reshape(NSEQ, -1, values.shape[-1]), 'seq', split_a...  12.1 us
    unnamed x39, local copies, waits for them, and re-layouts  6.4 us
    ppermute x1, waiting for transfers between devices, gather_over_chan(): lax.ppermute(jnp.concatenate([across, left[:half]]), 'chan', step_to((0,...  4.68 us
  transfers between devices with their start and end apart: 9, of which 5 were waited for; matrix products, arithmetic and copies ran while one was open for 3% of the time, Pallas kernels for 3%

profile of v4, /device:TPU:1, one launch (start us, length us, event | category | flops | bytes accessed | tf_op | source)
XLA Modules:
  0.0 202.8 jit_solution(4368067176956598720)
XLA Ops:
  0.6 0.0 copy-start.1
  0.6 3.4 %shard_map.119 = (bf16[512,384]{1,0:T(8,128)(2,1)}, bf16[96,2048]{1,0:T(8,128)(2,1)}) custom-call(f32[96,2048]{1,0:T(8,128)} %refs_3_.2, bf16[256,256]{1,0:T(8,128)(2,1)} %refs_1_.9, f32[8,256]{1,0:T(8,128)} %refs_3_.3), custom_call_target="tpu_custom_call" | custom-call | flops 100663296 | bytes 1712128 | tf_op jit(solution)/shard_map/pallas_call | solution.py:106
  4.1 0.0 copy-start.16
  4.1 18.3 %all-to-all-start = ((bf16[64,8,384]{2,1,0:T(8,128)(2,1)}), bf16[64,8,384]{2,1,0:T(8,128)(2,1)S(1)}, u32[]{:S(2)}, u32[]{:S(2)}) async-start(bf16[64,8,384]{2,1,0:T(8,128)(2,1)} %bitcast.19), calls=%async_computation | async-start | bytes 786432 | tf_op jit(solution)/shard_map/all_to_all | solution.py:340
  22.4 0.0 copy-start.8
  22.6 0.0 copy-start
  22.6 7.1 %collective-permute-start.3 = (bf16[96,2432]{1,0:T(8,128)(2,1)S(1)}, bf16[96,2432]{1,0:T(8,128)(2,1)}, u32[]{:S(2)}, u32[]{:S(2)}) collective-permute-start(bf16[96,2432]{1,0:T(8,128)(2,1)S(1)} %pad_maximum_fusion.2.refs_5_), channel_id=1, source_target_pairs={{0,6},{1,7},{2,4},{3,5},{4,2},{5,3},{6,0},{7,1},{8,14},{9,15},{10,... | collective-permute-start | bytes 1400840 | tf_op jit(solution)/shard_map/ppermute | solution.py:269
  29.7 2.8 %collective-permute-start.2 = (bf16[96,2432]{1,0:T(8,128)(2,1)S(1)}, bf16[96,2432]{1,0:T(8,128)(2,1)S(1)}, u32[]{:S(2)}, u32[]{:S(2)}) collective-permute-start(bf16[96,2432]{1,0:T(8,128)(2,1)S(1)} %pad_maximum_fusion.2.refs_5_), channel_id=1, source_target_pairs={{0,3},{1,0},{2,1},{3,2},{4,7},{5,4},{6,5},{7,6},{8,11},{9,8},{10,9... | collective-permute-start | bytes 1400840 | tf_op jit(solution)/shard_map/ppermute | solution.py:269
  32.5 2.5 %collective-permute-start.1 = (bf16[96,2432]{1,0:T(8,128)(2,1)S(1)}, bf16[96,2432]{1,0:T(8,128)(2,1)S(1)}, u32[]{:S(2)}, u32[]{:S(2)}) collective-permute-start(bf16[96,2432]{1,0:T(8,128)(2,1)S(1)} %pad_maximum_fusion.2.refs_5_), channel_id=1, source_target_pairs={{0,1},{1,2},{2,3},{3,0},{4,5},{5,6},{6,7},{7,4},{8,9},{9,10},{10,1... | collective-permute-start | bytes 1400840 | tf_op jit(solution)/shard_map/ppermute | solution.py:269
  35.0 2.3 %collective-permute-start = (bf16[96,2432]{1,0:T(8,128)(2,1)S(1)}, bf16[96,2432]{1,0:T(8,128)(2,1)S(1)}, u32[]{:S(2)}, u32[]{:S(2)}) collective-permute-start(bf16[96,2432]{1,0:T(8,128)(2,1)S(1)} %pad_maximum_fusion.2.refs_5_), channel_id=1, source_target_pairs={{0,4},{1,5},{2,6},{3,7},{4,0},{5,1},{6,2},{7,3},{8,12},{9,13},{10,... | collective-permute-start | bytes 1400840 | tf_op jit(solution)/shard_map/ppermute | solution.py:269
  37.3 0.0 copy-done.8
  37.3 0.2 copy.27
  37.5 0.9 copy.20.refs_2_
  38.4 0.0 copy-done
  38.4 1.0 copy.19
  39.5 10.2 %all-to-all-done = bf16[64,8,384]{2,1,0:T(8,128)(2,1)S(1)} async-done(((bf16[64,8,384]{2,1,0:T(8,128)(2,1)}), bf16[64,8,384]{2,1,0:T(8,128)(2,1)S(1)}, u32[]{:S(2)}, u32[]{:S(2)}) %all-to-all-start) | async-done | bytes 393248 | tf_op jit(solution)/shard_map/all_to_all | solution.py:340
  49.7 0.7 copy-done.5
  50.4 3.1 %shard_map.120 = (bf16[512,384]{1,0:T(8,128)(2,1)}, bf16[512,384]{1,0:T(8,128)(2,1)}) custom-call(bf16[512,384]{1,0:T(8,128)(2,1)} %bitcast.16, bf16[512,512]{1,0:T(8,128)(2,1)} %refs_1_.8, bf16[512,384]{1,0:T(8,128)(2,1)} %copy.20.refs_2_, bf16[512,512]{1,0:T(8,128)(2,1)} %bitcast.12), custom_call_target="tpu_custom_call" | custom-call | flops 402653184 | bytes 2621440 | tf_op jit(solution)/shard_map/pallas_call | solution.py:106
  53.6 5.1 %all-to-all-start.1 = ((bf16[64,8,384]{2,1,0:T(8,128)(2,1)}), bf16[64,8,384]{2,1,0:T(8,128)(2,1)S(1)}, u32[]{:S(2)}, u32[]{:S(2)}) async-start(bf16[64,8,384]{2,1,0:T(8,128)(2,1)} %bitcast.18), calls=%async_computation.1 | async-start | bytes 786432 | tf_op jit(solution)/shard_map/all_to_all | solution.py:340
  58.7 0.0 collective-permute-done.3.refs_9_
  58.7 0.0 collective-permute-done.2.refs_8_
  58.7 0.0 collective-permute-done.1.refs_7_
  58.7 0.0 collective-permute-done.refs_6_
  58.8 0.0 copy-start.14
  58.8 1.2 pad_maximum_fusion
  60.0 0.0 copy-done.3
  60.0 4.4 %collective-permute-start.5 = (bf16[144,2432]{1,0:T(8,128)(2,1)}, bf16[144,2432]{1,0:T(8,128)(2,1)S(1)}, u32[]{:S(2)}, u32[]{:S(2)}) collective-permute-start(bf16[144,2432]{1,0:T(8,128)(2,1)} %get-tuple-element.57), channel_id=1, source_target_pairs={{0,3},{1,0},{2,1},{3,2},{4,7},{5,4},{6,5},{7,6},{8,11},{9,8},{10,9... | collective-permute-start | bytes 2101256 | tf_op jit(solution)/shard_map/ppermute | solution.py:273
  64.4 1.9 collective-permute-start.4
  66.4 0.8 copy.21.refs_4_
  67.1 12.2 %collective-permute-done.5.refs_11_ = bf16[144,2432]{1,0:T(8,128)(2,1)S(1)} collective-permute-done((bf16[144,2432]{1,0:T(8,128)(2,1)}, bf16[144,2432]{1,0:T(8,128)(2,1)S(1)}, u32[]{:S(2)}, u32[]{:S(2)}) %collective-permute-start.5) | collective-permute-done | bytes 700448 | tf_op jit(solution)/shard_map/ppermute | solution.py:273
  79.3 4.7 %collective-permute-done.4.refs_10_ = bf16[144,2432]{1,0:T(8,128)(2,1)S(1)} collective-permute-done((bf16[144,2432]{1,0:T(8,128)(2,1)S(1)}, bf16[144,2432]{1,0:T(8,128)(2,1)S(1)}, u32[]{:S(2)}, u32[]{:S(2)}) %collective-permute-start.4) | collective-permute-done | bytes 700448 | tf_op jit(solution)/shard_map/ppermute | solution.py:272
  84.0 1.9 all-to-all-done.1
  85.9 0.7 copy-done.4
  86.7 9.8 %shard_map.121 = (bf16[64,2,2176]{2,1,0:T(2,128)(2,1)}, f32[8,256]{1,0:T(8,128)}, f32[96,2048]{1,0:T(8,128)}) custom-call(bf16[512,384]{1,0:T(8,128)(2,1)} %bitcast.15, bf16[256,256]{1,0:T(8,128)(2,1)} %refs_1_.9, f32[8,256]{1,0:T(8,128)} %refs_3_.3, f32[96,2048]{1,0:T(8,128)} %refs_3_.2, bf16[384,96]{1,0:T(8,128)(2,1)} %copy.21.refs_4_, ...), custom_call_target="tpu_custom_call" | custom-call | flops 956301312 | bytes 7340032 | tf_op jit(solution)/shard_map/pallas_call | solution.py:106
  96.5 46.2 %all_to_all.25.refs_0_ = bf16[64,2,2176]{2,1,0:T(2,128)(2,1)} all-to-all(bf16[64,2,2176]{2,1,0:T(2,128)(2,1)} %get-tuple-element.35), channel_id=1, replica_groups=mesh['seq'=64,'chan'=8] {'seq'}, dimensions={0} | all-to-all | bytes 1114112 | tf_op jit(solution)/shard_map/all_to_all | solution.py:340
  142.7 3.6 %shard_map.122 = (bf16[64,2,2176]{2,1,0:T(2,128)(2,1)}, f32[512,384]{1,0:T(8,128)}) custom-call(bf16[64,2,2176]{2,1,0:T(2,128)(2,1)} %all_to_all.25.refs_0_, bf16[512,512]{1,0:T(8,128)(2,1)} %refs_1_.8, bf16[512,384]{1,0:T(8,128)(2,1)} %copy.20.refs_2_, bf16[512,512]{1,0:T(8,128)(2,1)} %bitcast.13), custom_call_target="tpu_custom_call" | custom-call | flops 402653184 | bytes 3342336 | tf_op jit(solution)/shard_map/pallas_call | solution.py:106
  146.3 39.0 %all_to_all.26.refs_0_ = bf16[64,2,2176]{2,1,0:T(2,128)(2,1)} all-to-all(bf16[64,2,2176]{2,1,0:T(2,128)(2,1)} %get-tuple-element.36), channel_id=1, replica_groups=mesh['seq'=64,'chan'=8] {'seq'}, dimensions={0} | all-to-all | bytes 1114112 | tf_op jit(solution)/shard_map/all_to_all | solution.py:340
  185.4 3.7 %shard_map.123 = (bf16[8,64,128]{2,1,0:T(8,128)(2,1)}, bf16[96,2048]{1,0:T(8,128)(2,1)}, f32[384,96]{1,0:T(8,128)}) custom-call(bf16[64,2,2176]{2,1,0:T(2,128)(2,1)} %all_to_all.26.refs_0_, bf16[96,2048]{1,0:T(8,128)(2,1)} %get-tuple-element.37.refs_1_, f32[8,256]{1,0:T(8,128)} %get-tuple-element.38.refs_2_, f32[8,256]{1,0:T(8,128)} %refs_3_.3), custom_call_target="tpu_custom_call" | custom-call | bytes 1638400 | tf_op jit(solution)/shard_map/pallas_call | solution.py:106
  189.1 3.9 %all-to-all-start.4 = ((bf16[8,64,128]{2,1,0:T(8,128)(2,1)}), bf16[8,64,128]{2,1,0:T(8,128)(2,1)S(1)}, u32[]{:S(2)}, u32[]{:S(2)}) async-start(bf16[8,64,128]{2,1,0:T(8,128)(2,1)} %get-tuple-element.44), calls=%async_computation.4 | async-start | bytes 262144 | tf_op jit(solution)/shard_map/all_to_all | solution.py:431
  193.0 0.1 convert_multiply_fusion
  193.1 0.3 copy.23
  193.4 0.0 copy-start.15
  193.4 1.4 copy.24
  194.8 0.8 copy.25
  195.6 2.5 %shard_map.124 = f32[96,2048]{1,0:T(8,128)} custom-call(bf16[96,2048]{1,0:T(8,128)(2,1)} %get-tuple-element.39.refs_0_, bf16[256,256]{1,0:T(8,128)(2,1)} %refs_1_.9, f32[96,2048]{1,0:T(8,128)} %get-tuple-element.40.refs_2_), custom_call_target="tpu_custom_call" | custom-call | flops 100663296 | bytes 2097152 | tf_op jit(solution)/shard_map/pallas_call | solution.py:106
  198.1 2.1 %all-to-all-done.4.refs_0_ = bf16[8,64,128]{2,1,0:T(8,128)(2,1)S(1)} async-done(((bf16[8,64,128]{2,1,0:T(8,128)(2,1)}), bf16[8,64,128]{2,1,0:T(8,128)(2,1)S(1)}, u32[]{:S(2)}, u32[]{:S(2)}) %all-to-all-start.4) | async-done | bytes 131104 | tf_op jit(solution)/shard_map/all_to_all | solution.py:431
  200.2 0.6 copy-done.12
  200.8 1.8 shard_map.125
  (26 shorter events, 0.2 us)
Async XLA Ops:
  0.6 21.8 %copy-start.1 = (f32[96,2048]{1,0:T(8,128)S(1)}, f32[96,2048]{1,0:T(8,128)}, u32[]{:S(2)}) copy-start(f32[96,2048]{1,0:T(8,128)} %refs_13_.1) | copy-start | bytes 2359300
  4.1 18.4 %copy-start.16 = (bf16[96,384]{1,0:T(8,128)(2,1)S(1)}, bf16[96,384]{1,0:T(8,128)(2,1)}, u32[]{:S(2)}) copy-start(bf16[96,384]{1,0:T(8,128)(2,1)} %param.15) | copy-start | bytes 221188
  4.1 45.6 %all-to-all-start = ((bf16[64,8,384]{2,1,0:T(8,128)(2,1)}), bf16[64,8,384]{2,1,0:T(8,128)(2,1)S(1)}, u32[]{:S(2)}, u32[]{:S(2)}) async-start(bf16[64,8,384]{2,1,0:T(8,128)(2,1)} %bitcast.19), calls=%async_computation | async-start | bytes 786432 | tf_op jit(solution)/shard_map/all_to_all | solution.py:340
  22.4 14.8 %copy-start.8 = (f32[96,4,512]{2,1,0:T(4,128)S(1)}, f32[96,4,512]{2,1,0:T(4,128)}, u32[]{:S(2)}) copy-start(f32[96,4,512]{2,1,0:T(4,128)} %param.10) | copy-start | bytes 2359300
  22.6 15.9 %copy-start.2 = (bf16[96,2432]{1,0:T(8,128)(2,1)}, bf16[96,2432]{1,0:T(8,128)(2,1)S(1)}, u32[]{:S(2)}) copy-start(bf16[96,2432]{1,0:T(8,128)(2,1)S(1)} %pad_maximum_fusion.2.refs_5_) | copy-start | bytes 1400836
  22.6 15.9 %copy-start = (bf16[512,512]{1,0:T(8,128)(2,1)S(1)}, bf16[512,512]{1,0:T(8,128)(2,1)}, u32[]{:S(2)}) copy-start(bf16[512,512]{1,0:T(8,128)(2,1)} %refs_1_.8) | copy-start | bytes 1572868
  22.6 36.1 %collective-permute-start.3 = (bf16[96,2432]{1,0:T(8,128)(2,1)S(1)}, bf16[96,2432]{1,0:T(8,128)(2,1)}, u32[]{:S(2)}, u32[]{:S(2)}) collective-permute-start(bf16[96,2432]{1,0:T(8,128)(2,1)S(1)} %pad_maximum_fusion.2.refs_5_), channel_id=1, source_target_pairs={{0,6},{1,7},{2,4},{3,5},{4,2},{5,3},{6,0},{7,1},{8,14},{9,15},{10,... | collective-permute-start | bytes 1400840 | tf_op jit(solution)/shard_map/ppermute | solution.py:269
  29.7 29.0 %collective-permute-start.2 = (bf16[96,2432]{1,0:T(8,128)(2,1)S(1)}, bf16[96,2432]{1,0:T(8,128)(2,1)S(1)}, u32[]{:S(2)}, u32[]{:S(2)}) collective-permute-start(bf16[96,2432]{1,0:T(8,128)(2,1)S(1)} %pad_maximum_fusion.2.refs_5_), channel_id=1, source_target_pairs={{0,3},{1,0},{2,1},{3,2},{4,7},{5,4},{6,5},{7,6},{8,11},{9,8},{10,9... | collective-permute-start | bytes 1400840 | tf_op jit(solution)/shard_map/ppermute | solution.py:269
  32.5 26.2 %collective-permute-start.1 = (bf16[96,2432]{1,0:T(8,128)(2,1)S(1)}, bf16[96,2432]{1,0:T(8,128)(2,1)S(1)}, u32[]{:S(2)}, u32[]{:S(2)}) collective-permute-start(bf16[96,2432]{1,0:T(8,128)(2,1)S(1)} %pad_maximum_fusion.2.refs_5_), channel_id=1, source_target_pairs={{0,1},{1,2},{2,3},{3,0},{4,5},{5,6},{6,7},{7,4},{8,9},{9,10},{10,1... | collective-permute-start | bytes 1400840 | tf_op jit(solution)/shard_map/ppermute | solution.py:269
  35.0 23.7 %collective-permute-start = (bf16[96,2432]{1,0:T(8,128)(2,1)S(1)}, bf16[96,2432]{1,0:T(8,128)(2,1)S(1)}, u32[]{:S(2)}, u32[]{:S(2)}) collective-permute-start(bf16[96,2432]{1,0:T(8,128)(2,1)S(1)} %pad_maximum_fusion.2.refs_5_), channel_id=1, source_target_pairs={{0,4},{1,5},{2,6},{3,7},{4,0},{5,1},{6,2},{7,3},{8,12},{9,13},{10,... | collective-permute-start | bytes 1400840 | tf_op jit(solution)/shard_map/ppermute | solution.py:269
  49.7 0.7 copy-start.5
  53.6 32.3 %all-to-all-start.1 = ((bf16[64,8,384]{2,1,0:T(8,128)(2,1)}), bf16[64,8,384]{2,1,0:T(8,128)(2,1)S(1)}, u32[]{:S(2)}, u32[]{:S(2)}) async-start(bf16[64,8,384]{2,1,0:T(8,128)(2,1)} %bitcast.18), calls=%async_computation.1 | async-start | bytes 786432 | tf_op jit(solution)/shard_map/all_to_all | solution.py:340
  58.7 1.3 copy-start.6
  58.7 1.3 copy-start.7
  58.7 1.3 copy-start.3
  58.8 7.6 %copy-start.14 = (bf16[384,96]{0,1:T(8,128)(2,1)S(1)}, bf16[384,96]{0,1:T(8,128)(2,1)}, u32[]{:S(2)}) copy-start(bf16[384,96]{0,1:T(8,128)(2,1)} %param.14) | copy-start | bytes 221188
  60.0 19.3 %collective-permute-start.5 = (bf16[144,2432]{1,0:T(8,128)(2,1)}, bf16[144,2432]{1,0:T(8,128)(2,1)S(1)}, u32[]{:S(2)}, u32[]{:S(2)}) collective-permute-start(bf16[144,2432]{1,0:T(8,128)(2,1)} %get-tuple-element.57), channel_id=1, source_target_pairs={{0,3},{1,0},{2,1},{3,2},{4,7},{5,4},{6,5},{7,6},{8,11},{9,8},{10,9... | collective-permute-start | bytes 2101256 | tf_op jit(solution)/shard_map/ppermute | solution.py:273
  64.4 19.6 %collective-permute-start.4 = (bf16[144,2432]{1,0:T(8,128)(2,1)S(1)}, bf16[144,2432]{1,0:T(8,128)(2,1)S(1)}, u32[]{:S(2)}, u32[]{:S(2)}) collective-permute-start(bf16[144,2432]{1,0:T(8,128)(2,1)S(1)} %get-tuple-element.58), channel_id=1, source_target_pairs={{0,1},{1,2},{2,3},{3,0},{4,5},{5,6},{6,7},{7,4},{8,9},{9,10},{10,1... | collective-permute-start | bytes 2101256 | tf_op jit(solution)/shard_map/ppermute | solution.py:272
  79.3 6.6 %copy-start.10 = (bf16[144,2432]{1,0:T(8,128)(2,1)}, bf16[144,2432]{1,0:T(8,128)(2,1)S(1)}, u32[]{:S(2)}) copy-start(bf16[144,2432]{1,0:T(8,128)(2,1)S(1)} %collective-permute-done.5.refs_11_) | copy-start | bytes 2101252
  84.0 1.9 copy-start.11
  85.9 0.8 copy-start.4
  185.4 7.6 %copy-start.9 = (f32[512,384]{1,0:T(8,128)S(1)}, f32[512,384]{1,0:T(8,128)}, u32[]{:S(2)}) copy-start(f32[512,384]{1,0:T(8,128)} %get-tuple-element.41) | copy-start | bytes 2359300
  185.4 7.6 %copy-start.13 = (bf16[512,384]{1,0:T(8,128)(2,1)S(1)}, bf16[512,384]{1,0:T(8,128)(2,1)}, u32[]{:S(2)}) copy-start(bf16[512,384]{1,0:T(8,128)(2,1)} %get-tuple-element.42) | copy-start | bytes 1179652
  189.1 11.1 %all-to-all-start.4 = ((bf16[8,64,128]{2,1,0:T(8,128)(2,1)}), bf16[8,64,128]{2,1,0:T(8,128)(2,1)S(1)}, u32[]{:S(2)}, u32[]{:S(2)}) async-start(bf16[8,64,128]{2,1,0:T(8,128)(2,1)} %get-tuple-element.44), calls=%async_computation.4 | async-start | bytes 262144 | tf_op jit(solution)/shard_map/all_to_all | solution.py:431
  193.4 1.4 copy-start.15
  200.2 0.6 copy-start.12

commit v5 on v4

--- a/solution.py
+++ b/solution.py
@@ -29,6 +29,7 @@
 
 f32 = jnp.float32
 bf16 = jnp.bfloat16
+HIDE_FLOPS = 14 * 10**9
 NT = (((1,), (1,)), ((), ()))
 NN = (((1,), (0,)), ((), ()))
 
@@ -43,35 +44,31 @@
         self.dtype = parts[0].dtype
 
 
-def call(body, outs, *operands, flops=0, scratch=(), trans=0):
+def call(body, outs, *operands, flops=0, scratch=(), trans=0, arrived=(0,), grant=32):
     shapes = [jax.ShapeDtypeStruct(shape, dtype) for shape, dtype in outs]
     nbytes = sum(math.prod(o.shape) * o.dtype.itemsize for o in list(operands) + shapes)
-    arrays = []
-    for operand in operands:
-        arrays += list(operand.parts) if isinstance(operand, Stacked) else [operand]
+    arrays, specs = [], []
+    for i, operand in enumerate(operands):
+        parts = list(operand.parts) if isinstance(operand, Stacked) else [operand]
+        arrays += parts
+        specs += [pl.BlockSpec(memory_space=pl.ANY if i in arrived else pltpu.HBM)] * len(parts)
     n_in, n_out = len(operands), len(shapes)
 
     def kernel(*refs):
         sources, targets, refs = refs[: len(arrays)], refs[len(arrays) : len(arrays) + n_out], refs[len(arrays) + n_out :]
         held, built, refs = refs[:n_in], refs[n_in : n_in + n_out], refs[n_in + n_out :]
         in_sems, out_sems, refs = refs[0], refs[1], refs[2:]
-        loads, taken, n_copies = [], 0, 0
+        loads, taken = [], 0
         for operand, ref in zip(operands, held):
             if isinstance(operand, Stacked):
-                moves = [
-                    (source.at[pl.ds(start, rows)], place)
-                    for source, places in zip(sources[taken:], operand.places(ref))
-                    for start, rows, place in places
-                ]
-                taken += len(operand.parts)
+                places = operand.places(ref)
             else:
-                moves = [(sources[taken], ref)]
+                places = [ref]
+            copies = []
+            for place in places:
+                copies.append(pltpu.make_async_copy(sources[taken], place, in_sems.at[taken]))
+                copies[-1].start()
                 taken += 1
-            copies = []
-            for source, place in moves:
-                copies.append(pltpu.make_async_copy(source, place, in_sems.at[n_copies]))
-                copies[-1].start()
-                n_copies += 1
             loads.append(copies)
 
         def ready(i):
@@ -106,13 +103,13 @@
     return pl.pallas_call(
         kernel,
         out_shape=shapes,
-        in_specs=[pl.BlockSpec(memory_space=pltpu.HBM)] * len(arrays),
+        in_specs=specs,
         out_specs=[pl.BlockSpec(memory_space=pltpu.HBM)] * n_out,
         scratch_shapes=[pltpu.VMEM(o.shape, o.dtype) for o in list(operands) + shapes]
-        + [pltpu.SemaphoreType.DMA((2 * len(arrays),)), pltpu.SemaphoreType.DMA((n_out, ROWS))]
+        + [pltpu.SemaphoreType.DMA((len(arrays),)), pltpu.SemaphoreType.DMA((n_out, ROWS))]
         + list(scratch),
         cost_estimate=pl.CostEstimate(flops=flops, bytes_accessed=nbytes, transcendentals=trans),
-        compiler_params=pltpu.CompilerParams(vmem_limit_bytes=60 * 1024 * 1024),
+        compiler_params=pltpu.CompilerParams(vmem_limit_bytes=grant * 1024 * 1024),
     )(*arrays)
 
 
@@ -182,6 +179,19 @@
         to_message(first * twiddle()[a : a + 1, :], a, turned, stage)
     first_out.store()
     pack(stage, send.ref)
+
+
+def transpose_up(ins, outs):
+    (up,) = ins
+    outs[0].ref[...] = up()[...].astype(f32).T.astype(bf16)
+
+
+def prepare(ins, outs):
+    outer, kernel = ins
+    outer_t, kernel_t = outs
+    outer_t.ref[...] = outer()[...].astype(f32).T.astype(bf16)
+    parts = [kernel()[:, b, :].T for b in range(COLS)]
+    kernel_t.ref[...] = jnp.concatenate(parts, axis=1).astype(bf16)
 
 
 def columns(ins, outs):
@@ -212,7 +222,7 @@
     pack_wide(stage, send.ref)
 
 
-def mlp(ins, outs, turned, stage, turned_out, stage_out, down_t, down_own, grad_up, grad_down):
+def mlp(ins, outs, turned, stage, turned_out, stage_out, down_own, grad_up, grad_down):
     recv, w, twiddle, x_in, up, shared, up_t, cot = ins
     send, later, direct = outs
     me = lax.axis_index("chan")
@@ -230,17 +240,20 @@
         act = (hidden * cumulative).astype(bf16)
         slope = cumulative + hidden * density
         if a == 0:
+            column = lax.broadcasted_iota(jnp.int32, (SLICE, HB), 1)
+            own = column == lax.broadcasted_iota(jnp.int32, (SLICE, HB), 0) + me * SLICE
+            own = jnp.where(own, 1.0, 0.0).astype(bf16)
             for p in range(NBLK):
-                down_t[...] = shared()[p, :, TOK:].astype(f32).T
-                own = pl.ds(pl.multiple_of(me * SLICE, SLICE), SLICE)
-                down_own[p * SLICE : (p + 1) * SLICE, :] = down_t[own, :].astype(bf16)
-        grad_act, down_part = [], []
+                down_own[p * SLICE : (p + 1) * SLICE, :] = dot(own, shared()[p, :, TOK:], NT).astype(bf16)
+        grad_act = []
         for p in range(NBLK):
             rows = slice(p * SLICE, (p + 1) * SLICE)
-            cot_low = shared()[p, :, cols]
-            grad_act.append(dot(down_own[rows, :], cot_low).astype(bf16))
-            down_part.append(dot(act[rows], cot_low, NT))
+            grad_act.append(dot(down_own[rows, :], shared()[p, :, cols]).astype(bf16))
         grad_act = jnp.concatenate(grad_act, axis=0).astype(f32)
+        down_part = [
+            dot(act[2 * p * SLICE : 2 * (p + 1) * SLICE], shared()[2 * p : 2 * p + 2, :, cols].reshape(2 * BW, INNER), NT)
+            for p in range(NBLK // 2)
+        ]
         down_part = jnp.concatenate(down_part, axis=0)
         grad_hidden = (grad_act * slope).astype(bf16)
         up_part = dot(grad_hidden, low, NT)
@@ -258,7 +271,10 @@
         later.ref[a : a + 1, :] = jnp.sum(second * back, axis=0, keepdims=True)
         to_message(second * scale, a, turned_out, stage_out)
     pack_wide(stage_out, send.ref)
-    grads = jnp.concatenate([grad_up[...], grad_down[...]], axis=0)
+    grads = [grad_up[...]]
+    for p in range(NBLK):
+        grads.append(grad_down[p * SLICE : (p + 1) * SLICE, p % 2 * BW : (p % 2 + 1) * BW])
+    grads = jnp.concatenate(grads, axis=0)
     pieces = [grads[i * 2 * NSEQ : (i + 1) * 2 * NSEQ] for i in range(PIECES)]
     pieces.append(jnp.zeros((2 * NSEQ, WIDE - MIXED - PIECES * BW), f32))
     grads = jnp.concatenate(pieces, axis=1).reshape(NSEQ, 2, WIDE - MIXED)
@@ -266,64 +282,55 @@
 
 
 def gather_over_chan(block):
-    straight = [lax.ppermute(block, "chan", step_to(step)) for step in ((1, 0), (0, 1), (0, 3), (1, 2))]
-    across, left, right, far = lax.optimization_barrier(straight)
-    half = BW // 2
-    onward_left = lax.ppermute(jnp.concatenate([across, left[:half]]), "chan", step_to((0, 1)))
-    onward_right = lax.ppermute(jnp.concatenate([across, right[half:]]), "chan", step_to((0, 3)))
-    return block, across, left, right, far, onward_left, onward_right
+    steps = ((1, 0), (0, 1), (0, 3), (1, 2))
+    straight = lax.optimization_barrier([lax.ppermute(block, "chan", step_to(step)) for step in steps])
+    across, far = straight[0], straight[3]
+    onward = [
+        lax.ppermute(values, "chan", step_to(step)) for values, step in ((far, (1, 0)), (across, (0, 1)), (across, (0, 3)))
+    ]
+    return [block, *straight, *onward]
 
 
 def block_places(ref):
     me = lax.axis_index("chan")
-    half = BW // 2
-
-    def at(dy, dx):
-        return ref.at[(me // 4 + dy) % 2 * 4 + (me % 4 + dx) % 4]
-
-    return [
-        [(0, BW, at(0, 0))],
-        [(0, BW, at(1, 0))],
-        [(0, BW, at(0, 3))],
-        [(0, BW, at(0, 1))],
-        [(0, BW, at(1, 2))],
-        [(0, BW, at(1, 3)), (BW, half, at(0, 2).at[pl.ds(0, half)])],
-        [(0, BW, at(1, 1)), (BW, half, at(0, 2).at[pl.ds(half, half)])],
-    ]
+    steps = ((0, 0), (1, 0), (0, 3), (0, 1), (1, 2), (0, 2), (1, 3), (1, 1))
+    return [ref.at[(me // 4 + dy) % 2 * 4 + (me % 4 + dx) % 4] for dy, dx in steps]
 
 
 def twiddle_terms(ins, outs, turned, stage):
-    recv, first, later, twiddle = ins
-    shared, grad_back_out, grad_up = outs
+    recv, first, later = ins
+    (shared,) = outs
     unpack_wide(recv(), stage)
     terms = []
     for a in range(ROWS):
+        grad_back = from_message(a, turned, stage)
+        early = jnp.sum(grad_back * first()[:, token_columns(a)].astype(f32), axis=0, keepdims=True)
+        terms.append(early + later()[a : a + 1, :])
+    terms = jnp.concatenate(terms, axis=0)
+    terms = jnp.concatenate([terms[:, :LANE_TILE], terms[:, LANE_TILE:]], axis=0).astype(bf16)
+    grads = weight_grads(recv())[HB:]
+    zeros = jnp.zeros((SLICE, LANE_TILE - BW), f32)
+    for p in range(NBLK):
+        rows = slice(p * SLICE, (p + 1) * SLICE)
+        shared.ref[p, :SLICE, :] = jnp.concatenate([grads[rows], zeros], axis=1).astype(bf16)
+        shared.ref[p, SLICE:, :] = terms
+
+
+def weight_grads(recv_ref):
+    grads = recv_ref[:, :, MIXED:].astype(f32).reshape(2 * NSEQ, WIDE - MIXED)
+    return jnp.concatenate([grads[:, i * BW : (i + 1) * BW] for i in range(PIECES)], axis=0)
+
+
+def rows_out(ins, outs, turned, stage):
+    recv, twiddle, w, direct = ins
+    out, grad_up = outs
+    unpack_wide(recv(), stage)
+    for a in range(ROWS):
         cols = token_columns(a)
         grad_back = from_message(a, turned, stage)
-        terms.append(
-            jnp.sum(grad_back * first()[:, cols].astype(f32), axis=0, keepdims=True) + later()[a : a + 1, :]
-        )
-        grad_back_out.ref[:, cols] = (grad_back * twiddle()[a : a + 1, :]).astype(bf16)
-    grad_back_out.store()
-    terms = jnp.concatenate(terms, axis=0)
-    terms = jnp.concatenate([terms[:, :LANE_TILE], terms[:, LANE_TILE:]], axis=0).astype(bf16)
-    grads = recv()[:, :, MIXED:].astype(f32).reshape(2 * NSEQ, WIDE - MIXED)
-    grads = jnp.concatenate([grads[:, i * BW : (i + 1) * BW] for i in range(PIECES)], axis=0)
-    grad_up.ref[...] = grads[:HB] * (1.0 / math.sqrt(SEQ))
-    zeros = jnp.zeros((SLICE, LANE_TILE - BW), f32)
-    for p in range(NBLK):
-        rows = slice(HB + p * SLICE, HB + (p + 1) * SLICE)
-        shared.ref[p, :SLICE, :] = jnp.concatenate([grads[rows], zeros], axis=1).astype(bf16)
-        shared.ref[p, SLICE:, :] = terms
-
-
-def rows_out(ins, outs):
-    grad_back, w, direct = ins
-    (out,) = outs
-    for a in range(ROWS):
-        cols = token_columns(a)
-        out.ref[:, cols] = direct()[:, cols] + dot(grad_back()[:, cols], w()[...])
+        out.ref[:, cols] = direct()[:, cols] + dot((grad_back * twiddle()[a : a + 1, :]).astype(bf16), w()[...])
         out.store(slice(None), cols)
+    grad_up.ref[...] = weight_grads(recv())[:HB] * (1.0 / math.sqrt(SEQ))
 
 
 def finish(ins, outs):
@@ -359,15 +366,19 @@
         twiddle,
         flops=mix_flops,
         scratch=[TURNED, STAGE],
+        arrived=(),
+        grant=60,
     )
 
     cotangent_late, down_late, send = lax.optimization_barrier((cotangent, down_weight, send))
     block = jnp.concatenate([cotangent_late.astype(bf16), down_late], axis=1)
     shared = Stacked(gather_over_chan(block), (NBLK, BW, TOK + HB), block_places)
 
-    kernel_t = kernel.astype(bf16).transpose(2, 1, 0).reshape(OUTER, LANES)
-    outer_t = outer_weight.T
-    up_t = up_weight.T
+    kernel_late, send = lax.optimization_barrier((kernel, send))
+    outer_t, kernel_t = call(
+        prepare, [((OUTER, OUTER), bf16), ((OUTER, LANES), bf16)], outer_weight, kernel_late, arrived=()
+    )
+    (up_t,) = call(transpose_up, [((BW, HB), bf16)], up_weight, flops=HIDE_FLOPS, arrived=())
 
     recv = exchange(send)
     send, spectrum = call(
@@ -391,6 +402,8 @@
         shared,
         up_t,
         cotangent,
+        arrived=(0, 5),
+        grant=60,
         flops=2 * mix_flops + 5 * mlp_flops,
         trans=2 * HB * TOK,
         scratch=[
@@ -398,10 +411,9 @@
             STAGE,
             TURNED,
             STAGE,
-            pltpu.VMEM((HB, BW), f32),
             pltpu.VMEM((HB, BW), bf16),
             pltpu.VMEM((HB, BW), f32),
-            pltpu.VMEM((HB, BW), f32),
+            pltpu.VMEM((HB, 2 * BW), f32),
         ],
     )
     recv = exchange(send)
@@ -419,18 +431,24 @@
     recv = exchange(send)
     grad_kernel = (grad_spec * spectrum.astype(f32)).reshape(OUTER, COLS, BW).transpose(2, 1, 0)
 
-    shared, grad_back, grad_up = call(
+    (shared,) = call(
         twiddle_terms,
-        [((NBLK, SLICE + 2 * ROWS, LANE_TILE), bf16), ((BW, TOK), bf16), ((HB, BW), f32)],
+        [((NBLK, SLICE + 2 * ROWS, LANE_TILE), bf16)],
         recv,
         first,
         later,
+        scratch=[TURNED, STAGE],
+    )
+    shared = lax.all_to_all(shared, "chan", split_axis=0, concat_axis=0, tiled=True)
+    grad_inputs, grad_up = call(
+        rows_out,
+        [((BW, TOK), f32), ((HB, BW), f32)],
+        recv,
         twiddle,
+        inner_weight,
+        direct,
+        flops=mix_flops,
         scratch=[TURNED, STAGE],
-    )
-    shared = lax.all_to_all(shared, "chan", split_axis=0, concat_axis=0, tiled=True)
-    (grad_inputs,) = call(
-        rows_out, [((BW, TOK), f32)], grad_back, inner_weight, direct, flops=mix_flops
     )
     grad_down, grad_twiddle = call(finish, [((BW, HB), f32), ((ROWS, INNER), f32)], shared)
     return grad_inputs, grad_kernel, grad_up, grad_down, grad_twiddle

time: 204 us -> 198 us (0.971)
  starting transfers between devices: 48.2 us -> 54.8 us
  waiting for transfers between devices: 31.1 us -> 27.1 us
  Pallas kernels: 28.1 us -> 25.1 us
    ppermute x2 -> x3, waiting for transfers between devices: 16.9 us -> 12 us  [gather_over_chan(): lax.ppermute(values, 'chan', step_to(step))]
    ppermute x2 -> x3, starting transfers between devices: 6.29 us -> 10.7 us  [gather_over_chan(): lax.ppermute(values, 'chan', step_to(step))]
    pallas_call x7 -> x9, Pallas kernels: 28.1 us -> 25.1 us  [call(): pl.pallas_call(kernel, out_shape=shapes, in_specs=specs, out_specs=[pl.Bl...]
    all_to_all x1, starting transfers between devices: 3.89 us -> 5.96 us  [on_device(): lax.all_to_all(shared, 'chan', split_axis=0, concat_axis=0, tiled=True)]
    unnamed x39 -> x37, local copies, waits for them, and re-layouts: 6.4 us -> 5.36 us
  transfers between devices with their start and end apart: 9 -> 10, of which waited for: 5 -> 4; matrix products, arithmetic and copies ran while one was open for 3% -> 1% of each run, Pallas kernels for 3% -> 3%
where the time goes in v5:
time: 198 us; the launch traced here: 197 us
  blocking collectives  83.4 us (42%)
  starting transfers between devices  54.8 us (28%)
  waiting for transfers between devices  27.1 us (14%)
  Pallas kernels  25.1 us (13%)
  local copies, waits for them, and re-layouts  5.63 us (3%)
    all_to_all x2, blocking collectives, exchange(): lax.all_to_all(values.reshape(NSEQ, -1, values.shape[-1]), 'seq', split_a...  83.4 us
    pallas_call x9, Pallas kernels, call(): pl.pallas_call(kernel, out_shape=shapes, in_specs=specs, out_specs=[pl.Bl...  25.1 us
    all_to_all x2, starting transfers between devices, exchange(): lax.all_to_all(values.reshape(NSEQ, -1, values.shape[-1]), 'seq', split_a...  23.5 us
    ppermute x4, starting transfers between devices, gather_over_chan(): lax.ppermute(block, 'chan', step_to(step))  14.7 us
    all_to_all x2, waiting for transfers between devices, exchange(): lax.all_to_all(values.reshape(NSEQ, -1, values.shape[-1]), 'seq', split_a...  13 us
    ppermute x3, waiting for transfers between devices, gather_over_chan(): lax.ppermute(values, 'chan', step_to(step))  12 us
    ppermute x3, starting transfers between devices, gather_over_chan(): lax.ppermute(values, 'chan', step_to(step))  10.7 us
    all_to_all x1, starting transfers between devices, on_device(): lax.all_to_all(shared, 'chan', split_axis=0, concat_axis=0, tiled=True)  5.96 us
  transfers between devices with their start and end apart: 10, of which 4 were waited for; matrix products, arithmetic and copies ran while one was open for 1% of the time, Pallas kernels for 3%

profile of v5, /device:TPU:1, one launch (start us, length us, event | category | flops | bytes accessed | tf_op | source)
XLA Modules:
  0.0 197.4 jit_solution(3619831119168810419)
XLA Ops:
  0.6 0.0 copy-start.9
  0.6 3.4 %shard_map.119 = (bf16[512,384]{1,0:T(8,128)(2,1)}, bf16[96,2048]{1,0:T(8,128)(2,1)}) custom-call(f32[96,2048]{1,0:T(8,128)} %refs_3_.1, bf16[256,256]{1,0:T(8,128)(2,1)} %refs_2_.5, f32[8,256]{1,0:T(8,128)} %refs_1_.10), custom_call_target="tpu_custom_call" | custom-call | flops 100663296 | bytes 1712128 | tf_op jit(solution)/shard_map/pallas_call | solution.py:103
  4.1 18.2 %all-to-all-start = ((bf16[64,8,384]{2,1,0:T(8,128)(2,1)}), bf16[64,8,384]{2,1,0:T(8,128)(2,1)S(1)}, u32[]{:S(2)}, u32[]{:S(2)}) async-start(bf16[64,8,384]{2,1,0:T(8,128)(2,1)} %bitcast.10), calls=%async_computation | async-start | bytes 786432 | tf_op jit(solution)/shard_map/all_to_all | solution.py:347
  22.3 0.0 copy-start.15
  22.3 0.0 copy-start.2
  22.3 0.8 copy-done.15
  23.2 7.1 %collective-permute-start.3 = (bf16[96,2432]{1,0:T(8,128)(2,1)S(1)}, bf16[96,2432]{1,0:T(8,128)(2,1)S(1)}, u32[]{:S(2)}, u32[]{:S(2)}) collective-permute-start(bf16[96,2432]{1,0:T(8,128)(2,1)S(1)} %pad_maximum_fusion.refs_5_), channel_id=1, source_target_pairs={{0,6},{1,7},{2,4},{3,5},{4,2},{5,3},{6,0},{7,1},{8,14},{9,15},{10,... | collective-permute-start | bytes 1400840 | tf_op jit(solution)/shard_map/ppermute | solution.py:286
  30.3 2.8 %collective-permute-start.2 = (bf16[96,2432]{1,0:T(8,128)(2,1)S(1)}, bf16[96,2432]{1,0:T(8,128)(2,1)}, u32[]{:S(2)}, u32[]{:S(2)}) collective-permute-start(bf16[96,2432]{1,0:T(8,128)(2,1)S(1)} %pad_maximum_fusion.refs_5_), channel_id=1, source_target_pairs={{0,3},{1,0},{2,1},{3,2},{4,7},{5,4},{6,5},{7,6},{8,11},{9,8},{10,9... | collective-permute-start | bytes 1400840 | tf_op jit(solution)/shard_map/ppermute | solution.py:286
  33.1 2.5 %collective-permute-start.1 = (bf16[96,2432]{1,0:T(8,128)(2,1)S(1)}, bf16[96,2432]{1,0:T(8,128)(2,1)}, u32[]{:S(2)}, u32[]{:S(2)}) collective-permute-start(bf16[96,2432]{1,0:T(8,128)(2,1)S(1)} %pad_maximum_fusion.refs_5_), channel_id=1, source_target_pairs={{0,1},{1,2},{2,3},{3,0},{4,5},{5,6},{6,7},{7,4},{8,9},{9,10},{10,1... | collective-permute-start | bytes 1400840 | tf_op jit(solution)/shard_map/ppermute | solution.py:286
  35.6 2.3 %collective-permute-start = (bf16[96,2432]{1,0:T(8,128)(2,1)S(1)}, bf16[96,2432]{1,0:T(8,128)(2,1)}, u32[]{:S(2)}, u32[]{:S(2)}) collective-permute-start(bf16[96,2432]{1,0:T(8,128)(2,1)S(1)} %pad_maximum_fusion.refs_5_), channel_id=1, source_target_pairs={{0,4},{1,5},{2,6},{3,7},{4,0},{5,1},{6,2},{7,3},{8,12},{9,13},{10,... | collective-permute-start | bytes 1400840 | tf_op jit(solution)/shard_map/ppermute | solution.py:286
  37.9 1.1 shard_map.120
  39.0 10.5 %all-to-all-done = bf16[64,8,384]{2,1,0:T(8,128)(2,1)S(1)} async-done(((bf16[64,8,384]{2,1,0:T(8,128)(2,1)}), bf16[64,8,384]{2,1,0:T(8,128)(2,1)S(1)}, u32[]{:S(2)}, u32[]{:S(2)}) %all-to-all-start) | async-done | bytes 393248 | tf_op jit(solution)/shard_map/all_to_all | solution.py:347
  49.5 2.6 %shard_map.121 = (bf16[512,384]{1,0:T(8,128)(2,1)}, bf16[512,384]{1,0:T(8,128)(2,1)S(1)}) custom-call(bf16[512,384]{1,0:T(8,128)(2,1)S(1)} %bitcast.7, bf16[512,512]{1,0:T(8,128)(2,1)S(1)} %copy-done, bf16[512,384]{1,0:T(8,128)(2,1)S(1)} %get-tuple-element.33.refs_2_, bf16[512,512]{1,0:T(8,128)(2,1)S(1)} %get-tuple-element.34.refs_3_), custom_call_target="tpu_custom_call" | custom-call | flops 402653184 | bytes 2621440 | tf_op jit(solution)/shard_map/pallas_call | solution.py:103
  52.1 0.0 copy-start.16
  52.1 5.4 %all-to-all-start.1 = ((bf16[64,8,384]{2,1,0:T(8,128)(2,1)}), bf16[64,8,384]{2,1,0:T(8,128)(2,1)S(1)}, u32[]{:S(2)}, u32[]{:S(2)}) async-start(bf16[64,8,384]{2,1,0:T(8,128)(2,1)} %bitcast.2), calls=%async_computation.1 | async-start | bytes 786432 | tf_op jit(solution)/shard_map/all_to_all | solution.py:347
  57.5 0.1 copy.18.refs_0_.refs_4_
  57.6 0.0 copy-start.5
  57.6 0.0 collective-permute-done.3.refs_9_
  57.6 0.0 collective-permute-done.2.refs_8_
  57.7 0.0 collective-permute-done.refs_6_
  57.7 4.4 %collective-permute-start.6 = (bf16[96,2432]{1,0:T(8,128)(2,1)}, bf16[96,2432]{1,0:T(8,128)(2,1)S(1)}, u32[]{:S(2)}, u32[]{:S(2)}) collective-permute-start(bf16[96,2432]{1,0:T(8,128)(2,1)} %collective-permute-done.refs_6_), channel_id=1, source_target_pairs={{0,3},{1,0},{2,1},{3,2},{4,7},{5,4},{6,5},{7,6},{8,11},{9,8},{10,9... | collective-permute-start | bytes 1400840 | tf_op jit(solution)/shard_map/ppermute | solution.py:289
  62.1 1.9 collective-permute-start.5
  64.0 4.4 %collective-permute-start.4 = (bf16[96,2432]{1,0:T(8,128)(2,1)S(1)}, bf16[96,2432]{1,0:T(8,128)(2,1)S(1)}, u32[]{:S(2)}, u32[]{:S(2)}) collective-permute-start(bf16[96,2432]{1,0:T(8,128)(2,1)S(1)} %collective-permute-done.3.refs_9_), channel_id=1, source_target_pairs={{0,4},{1,5},{2,6},{3,7},{4,0},{5,1},{6,2},{7,3},{8,12},{9,13},{10,... | collective-permute-start | bytes 1400840 | tf_op jit(solution)/shard_map/ppermute | solution.py:289
  68.4 0.4 shard_map.122.refs_13_
  68.8 0.0 copy-start.7
  68.8 0.6 copy-done.7
  69.4 12.0 %collective-permute-done.4.refs_10_ = bf16[96,2432]{1,0:T(8,128)(2,1)S(1)} collective-permute-done((bf16[96,2432]{1,0:T(8,128)(2,1)S(1)}, bf16[96,2432]{1,0:T(8,128)(2,1)S(1)}, u32[]{:S(2)}, u32[]{:S(2)}) %collective-permute-start.4) | collective-permute-done | bytes 466976 | tf_op jit(solution)/shard_map/ppermute | solution.py:289
  81.4 0.0 collective-permute-done.6.refs_12_
  81.4 0.8 copy-done.14
  82.2 2.5 %all-to-all-done.1 = bf16[64,8,384]{2,1,0:T(8,128)(2,1)S(1)} async-done(((bf16[64,8,384]{2,1,0:T(8,128)(2,1)}), bf16[64,8,384]{2,1,0:T(8,128)(2,1)S(1)}, u32[]{:S(2)}, u32[]{:S(2)}) %all-to-all-start.1) | async-done | bytes 393248 | tf_op jit(solution)/shard_map/all_to_all | solution.py:347
  84.7 0.8 copy-done.11
  85.5 9.4 %shard_map.123 = (bf16[64,2,2176]{2,1,0:T(2,128)(2,1)}, f32[8,256]{1,0:T(8,128)}, f32[96,2048]{1,0:T(8,128)}) custom-call(bf16[512,384]{1,0:T(8,128)(2,1)} %bitcast.9, bf16[256,256]{1,0:T(8,128)(2,1)} %refs_2_.5, f32[8,256]{1,0:T(8,128)} %refs_1_.10, f32[96,2048]{1,0:T(8,128)} %refs_3_.1, bf16[384,96]{1,0:T(8,128)(2,1)} %copy-done.5, ...), custom_call_target="tpu_custom_call" | custom-call | flops 956301312 | bytes 7340032 | tf_op jit(solution)/shard_map/pallas_call | solution.py:103
  95.0 44.5 %all_to_all.25.refs_0_ = bf16[64,2,2176]{2,1,0:T(2,128)(2,1)S(1)} all-to-all(bf16[64,2,2176]{2,1,0:T(2,128)(2,1)} %get-tuple-element.42), channel_id=1, replica_groups=mesh['seq'=64,'chan'=8] {'seq'}, dimensions={0} | all-to-all | bytes 1114112 | tf_op jit(solution)/shard_map/all_to_all | solution.py:347
  139.5 2.4 %shard_map.124 = (bf16[64,2,2176]{2,1,0:T(2,128)(2,1)S(1)}, f32[512,384]{1,0:T(8,128)S(1)}) custom-call(bf16[64,2,2176]{2,1,0:T(2,128)(2,1)S(1)} %all_to_all.25.refs_0_, bf16[512,512]{1,0:T(8,128)(2,1)S(1)} %copy-done, bf16[512,384]{1,0:T(8,128)(2,1)S(1)} %get-tuple-element.33.refs_2_, bf16[512,512]{1,0:T(8,128)(2,1)S(1)} %get-tuple-element.34.refs_3_), custom_call_target="tpu_custom_call" | custom-call | flops 402653184 | bytes 3342336 | tf_op jit(solution)/shard_map/pallas_call | solution.py:103
  141.9 0.0 copy-start.8
  141.9 38.9 %all_to_all.26.refs_0_ = bf16[64,2,2176]{2,1,0:T(2,128)(2,1)S(1)} all-to-all(bf16[64,2,2176]{2,1,0:T(2,128)(2,1)S(1)} %get-tuple-element.43), channel_id=1, replica_groups=mesh['seq'=64,'chan'=8] {'seq'}, dimensions={0} | all-to-all | bytes 1114112 | tf_op jit(solution)/shard_map/all_to_all | solution.py:347
  180.7 2.3 %shard_map.126 = bf16[8,64,128]{2,1,0:T(8,128)(2,1)} custom-call(bf16[64,2,2176]{2,1,0:T(2,128)(2,1)S(1)} %all_to_all.26.refs_0_, bf16[96,2048]{1,0:T(8,128)(2,1)S(1)} %copy-done.4, f32[8,256]{1,0:T(8,128)S(1)} %copy-done.8), custom_call_target="tpu_custom_call" | custom-call | bytes 1089536 | tf_op jit(solution)/shard_map/pallas_call | solution.py:103
  183.1 6.0 %all-to-all-start.4 = ((bf16[8,64,128]{2,1,0:T(8,128)(2,1)}), bf16[8,64,128]{2,1,0:T(8,128)(2,1)S(1)}, u32[]{:S(2)}, u32[]{:S(2)}) async-start(bf16[8,64,128]{2,1,0:T(8,128)(2,1)} %shard_map.126), calls=%async_computation.4 | async-start | bytes 262144 | tf_op jit(solution)/shard_map/all_to_all | solution.py:442
  189.0 0.1 convert_multiply_fusion
  189.1 0.3 copy.19
  189.4 0.0 copy-start.1
  189.4 0.0 copy-start.3
  189.4 0.0 copy-start.6
  189.4 1.4 copy.20
  190.8 2.5 %shard_map.125 = (f32[96,2048]{1,0:T(8,128)}, f32[384,96]{1,0:T(8,128)S(1)}) custom-call(bf16[64,2,2176]{2,1,0:T(2,128)(2,1)S(1)} %all_to_all.26.refs_0_, f32[8,256]{1,0:T(8,128)S(1)} %copy-done.6, bf16[256,256]{1,0:T(8,128)(2,1)S(1)} %copy-done.1, f32[96,2048]{1,0:T(8,128)S(1)} %copy-done.3), custom_call_target="tpu_custom_call" | custom-call | flops 100663296 | bytes 2416640 | tf_op jit(solution)/shard_map/pallas_call | solution.py:103
  193.3 0.8 copy.21
  194.1 2.1 %all-to-all-done.4.refs_0_ = bf16[8,64,128]{2,1,0:T(8,128)(2,1)S(1)} async-done(((bf16[8,64,128]{2,1,0:T(8,128)(2,1)}), bf16[8,64,128]{2,1,0:T(8,128)(2,1)S(1)}, u32[]{:S(2)}, u32[]{:S(2)}) %all-to-all-start.4) | async-done | bytes 131104 | tf_op jit(solution)/shard_map/all_to_all | solution.py:442
  196.2 1.0 shard_map.127
  (24 shorter events, 0.1 us)
Async XLA Ops:
  0.6 21.6 %copy-start.9 = (f32[96,2048]{1,0:T(8,128)S(1)}, f32[96,2048]{1,0:T(8,128)}, u32[]{:S(2)}) copy-start(f32[96,2048]{1,0:T(8,128)} %refs_14_.1) | copy-start | bytes 2359300
  4.1 45.4 %all-to-all-start = ((bf16[64,8,384]{2,1,0:T(8,128)(2,1)}), bf16[64,8,384]{2,1,0:T(8,128)(2,1)S(1)}, u32[]{:S(2)}, u32[]{:S(2)}) async-start(bf16[64,8,384]{2,1,0:T(8,128)(2,1)} %bitcast.10), calls=%async_computation | async-start | bytes 786432 | tf_op jit(solution)/shard_map/all_to_all | solution.py:347
  22.3 0.9 copy-start.15
  22.3 15.6 %copy-start.2 = (f32[96,4,512]{2,1,0:T(4,128)S(1)}, f32[96,4,512]{2,1,0:T(4,128)}, u32[]{:S(2)}) copy-start(f32[96,4,512]{2,1,0:T(4,128)} %refs_1_.6) | copy-start | bytes 2359300
  23.2 14.8 %copy-start = (bf16[512,512]{1,0:T(8,128)(2,1)S(1)}, bf16[512,512]{1,0:T(8,128)(2,1)}, u32[]{:S(2)}) copy-start(bf16[512,512]{1,0:T(8,128)(2,1)} %refs_1_.9) | copy-start | bytes 1572868
  23.2 15.8 %copy-start.10 = (bf16[96,2432]{1,0:T(8,128)(2,1)}, bf16[96,2432]{1,0:T(8,128)(2,1)S(1)}, u32[]{:S(2)}) copy-start(bf16[96,2432]{1,0:T(8,128)(2,1)S(1)} %pad_maximum_fusion.refs_5_) | copy-start | bytes 1400836
  23.2 34.4 %collective-permute-start.3 = (bf16[96,2432]{1,0:T(8,128)(2,1)S(1)}, bf16[96,2432]{1,0:T(8,128)(2,1)S(1)}, u32[]{:S(2)}, u32[]{:S(2)}) collective-permute-start(bf16[96,2432]{1,0:T(8,128)(2,1)S(1)} %pad_maximum_fusion.refs_5_), channel_id=1, source_target_pairs={{0,6},{1,7},{2,4},{3,5},{4,2},{5,3},{6,0},{7,1},{8,14},{9,15},{10,... | collective-permute-start | bytes 1400840 | tf_op jit(solution)/shard_map/ppermute | solution.py:286
  30.3 27.3 %collective-permute-start.2 = (bf16[96,2432]{1,0:T(8,128)(2,1)S(1)}, bf16[96,2432]{1,0:T(8,128)(2,1)}, u32[]{:S(2)}, u32[]{:S(2)}) collective-permute-start(bf16[96,2432]{1,0:T(8,128)(2,1)S(1)} %pad_maximum_fusion.refs_5_), channel_id=1, source_target_pairs={{0,3},{1,0},{2,1},{3,2},{4,7},{5,4},{6,5},{7,6},{8,11},{9,8},{10,9... | collective-permute-start | bytes 1400840 | tf_op jit(solution)/shard_map/ppermute | solution.py:286
  33.1 24.5 %collective-permute-start.1 = (bf16[96,2432]{1,0:T(8,128)(2,1)S(1)}, bf16[96,2432]{1,0:T(8,128)(2,1)}, u32[]{:S(2)}, u32[]{:S(2)}) collective-permute-start(bf16[96,2432]{1,0:T(8,128)(2,1)S(1)} %pad_maximum_fusion.refs_5_), channel_id=1, source_target_pairs={{0,1},{1,2},{2,3},{3,0},{4,5},{5,6},{6,7},{7,4},{8,9},{9,10},{10,1... | collective-permute-start | bytes 1400840 | tf_op jit(solution)/shard_map/ppermute | solution.py:286
  35.6 22.0 %collective-permute-start = (bf16[96,2432]{1,0:T(8,128)(2,1)S(1)}, bf16[96,2432]{1,0:T(8,128)(2,1)}, u32[]{:S(2)}, u32[]{:S(2)}) collective-permute-start(bf16[96,2432]{1,0:T(8,128)(2,1)S(1)} %pad_maximum_fusion.refs_5_), channel_id=1, source_target_pairs={{0,4},{1,5},{2,6},{3,7},{4,0},{5,1},{6,2},{7,3},{8,12},{9,13},{10,... | collective-permute-start | bytes 1400840 | tf_op jit(solution)/shard_map/ppermute | solution.py:286
  52.1 5.4 %copy-start.16 = (bf16[384,96]{0,1:T(8,128)(2,1)S(1)}, bf16[384,96]{0,1:T(8,128)(2,1)}, u32[]{:S(2)}) copy-start(bf16[384,96]{0,1:T(8,128)(2,1)} %param.14) | copy-start | bytes 221188
  52.1 32.6 %all-to-all-start.1 = ((bf16[64,8,384]{2,1,0:T(8,128)(2,1)}), bf16[64,8,384]{2,1,0:T(8,128)(2,1)S(1)}, u32[]{:S(2)}, u32[]{:S(2)}) async-start(bf16[64,8,384]{2,1,0:T(8,128)(2,1)} %bitcast.2), calls=%async_computation.1 | async-start | bytes 786432 | tf_op jit(solution)/shard_map/all_to_all | solution.py:347
  57.6 11.2 %copy-start.5 = (bf16[384,96]{1,0:T(8,128)(2,1)}, bf16[384,96]{1,0:T(8,128)(2,1)S(1)}, u32[]{:S(2)}) copy-start(bf16[384,96]{1,0:T(8,128)(2,1)S(1)} %copy.18.refs_0_.refs_4_) | copy-start | bytes 221188
  57.6 11.2 %copy-start.12 = (bf16[96,2432]{1,0:T(8,128)(2,1)}, bf16[96,2432]{1,0:T(8,128)(2,1)S(1)}, u32[]{:S(2)}) copy-start(bf16[96,2432]{1,0:T(8,128)(2,1)S(1)} %collective-permute-done.3.refs_9_) | copy-start | bytes 1400836
  57.7 23.8 %collective-permute-start.6 = (bf16[96,2432]{1,0:T(8,128)(2,1)}, bf16[96,2432]{1,0:T(8,128)(2,1)S(1)}, u32[]{:S(2)}, u32[]{:S(2)}) collective-permute-start(bf16[96,2432]{1,0:T(8,128)(2,1)} %collective-permute-done.refs_6_), channel_id=1, source_target_pairs={{0,3},{1,0},{2,1},{3,2},{4,7},{5,4},{6,5},{7,6},{8,11},{9,8},{10,9... | collective-permute-start | bytes 1400840 | tf_op jit(solution)/shard_map/ppermute | solution.py:289
  62.1 20.2 %collective-permute-start.5 = (bf16[96,2432]{1,0:T(8,128)(2,1)}, bf16[96,2432]{1,0:T(8,128)(2,1)}, u32[]{:S(2)}, u32[]{:S(2)}) collective-permute-start(bf16[96,2432]{1,0:T(8,128)(2,1)} %collective-permute-done.refs_6_), channel_id=1, source_target_pairs={{0,1},{1,2},{2,3},{3,0},{4,5},{5,6},{6,7},{7,4},{8,9},{9,10},{10,1... | collective-permute-start | bytes 1400840 | tf_op jit(solution)/shard_map/ppermute | solution.py:289
  64.0 17.4 %collective-permute-start.4 = (bf16[96,2432]{1,0:T(8,128)(2,1)S(1)}, bf16[96,2432]{1,0:T(8,128)(2,1)S(1)}, u32[]{:S(2)}, u32[]{:S(2)}) collective-permute-start(bf16[96,2432]{1,0:T(8,128)(2,1)S(1)} %collective-permute-done.3.refs_9_), channel_id=1, source_target_pairs={{0,4},{1,5},{2,6},{3,7},{4,0},{5,1},{6,2},{7,3},{8,12},{9,13},{10,... | collective-permute-start | bytes 1400840 | tf_op jit(solution)/shard_map/ppermute | solution.py:289
  68.8 0.6 copy-start.7
  81.4 0.8 copy-start.14
  82.2 2.5 %copy-start.13 = (bf16[96,2432]{1,0:T(8,128)(2,1)}, bf16[96,2432]{1,0:T(8,128)(2,1)S(1)}, u32[]{:S(2)}) copy-start(bf16[96,2432]{1,0:T(8,128)(2,1)S(1)} %collective-permute-done.6.refs_12_) | copy-start | bytes 1400836
  84.7 0.8 copy-start.11
  141.9 38.9 %copy-start.4 = (bf16[96,2048]{1,0:T(8,128)(2,1)S(1)}, bf16[96,2048]{1,0:T(8,128)(2,1)}, u32[]{:S(2)}) copy-start(bf16[96,2048]{1,0:T(8,128)(2,1)} %get-tuple-element.49.refs_1_) | copy-start | bytes 1179652
  141.9 38.9 %copy-start.8 = (f32[8,256]{1,0:T(8,128)S(1)}, f32[8,256]{1,0:T(8,128)}, u32[]{:S(2)}) copy-start(f32[8,256]{1,0:T(8,128)} %get-tuple-element.50.refs_2_) | copy-start | bytes 24580
  183.1 13.1 %all-to-all-start.4 = ((bf16[8,64,128]{2,1,0:T(8,128)(2,1)}), bf16[8,64,128]{2,1,0:T(8,128)(2,1)S(1)}, u32[]{:S(2)}, u32[]{:S(2)}) async-start(bf16[8,64,128]{2,1,0:T(8,128)(2,1)} %shard_map.126), calls=%async_computation.4 | async-start | bytes 262144 | tf_op jit(solution)/shard_map/all_to_all | solution.py:442
  189.4 1.4 copy-start.1
  189.4 1.4 copy-start.3
  189.4 1.4 copy-start.6

commit v6 on v5

--- a/solution.py
+++ b/solution.py
@@ -227,18 +227,21 @@
     send, later, direct = outs
     me = lax.axis_index("chan")
     unpack(recv(), stage)
-    for a in range(ROWS):
+
+    def forward(a):
         cols = token_columns(a)
-        scale = twiddle()[a : a + 1, :]
         back = from_message(a, turned, stage)
-        mixing = dot((back * scale).astype(bf16), w()[...])
+        mixing = dot((back * twiddle()[a : a + 1, :]).astype(bf16), w()[...])
         x = x_in()[:, cols]
         low = (x + x * mixing).astype(bf16)
         hidden = dot(up()[...], low)
         cumulative = 0.5 * (1.0 + lax.erf(hidden * (1.0 / math.sqrt(2.0))))
         density = jnp.exp(-0.5 * hidden * hidden) * (1.0 / math.sqrt(2.0 * math.pi))
         act = (hidden * cumulative).astype(bf16)
-        slope = cumulative + hidden * density
+        return back, mixing, low, act, cumulative + hidden * density
+
+    def backward(a, back, mixing, low, act, slope):
+        cols = token_columns(a)
         if a == 0:
             column = lax.broadcasted_iota(jnp.int32, (SLICE, HB), 1)
             own = column == lax.broadcasted_iota(jnp.int32, (SLICE, HB), 0) + me * SLICE
@@ -266,10 +269,16 @@
         grad_gated = cot()[:, cols] + dot(up_t()[...], grad_hidden)
         direct.ref[:, cols] = grad_gated * (1.0 + mixing)
         direct.store(slice(None), cols)
-        grad_mix = (grad_gated * x).astype(bf16)
+        grad_mix = (grad_gated * x_in()[:, cols]).astype(bf16)
         second = dot(grad_mix, w()[...], NT)
         later.ref[a : a + 1, :] = jnp.sum(second * back, axis=0, keepdims=True)
-        to_message(second * scale, a, turned_out, stage_out)
+        to_message(second * twiddle()[a : a + 1, :], a, turned_out, stage_out)
+
+    held = [forward(0)]
+    for a in range(ROWS):
+        if a + 1 < ROWS:
+            held.append(forward(a + 1))
+        backward(a, *held.pop(0))
     pack_wide(stage_out, send.ref)
     grads = [grad_up[...]]
     for p in range(NBLK):

time: 198 us -> 197 us (level)
  no operation moved by 1% of the time
where the time goes in v6:
time: 197 us
  blocking collectives  83.4 us (42%)
  starting transfers between devices  54.8 us (28%)
  waiting for transfers between devices  27.1 us (14%)
  Pallas kernels  24.3 us (12%)
  local copies, waits for them, and re-layouts  5.63 us (3%)
    all_to_all x2, blocking collectives, exchange(): lax.all_to_all(values.reshape(NSEQ, -1, values.shape[-1]), 'seq', split_a...  83.4 us
    pallas_call x9, Pallas kernels, call(): pl.pallas_call(kernel, out_shape=shapes, in_specs=specs, out_specs=[pl.Bl...  24.3 us
    all_to_all x2, starting transfers between devices, exchange(): lax.all_to_all(values.reshape(NSEQ, -1, values.shape[-1]), 'seq', split_a...  23.5 us
    ppermute x4, starting transfers between devices, gather_over_chan(): lax.ppermute(block, 'chan', step_to(step))  14.7 us
    all_to_all x2, waiting for transfers between devices, exchange(): lax.all_to_all(values.reshape(NSEQ, -1, values.shape[-1]), 'seq', split_a...  13 us
    ppermute x3, waiting for transfers between devices, gather_over_chan(): lax.ppermute(values, 'chan', step_to(step))  12 us
    ppermute x3, starting transfers between devices, gather_over_chan(): lax.ppermute(values, 'chan', step_to(step))  10.7 us
    all_to_all x1, starting transfers between devices, on_device(): lax.all_to_all(shared, 'chan', split_axis=0, concat_axis=0, tiled=True)  5.96 us
  transfers between devices with their start and end apart: 10, of which 4 were waited for; matrix products, arithmetic and copies ran while one was open for 1% of the time, Pallas kernels for 3%

profile of v6, /device:TPU:1, one launch (start us, length us, event | category | flops | bytes accessed | tf_op | source)
XLA Modules:
  0.0 196.6 jit_solution(2282217301839857290)
XLA Ops:
  0.6 0.0 copy-start.9
  0.6 3.4 %shard_map.119 = (bf16[512,384]{1,0:T(8,128)(2,1)}, bf16[96,2048]{1,0:T(8,128)(2,1)}) custom-call(f32[96,2048]{1,0:T(8,128)} %refs_3_.1, bf16[256,256]{1,0:T(8,128)(2,1)} %refs_2_.5, f32[8,256]{1,0:T(8,128)} %refs_1_.10), custom_call_target="tpu_custom_call" | custom-call | flops 100663296 | bytes 1712128 | tf_op jit(solution)/shard_map/pallas_call | solution.py:103
  4.1 18.2 %all-to-all-start = ((bf16[64,8,384]{2,1,0:T(8,128)(2,1)}), bf16[64,8,384]{2,1,0:T(8,128)(2,1)S(1)}, u32[]{:S(2)}, u32[]{:S(2)}) async-start(bf16[64,8,384]{2,1,0:T(8,128)(2,1)} %bitcast.10), calls=%async_computation | async-start | bytes 786432 | tf_op jit(solution)/shard_map/all_to_all | solution.py:356
  22.3 0.0 copy-start.15
  22.3 0.0 copy-start.2
  22.3 0.8 copy-done.15
  23.2 7.1 %collective-permute-start.3 = (bf16[96,2432]{1,0:T(8,128)(2,1)S(1)}, bf16[96,2432]{1,0:T(8,128)(2,1)S(1)}, u32[]{:S(2)}, u32[]{:S(2)}) collective-permute-start(bf16[96,2432]{1,0:T(8,128)(2,1)S(1)} %pad_maximum_fusion.refs_5_), channel_id=1, source_target_pairs={{0,6},{1,7},{2,4},{3,5},{4,2},{5,3},{6,0},{7,1},{8,14},{9,15},{10,... | collective-permute-start | bytes 1400840 | tf_op jit(solution)/shard_map/ppermute | solution.py:295
  30.3 2.8 %collective-permute-start.2 = (bf16[96,2432]{1,0:T(8,128)(2,1)S(1)}, bf16[96,2432]{1,0:T(8,128)(2,1)}, u32[]{:S(2)}, u32[]{:S(2)}) collective-permute-start(bf16[96,2432]{1,0:T(8,128)(2,1)S(1)} %pad_maximum_fusion.refs_5_), channel_id=1, source_target_pairs={{0,3},{1,0},{2,1},{3,2},{4,7},{5,4},{6,5},{7,6},{8,11},{9,8},{10,9... | collective-permute-start | bytes 1400840 | tf_op jit(solution)/shard_map/ppermute | solution.py:295
  33.1 2.5 %collective-permute-start.1 = (bf16[96,2432]{1,0:T(8,128)(2,1)S(1)}, bf16[96,2432]{1,0:T(8,128)(2,1)}, u32[]{:S(2)}, u32[]{:S(2)}) collective-permute-start(bf16[96,2432]{1,0:T(8,128)(2,1)S(1)} %pad_maximum_fusion.refs_5_), channel_id=1, source_target_pairs={{0,1},{1,2},{2,3},{3,0},{4,5},{5,6},{6,7},{7,4},{8,9},{9,10},{10,1... | collective-permute-start | bytes 1400840 | tf_op jit(solution)/shard_map/ppermute | solution.py:295
  35.6 2.3 %collective-permute-start = (bf16[96,2432]{1,0:T(8,128)(2,1)S(1)}, bf16[96,2432]{1,0:T(8,128)(2,1)}, u32[]{:S(2)}, u32[]{:S(2)}) collective-permute-start(bf16[96,2432]{1,0:T(8,128)(2,1)S(1)} %pad_maximum_fusion.refs_5_), channel_id=1, source_target_pairs={{0,4},{1,5},{2,6},{3,7},{4,0},{5,1},{6,2},{7,3},{8,12},{9,13},{10,... | collective-permute-start | bytes 1400840 | tf_op jit(solution)/shard_map/ppermute | solution.py:295
  37.9 1.1 shard_map.120
  39.0 10.5 %all-to-all-done = bf16[64,8,384]{2,1,0:T(8,128)(2,1)S(1)} async-done(((bf16[64,8,384]{2,1,0:T(8,128)(2,1)}), bf16[64,8,384]{2,1,0:T(8,128)(2,1)S(1)}, u32[]{:S(2)}, u32[]{:S(2)}) %all-to-all-start) | async-done | bytes 393248 | tf_op jit(solution)/shard_map/all_to_all | solution.py:356
  49.5 2.6 %shard_map.121 = (bf16[512,384]{1,0:T(8,128)(2,1)}, bf16[512,384]{1,0:T(8,128)(2,1)S(1)}) custom-call(bf16[512,384]{1,0:T(8,128)(2,1)S(1)} %bitcast.7, bf16[512,512]{1,0:T(8,128)(2,1)S(1)} %copy-done, bf16[512,384]{1,0:T(8,128)(2,1)S(1)} %get-tuple-element.33.refs_2_, bf16[512,512]{1,0:T(8,128)(2,1)S(1)} %get-tuple-element.34.refs_3_), custom_call_target="tpu_custom_call" | custom-call | flops 402653184 | bytes 2621440 | tf_op jit(solution)/shard_map/pallas_call | solution.py:103
  52.1 0.0 copy-start.16
  52.1 5.4 %all-to-all-start.1 = ((bf16[64,8,384]{2,1,0:T(8,128)(2,1)}), bf16[64,8,384]{2,1,0:T(8,128)(2,1)S(1)}, u32[]{:S(2)}, u32[]{:S(2)}) async-start(bf16[64,8,384]{2,1,0:T(8,128)(2,1)} %bitcast.2), calls=%async_computation.1 | async-start | bytes 786432 | tf_op jit(solution)/shard_map/all_to_all | solution.py:356
  57.5 0.1 copy.18.refs_0_.refs_4_
  57.6 0.0 copy-start.5
  57.6 0.0 collective-permute-done.3.refs_9_
  57.6 0.0 collective-permute-done.2.refs_8_
  57.7 0.0 collective-permute-done.refs_6_
  57.7 4.4 %collective-permute-start.6 = (bf16[96,2432]{1,0:T(8,128)(2,1)}, bf16[96,2432]{1,0:T(8,128)(2,1)S(1)}, u32[]{:S(2)}, u32[]{:S(2)}) collective-permute-start(bf16[96,2432]{1,0:T(8,128)(2,1)} %collective-permute-done.refs_6_), channel_id=1, source_target_pairs={{0,3},{1,0},{2,1},{3,2},{4,7},{5,4},{6,5},{7,6},{8,11},{9,8},{10,9... | collective-permute-start | bytes 1400840 | tf_op jit(solution)/shard_map/ppermute | solution.py:298
  62.1 1.9 collective-permute-start.5
  64.0 4.4 %collective-permute-start.4 = (bf16[96,2432]{1,0:T(8,128)(2,1)S(1)}, bf16[96,2432]{1,0:T(8,128)(2,1)S(1)}, u32[]{:S(2)}, u32[]{:S(2)}) collective-permute-start(bf16[96,2432]{1,0:T(8,128)(2,1)S(1)} %collective-permute-done.3.refs_9_), channel_id=1, source_target_pairs={{0,4},{1,5},{2,6},{3,7},{4,0},{5,1},{6,2},{7,3},{8,12},{9,13},{10,... | collective-permute-start | bytes 1400840 | tf_op jit(solution)/shard_map/ppermute | solution.py:298
  68.4 0.4 shard_map.122.refs_13_
  68.8 0.0 copy-start.7
  68.8 0.6 copy-done.7
  69.4 12.0 %collective-permute-done.4.refs_10_ = bf16[96,2432]{1,0:T(8,128)(2,1)S(1)} collective-permute-done((bf16[96,2432]{1,0:T(8,128)(2,1)S(1)}, bf16[96,2432]{1,0:T(8,128)(2,1)S(1)}, u32[]{:S(2)}, u32[]{:S(2)}) %collective-permute-start.4) | collective-permute-done | bytes 466976 | tf_op jit(solution)/shard_map/ppermute | solution.py:298
  81.4 0.0 collective-permute-done.6.refs_12_
  81.4 0.8 copy-done.14
  82.2 2.5 %all-to-all-done.1 = bf16[64,8,384]{2,1,0:T(8,128)(2,1)S(1)} async-done(((bf16[64,8,384]{2,1,0:T(8,128)(2,1)}), bf16[64,8,384]{2,1,0:T(8,128)(2,1)S(1)}, u32[]{:S(2)}, u32[]{:S(2)}) %all-to-all-start.1) | async-done | bytes 393248 | tf_op jit(solution)/shard_map/all_to_all | solution.py:356
  84.7 0.8 copy-done.11
  85.5 8.6 %shard_map.123 = (bf16[64,2,2176]{2,1,0:T(2,128)(2,1)}, f32[8,256]{1,0:T(8,128)}, f32[96,2048]{1,0:T(8,128)}) custom-call(bf16[512,384]{1,0:T(8,128)(2,1)} %bitcast.9, bf16[256,256]{1,0:T(8,128)(2,1)} %refs_2_.5, f32[8,256]{1,0:T(8,128)} %refs_1_.10, f32[96,2048]{1,0:T(8,128)} %refs_3_.1, bf16[384,96]{1,0:T(8,128)(2,1)} %copy-done.5, ...), custom_call_target="tpu_custom_call" | custom-call | flops 956301312 | bytes 7340032 | tf_op jit(solution)/shard_map/pallas_call | solution.py:103
  94.2 44.5 %all_to_all.25.refs_0_ = bf16[64,2,2176]{2,1,0:T(2,128)(2,1)S(1)} all-to-all(bf16[64,2,2176]{2,1,0:T(2,128)(2,1)} %get-tuple-element.42), channel_id=1, replica_groups=mesh['seq'=64,'chan'=8] {'seq'}, dimensions={0} | all-to-all | bytes 1114112 | tf_op jit(solution)/shard_map/all_to_all | solution.py:356
  138.7 2.4 %shard_map.124 = (bf16[64,2,2176]{2,1,0:T(2,128)(2,1)S(1)}, f32[512,384]{1,0:T(8,128)S(1)}) custom-call(bf16[64,2,2176]{2,1,0:T(2,128)(2,1)S(1)} %all_to_all.25.refs_0_, bf16[512,512]{1,0:T(8,128)(2,1)S(1)} %copy-done, bf16[512,384]{1,0:T(8,128)(2,1)S(1)} %get-tuple-element.33.refs_2_, bf16[512,512]{1,0:T(8,128)(2,1)S(1)} %get-tuple-element.34.refs_3_), custom_call_target="tpu_custom_call" | custom-call | flops 402653184 | bytes 3342336 | tf_op jit(solution)/shard_map/pallas_call | solution.py:103
  141.1 0.0 copy-start.8
  141.1 38.9 %all_to_all.26.refs_0_ = bf16[64,2,2176]{2,1,0:T(2,128)(2,1)S(1)} all-to-all(bf16[64,2,2176]{2,1,0:T(2,128)(2,1)S(1)} %get-tuple-element.43), channel_id=1, replica_groups=mesh['seq'=64,'chan'=8] {'seq'}, dimensions={0} | all-to-all | bytes 1114112 | tf_op jit(solution)/shard_map/all_to_all | solution.py:356
  179.9 2.3 %shard_map.126 = bf16[8,64,128]{2,1,0:T(8,128)(2,1)} custom-call(bf16[64,2,2176]{2,1,0:T(2,128)(2,1)S(1)} %all_to_all.26.refs_0_, bf16[96,2048]{1,0:T(8,128)(2,1)S(1)} %copy-done.4, f32[8,256]{1,0:T(8,128)S(1)} %copy-done.8), custom_call_target="tpu_custom_call" | custom-call | bytes 1089536 | tf_op jit(solution)/shard_map/pallas_call | solution.py:103
  182.3 6.0 %all-to-all-start.4 = ((bf16[8,64,128]{2,1,0:T(8,128)(2,1)}), bf16[8,64,128]{2,1,0:T(8,128)(2,1)S(1)}, u32[]{:S(2)}, u32[]{:S(2)}) async-start(bf16[8,64,128]{2,1,0:T(8,128)(2,1)} %shard_map.126), calls=%async_computation.4 | async-start | bytes 262144 | tf_op jit(solution)/shard_map/all_to_all | solution.py:451
  188.2 0.1 convert_multiply_fusion
  188.3 0.3 copy.19
  188.6 0.0 copy-start.1
  188.6 0.0 copy-start.3
  188.6 0.0 copy-start.6
  188.6 1.4 copy.20
  190.0 2.5 %shard_map.125 = (f32[96,2048]{1,0:T(8,128)}, f32[384,96]{1,0:T(8,128)S(1)}) custom-call(bf16[64,2,2176]{2,1,0:T(2,128)(2,1)S(1)} %all_to_all.26.refs_0_, f32[8,256]{1,0:T(8,128)S(1)} %copy-done.6, bf16[256,256]{1,0:T(8,128)(2,1)S(1)} %copy-done.1, f32[96,2048]{1,0:T(8,128)S(1)} %copy-done.3), custom_call_target="tpu_custom_call" | custom-call | flops 100663296 | bytes 2416640 | tf_op jit(solution)/shard_map/pallas_call | solution.py:103
  192.5 0.8 copy.21
  193.3 2.1 %all-to-all-done.4.refs_0_ = bf16[8,64,128]{2,1,0:T(8,128)(2,1)S(1)} async-done(((bf16[8,64,128]{2,1,0:T(8,128)(2,1)}), bf16[8,64,128]{2,1,0:T(8,128)(2,1)S(1)}, u32[]{:S(2)}, u32[]{:S(2)}) %all-to-all-start.4) | async-done | bytes 131104 | tf_op jit(solution)/shard_map/all_to_all | solution.py:451
  195.4 1.0 shard_map.127
  (24 shorter events, 0.1 us)
Async XLA Ops:
  0.6 21.6 %copy-start.9 = (f32[96,2048]{1,0:T(8,128)S(1)}, f32[96,2048]{1,0:T(8,128)}, u32[]{:S(2)}) copy-start(f32[96,2048]{1,0:T(8,128)} %refs_14_.1) | copy-start | bytes 2359300
  4.1 45.4 %all-to-all-start = ((bf16[64,8,384]{2,1,0:T(8,128)(2,1)}), bf16[64,8,384]{2,1,0:T(8,128)(2,1)S(1)}, u32[]{:S(2)}, u32[]{:S(2)}) async-start(bf16[64,8,384]{2,1,0:T(8,128)(2,1)} %bitcast.10), calls=%async_computation | async-start | bytes 786432 | tf_op jit(solution)/shard_map/all_to_all | solution.py:356
  22.3 0.9 copy-start.15
  22.3 15.6 %copy-start.2 = (f32[96,4,512]{2,1,0:T(4,128)S(1)}, f32[96,4,512]{2,1,0:T(4,128)}, u32[]{:S(2)}) copy-start(f32[96,4,512]{2,1,0:T(4,128)} %refs_1_.6) | copy-start | bytes 2359300
  23.2 14.8 %copy-start = (bf16[512,512]{1,0:T(8,128)(2,1)S(1)}, bf16[512,512]{1,0:T(8,128)(2,1)}, u32[]{:S(2)}) copy-start(bf16[512,512]{1,0:T(8,128)(2,1)} %refs_1_.9) | copy-start | bytes 1572868
  23.2 15.8 %copy-start.10 = (bf16[96,2432]{1,0:T(8,128)(2,1)}, bf16[96,2432]{1,0:T(8,128)(2,1)S(1)}, u32[]{:S(2)}) copy-start(bf16[96,2432]{1,0:T(8,128)(2,1)S(1)} %pad_maximum_fusion.refs_5_) | copy-start | bytes 1400836
  23.2 34.4 %collective-permute-start.3 = (bf16[96,2432]{1,0:T(8,128)(2,1)S(1)}, bf16[96,2432]{1,0:T(8,128)(2,1)S(1)}, u32[]{:S(2)}, u32[]{:S(2)}) collective-permute-start(bf16[96,2432]{1,0:T(8,128)(2,1)S(1)} %pad_maximum_fusion.refs_5_), channel_id=1, source_target_pairs={{0,6},{1,7},{2,4},{3,5},{4,2},{5,3},{6,0},{7,1},{8,14},{9,15},{10,... | collective-permute-start | bytes 1400840 | tf_op jit(solution)/shard_map/ppermute | solution.py:295
  30.3 27.3 %collective-permute-start.2 = (bf16[96,2432]{1,0:T(8,128)(2,1)S(1)}, bf16[96,2432]{1,0:T(8,128)(2,1)}, u32[]{:S(2)}, u32[]{:S(2)}) collective-permute-start(bf16[96,2432]{1,0:T(8,128)(2,1)S(1)} %pad_maximum_fusion.refs_5_), channel_id=1, source_target_pairs={{0,3},{1,0},{2,1},{3,2},{4,7},{5,4},{6,5},{7,6},{8,11},{9,8},{10,9... | collective-permute-start | bytes 1400840 | tf_op jit(solution)/shard_map/ppermute | solution.py:295
  33.1 24.5 %collective-permute-start.1 = (bf16[96,2432]{1,0:T(8,128)(2,1)S(1)}, bf16[96,2432]{1,0:T(8,128)(2,1)}, u32[]{:S(2)}, u32[]{:S(2)}) collective-permute-start(bf16[96,2432]{1,0:T(8,128)(2,1)S(1)} %pad_maximum_fusion.refs_5_), channel_id=1, source_target_pairs={{0,1},{1,2},{2,3},{3,0},{4,5},{5,6},{6,7},{7,4},{8,9},{9,10},{10,1... | collective-permute-start | bytes 1400840 | tf_op jit(solution)/shard_map/ppermute | solution.py:295
  35.6 22.0 %collective-permute-start = (bf16[96,2432]{1,0:T(8,128)(2,1)S(1)}, bf16[96,2432]{1,0:T(8,128)(2,1)}, u32[]{:S(2)}, u32[]{:S(2)}) collective-permute-start(bf16[96,2432]{1,0:T(8,128)(2,1)S(1)} %pad_maximum_fusion.refs_5_), channel_id=1, source_target_pairs={{0,4},{1,5},{2,6},{3,7},{4,0},{5,1},{6,2},{7,3},{8,12},{9,13},{10,... | collective-permute-start | bytes 1400840 | tf_op jit(solution)/shard_map/ppermute | solution.py:295
  52.1 5.4 %copy-start.16 = (bf16[384,96]{0,1:T(8,128)(2,1)S(1)}, bf16[384,96]{0,1:T(8,128)(2,1)}, u32[]{:S(2)}) copy-start(bf16[384,96]{0,1:T(8,128)(2,1)} %param.14) | copy-start | bytes 221188
  52.1 32.6 %all-to-all-start.1 = ((bf16[64,8,384]{2,1,0:T(8,128)(2,1)}), bf16[64,8,384]{2,1,0:T(8,128)(2,1)S(1)}, u32[]{:S(2)}, u32[]{:S(2)}) async-start(bf16[64,8,384]{2,1,0:T(8,128)(2,1)} %bitcast.2), calls=%async_computation.1 | async-start | bytes 786432 | tf_op jit(solution)/shard_map/all_to_all | solution.py:356
  57.6 11.2 %copy-start.5 = (bf16[384,96]{1,0:T(8,128)(2,1)}, bf16[384,96]{1,0:T(8,128)(2,1)S(1)}, u32[]{:S(2)}) copy-start(bf16[384,96]{1,0:T(8,128)(2,1)S(1)} %copy.18.refs_0_.refs_4_) | copy-start | bytes 221188
  57.6 11.2 %copy-start.12 = (bf16[96,2432]{1,0:T(8,128)(2,1)}, bf16[96,2432]{1,0:T(8,128)(2,1)S(1)}, u32[]{:S(2)}) copy-start(bf16[96,2432]{1,0:T(8,128)(2,1)S(1)} %collective-permute-done.3.refs_9_) | copy-start | bytes 1400836
  57.7 23.8 %collective-permute-start.6 = (bf16[96,2432]{1,0:T(8,128)(2,1)}, bf16[96,2432]{1,0:T(8,128)(2,1)S(1)}, u32[]{:S(2)}, u32[]{:S(2)}) collective-permute-start(bf16[96,2432]{1,0:T(8,128)(2,1)} %collective-permute-done.refs_6_), channel_id=1, source_target_pairs={{0,3},{1,0},{2,1},{3,2},{4,7},{5,4},{6,5},{7,6},{8,11},{9,8},{10,9... | collective-permute-start | bytes 1400840 | tf_op jit(solution)/shard_map/ppermute | solution.py:298
  62.1 20.2 %collective-permute-start.5 = (bf16[96,2432]{1,0:T(8,128)(2,1)}, bf16[96,2432]{1,0:T(8,128)(2,1)}, u32[]{:S(2)}, u32[]{:S(2)}) collective-permute-start(bf16[96,2432]{1,0:T(8,128)(2,1)} %collective-permute-done.refs_6_), channel_id=1, source_target_pairs={{0,1},{1,2},{2,3},{3,0},{4,5},{5,6},{6,7},{7,4},{8,9},{9,10},{10,1... | collective-permute-start | bytes 1400840 | tf_op jit(solution)/shard_map/ppermute | solution.py:298
  64.0 17.4 %collective-permute-start.4 = (bf16[96,2432]{1,0:T(8,128)(2,1)S(1)}, bf16[96,2432]{1,0:T(8,128)(2,1)S(1)}, u32[]{:S(2)}, u32[]{:S(2)}) collective-permute-start(bf16[96,2432]{1,0:T(8,128)(2,1)S(1)} %collective-permute-done.3.refs_9_), channel_id=1, source_target_pairs={{0,4},{1,5},{2,6},{3,7},{4,0},{5,1},{6,2},{7,3},{8,12},{9,13},{10,... | collective-permute-start | bytes 1400840 | tf_op jit(solution)/shard_map/ppermute | solution.py:298
  68.8 0.6 copy-start.7
  81.4 0.8 copy-start.14
  82.2 2.5 %copy-start.13 = (bf16[96,2432]{1,0:T(8,128)(2,1)}, bf16[96,2432]{1,0:T(8,128)(2,1)S(1)}, u32[]{:S(2)}) copy-start(bf16[96,2432]{1,0:T(8,128)(2,1)S(1)} %collective-permute-done.6.refs_12_) | copy-start | bytes 1400836
  84.7 0.8 copy-start.11
  141.1 38.9 %copy-start.4 = (bf16[96,2048]{1,0:T(8,128)(2,1)S(1)}, bf16[96,2048]{1,0:T(8,128)(2,1)}, u32[]{:S(2)}) copy-start(bf16[96,2048]{1,0:T(8,128)(2,1)} %get-tuple-element.49.refs_1_) | copy-start | bytes 1179652
  141.1 38.9 %copy-start.8 = (f32[8,256]{1,0:T(8,128)S(1)}, f32[8,256]{1,0:T(8,128)}, u32[]{:S(2)}) copy-start(f32[8,256]{1,0:T(8,128)} %get-tuple-element.50.refs_2_) | copy-start | bytes 24580
  182.3 13.1 %all-to-all-start.4 = ((bf16[8,64,128]{2,1,0:T(8,128)(2,1)}), bf16[8,64,128]{2,1,0:T(8,128)(2,1)S(1)}, u32[]{:S(2)}, u32[]{:S(2)}) async-start(bf16[8,64,128]{2,1,0:T(8,128)(2,1)} %shard_map.126), calls=%async_computation.4 | async-start | bytes 262144 | tf_op jit(solution)/shard_map/all_to_all | solution.py:451
  188.6 1.4 copy-start.1
  188.6 1.4 copy-start.3
  188.6 1.4 copy-start.6

commit v7 on v6

--- a/solution.py
+++ b/solution.py
@@ -412,7 +412,7 @@
         up_t,
         cotangent,
         arrived=(0, 5),
-        grant=60,
+        grant=52,
         flops=2 * mix_flops + 5 * mlp_flops,
         trans=2 * HB * TOK,
         scratch=[

time: 197 us -> 198 us (level)
  waiting for transfers between devices: 27.1 us -> 24.9 us
    unnamed x37 -> x25, local copies, waits for them, and re-layouts: 5.36 us -> 4.69 us
  transfers between devices with their start and end apart: 10 -> 10, of which waited for: 4 -> 4; matrix products, arithmetic and copies ran while one was open for 1% -> 2% of each run, Pallas kernels for 3% -> 3%
where the time goes in v7:
time: 198 us; the launch traced here: 197 us
  blocking collectives  84.3 us (43%)
  starting transfers between devices  55 us (28%)
  waiting for transfers between devices  24.9 us (13%)
  Pallas kernels  24.8 us (13%)
  local copies, waits for them, and re-layouts  6.09 us (3%)
    all_to_all x2, blocking collectives, exchange(): lax.all_to_all(values.reshape(NSEQ, -1, values.shape[-1]), 'seq', split_a...  84.3 us
    pallas_call x9, Pallas kernels, call(): pl.pallas_call(kernel, out_shape=shapes, in_specs=specs, out_specs=[pl.Bl...  24.8 us
    all_to_all x2, starting transfers between devices, exchange(): lax.all_to_all(values.reshape(NSEQ, -1, values.shape[-1]), 'seq', split_a...  23.5 us
    ppermute x4, starting transfers between devices, gather_over_chan(): lax.ppermute(block, 'chan', step_to(step))  14.7 us
    ppermute x3, waiting for transfers between devices, gather_over_chan(): lax.ppermute(values, 'chan', step_to(step))  12.9 us
    all_to_all x2, waiting for transfers between devices, exchange(): lax.all_to_all(values.reshape(NSEQ, -1, values.shape[-1]), 'seq', split_a...  11.9 us
    ppermute x3, starting transfers between devices, gather_over_chan(): lax.ppermute(values, 'chan', step_to(step))  10.8 us
    all_to_all x1, starting transfers between devices, on_device(): lax.all_to_all(shared, 'chan', split_axis=0, concat_axis=0, tiled=True)  5.97 us
  transfers between devices with their start and end apart: 10, of which 4 were waited for; matrix products, arithmetic and copies ran while one was open for 2% of the time, Pallas kernels for 3%

profile of v7, /device:TPU:1, one launch (start us, length us, event | category | flops | bytes accessed | tf_op | source)
XLA Modules:
  0.0 197.2 jit_solution(16632520350345498733)
XLA Ops:
  0.6 0.0 copy-start.6
  0.6 3.4 %shard_map.119 = (bf16[512,384]{1,0:T(8,128)(2,1)}, bf16[96,2048]{1,0:T(8,128)(2,1)}) custom-call(f32[96,2048]{1,0:T(8,128)} %refs_3_.1, bf16[256,256]{1,0:T(8,128)(2,1)} %refs_2_.5, f32[8,256]{1,0:T(8,128)} %refs_1_.10), custom_call_target="tpu_custom_call" | custom-call | flops 100663296 | bytes 1712128 | tf_op jit(solution)/shard_map/pallas_call | solution.py:103
  4.1 18.2 %all-to-all-start = ((bf16[64,8,384]{2,1,0:T(8,128)(2,1)}), bf16[64,8,384]{2,1,0:T(8,128)(2,1)S(1)}, u32[]{:S(2)}, u32[]{:S(2)}) async-start(bf16[64,8,384]{2,1,0:T(8,128)(2,1)} %bitcast.10), calls=%async_computation | async-start | bytes 786432 | tf_op jit(solution)/shard_map/all_to_all | solution.py:356
  22.3 0.0 copy-done.6
  22.3 0.0 copy-start.9
  22.3 0.0 copy-start.2
  22.3 0.8 copy-done.9
  23.2 7.1 %collective-permute-start.3 = (bf16[96,2432]{1,0:T(8,128)(2,1)S(1)}, bf16[96,2432]{1,0:T(8,128)(2,1)}, u32[]{:S(2)}, u32[]{:S(2)}) collective-permute-start(bf16[96,2432]{1,0:T(8,128)(2,1)S(1)} %pad_maximum_fusion.refs_5_), channel_id=1, source_target_pairs={{0,6},{1,7},{2,4},{3,5},{4,2},{5,3},{6,0},{7,1},{8,14},{9,15},{10,... | collective-permute-start | bytes 1400840 | tf_op jit(solution)/shard_map/ppermute | solution.py:295
  30.3 2.8 %collective-permute-start.2 = (bf16[96,2432]{1,0:T(8,128)(2,1)S(1)}, bf16[96,2432]{1,0:T(8,128)(2,1)}, u32[]{:S(2)}, u32[]{:S(2)}) collective-permute-start(bf16[96,2432]{1,0:T(8,128)(2,1)S(1)} %pad_maximum_fusion.refs_5_), channel_id=1, source_target_pairs={{0,3},{1,0},{2,1},{3,2},{4,7},{5,4},{6,5},{7,6},{8,11},{9,8},{10,9... | collective-permute-start | bytes 1400840 | tf_op jit(solution)/shard_map/ppermute | solution.py:295
  33.1 2.5 %collective-permute-start.1 = (bf16[96,2432]{1,0:T(8,128)(2,1)S(1)}, bf16[96,2432]{1,0:T(8,128)(2,1)}, u32[]{:S(2)}, u32[]{:S(2)}) collective-permute-start(bf16[96,2432]{1,0:T(8,128)(2,1)S(1)} %pad_maximum_fusion.refs_5_), channel_id=1, source_target_pairs={{0,1},{1,2},{2,3},{3,0},{4,5},{5,6},{6,7},{7,4},{8,9},{9,10},{10,1... | collective-permute-start | bytes 1400840 | tf_op jit(solution)/shard_map/ppermute | solution.py:295
  35.6 2.3 %collective-permute-start = (bf16[96,2432]{1,0:T(8,128)(2,1)S(1)}, bf16[96,2432]{1,0:T(8,128)(2,1)S(1)}, u32[]{:S(2)}, u32[]{:S(2)}) collective-permute-start(bf16[96,2432]{1,0:T(8,128)(2,1)S(1)} %pad_maximum_fusion.refs_5_), channel_id=1, source_target_pairs={{0,4},{1,5},{2,6},{3,7},{4,0},{5,1},{6,2},{7,3},{8,12},{9,13},{10,... | collective-permute-start | bytes 1400840 | tf_op jit(solution)/shard_map/ppermute | solution.py:295
  37.9 1.1 shard_map.120
  39.0 10.5 %all-to-all-done = bf16[64,8,384]{2,1,0:T(8,128)(2,1)S(1)} async-done(((bf16[64,8,384]{2,1,0:T(8,128)(2,1)}), bf16[64,8,384]{2,1,0:T(8,128)(2,1)S(1)}, u32[]{:S(2)}, u32[]{:S(2)}) %all-to-all-start) | async-done | bytes 393248 | tf_op jit(solution)/shard_map/all_to_all | solution.py:356
  49.5 2.6 %shard_map.121 = (bf16[512,384]{1,0:T(8,128)(2,1)}, bf16[512,384]{1,0:T(8,128)(2,1)S(1)}) custom-call(bf16[512,384]{1,0:T(8,128)(2,1)S(1)} %bitcast.8, bf16[512,512]{1,0:T(8,128)(2,1)S(1)} %copy-done, bf16[512,384]{1,0:T(8,128)(2,1)S(1)} %get-tuple-element.33.refs_2_, bf16[512,512]{1,0:T(8,128)(2,1)S(1)} %get-tuple-element.34.refs_3_), custom_call_target="tpu_custom_call" | custom-call | flops 402653184 | bytes 2621440 | tf_op jit(solution)/shard_map/pallas_call | solution.py:103
  52.1 0.0 copy-start.10
  52.1 5.4 %all-to-all-start.1 = ((bf16[64,8,384]{2,1,0:T(8,128)(2,1)}), bf16[64,8,384]{2,1,0:T(8,128)(2,1)S(1)}, u32[]{:S(2)}, u32[]{:S(2)}) async-start(bf16[64,8,384]{2,1,0:T(8,128)(2,1)} %bitcast.2), calls=%async_computation.1 | async-start | bytes 786432 | tf_op jit(solution)/shard_map/all_to_all | solution.py:356
  57.5 0.1 copy.18.refs_0_.refs_4_
  57.6 0.0 copy-start.1
  57.6 0.0 copy-start.5
  57.6 0.0 collective-permute-done.3.refs_9_
  57.6 0.0 collective-permute-done.2.refs_8_
  57.7 0.0 collective-permute-done.1.refs_7_
  57.7 0.0 collective-permute-done.refs_6_
  57.7 4.5 %collective-permute-start.6 = (bf16[96,2432]{1,0:T(8,128)(2,1)S(1)}, bf16[96,2432]{1,0:T(8,128)(2,1)S(1)}, u32[]{:S(2)}, u32[]{:S(2)}) collective-permute-start(bf16[96,2432]{1,0:T(8,128)(2,1)S(1)} %collective-permute-done.refs_6_), channel_id=1, source_target_pairs={{0,3},{1,0},{2,1},{3,2},{4,7},{5,4},{6,5},{7,6},{8,11},{9,8},{10,9... | collective-permute-start | bytes 1400840 | tf_op jit(solution)/shard_map/ppermute | solution.py:298
  62.2 1.9 collective-permute-start.5
  64.1 4.4 %collective-permute-start.4 = (bf16[96,2432]{1,0:T(8,128)(2,1)}, bf16[96,2432]{1,0:T(8,128)(2,1)S(1)}, u32[]{:S(2)}, u32[]{:S(2)}) collective-permute-start(bf16[96,2432]{1,0:T(8,128)(2,1)} %collective-permute-done.3.refs_9_), channel_id=1, source_target_pairs={{0,4},{1,5},{2,6},{3,7},{4,0},{5,1},{6,2},{7,3},{8,12},{9,13},{10,... | collective-permute-start | bytes 1400840 | tf_op jit(solution)/shard_map/ppermute | solution.py:298
  68.5 0.4 shard_map.122.refs_13_
  68.9 12.9 %collective-permute-done.4.refs_10_ = bf16[96,2432]{1,0:T(8,128)(2,1)S(1)} collective-permute-done((bf16[96,2432]{1,0:T(8,128)(2,1)}, bf16[96,2432]{1,0:T(8,128)(2,1)S(1)}, u32[]{:S(2)}, u32[]{:S(2)}) %collective-permute-start.4) | collective-permute-done | bytes 466976 | tf_op jit(solution)/shard_map/ppermute | solution.py:298
  81.8 0.0 collective-permute-done.6.refs_12_
  81.8 0.8 copy-done.8
  82.6 0.8 copy-done.7
  83.4 0.0 collective-permute-done.5.refs_11_
  83.4 1.3 all-to-all-done.1
  84.7 0.0 copy-done.5
  84.7 9.1 %shard_map.123 = (bf16[64,2,2176]{2,1,0:T(2,128)(2,1)}, f32[8,256]{1,0:T(8,128)S(1)}, f32[96,2048]{1,0:T(8,128)}) custom-call(bf16[512,384]{1,0:T(8,128)(2,1)S(1)} %bitcast.7, bf16[256,256]{1,0:T(8,128)(2,1)S(1)} %copy-done.1, f32[8,256]{1,0:T(8,128)S(1)} %copy-done.5, f32[96,2048]{1,0:T(8,128)} %refs_3_.1, bf16[384,96]{1,0:T(8,128)(2,1)S(1)} %copy.18.refs_0_.refs_4_, ...), custom_call_target="tpu_custom_call" | custom-call | flops 956301312 | bytes 7340032 | tf_op jit(solution)/shard_map/pallas_call | solution.py:103
  93.8 45.4 %all_to_all.25.refs_0_ = bf16[64,2,2176]{2,1,0:T(2,128)(2,1)S(1)} all-to-all(bf16[64,2,2176]{2,1,0:T(2,128)(2,1)} %get-tuple-element.42), channel_id=1, replica_groups=mesh['seq'=64,'chan'=8] {'seq'}, dimensions={0} | all-to-all | bytes 1114112 | tf_op jit(solution)/shard_map/all_to_all | solution.py:356
  139.3 2.4 %shard_map.124 = (bf16[64,2,2176]{2,1,0:T(2,128)(2,1)S(1)}, f32[512,384]{1,0:T(8,128)S(1)}) custom-call(bf16[64,2,2176]{2,1,0:T(2,128)(2,1)S(1)} %all_to_all.25.refs_0_, bf16[512,512]{1,0:T(8,128)(2,1)S(1)} %copy-done, bf16[512,384]{1,0:T(8,128)(2,1)S(1)} %get-tuple-element.33.refs_2_, bf16[512,512]{1,0:T(8,128)(2,1)S(1)} %get-tuple-element.34.refs_3_), custom_call_target="tpu_custom_call" | custom-call | flops 402653184 | bytes 3342336 | tf_op jit(solution)/shard_map/pallas_call | solution.py:103
  141.6 38.9 %all_to_all.26.refs_0_ = bf16[64,2,2176]{2,1,0:T(2,128)(2,1)S(1)} all-to-all(bf16[64,2,2176]{2,1,0:T(2,128)(2,1)S(1)} %get-tuple-element.43), channel_id=1, replica_groups=mesh['seq'=64,'chan'=8] {'seq'}, dimensions={0} | all-to-all | bytes 1114112 | tf_op jit(solution)/shard_map/all_to_all | solution.py:356
  180.5 2.3 %shard_map.126 = bf16[8,64,128]{2,1,0:T(8,128)(2,1)} custom-call(bf16[64,2,2176]{2,1,0:T(2,128)(2,1)S(1)} %all_to_all.26.refs_0_, bf16[96,2048]{1,0:T(8,128)(2,1)S(1)} %copy-done.4, f32[8,256]{1,0:T(8,128)S(1)} %get-tuple-element.50.refs_2_), custom_call_target="tpu_custom_call" | custom-call | bytes 1089536 | tf_op jit(solution)/shard_map/pallas_call | solution.py:103
  182.8 6.0 %all-to-all-start.4 = ((bf16[8,64,128]{2,1,0:T(8,128)(2,1)}), bf16[8,64,128]{2,1,0:T(8,128)(2,1)S(1)}, u32[]{:S(2)}, u32[]{:S(2)}) async-start(bf16[8,64,128]{2,1,0:T(8,128)(2,1)} %shard_map.126), calls=%async_computation.4 | async-start | bytes 262144 | tf_op jit(solution)/shard_map/all_to_all | solution.py:451
  188.8 0.9 convert_multiply_fusion
  189.8 1.4 copy.19
  191.2 0.0 copy-start.3
  191.2 1.4 copy.20
  192.6 2.5 %shard_map.125 = (f32[96,2048]{1,0:T(8,128)}, f32[384,96]{1,0:T(8,128)S(1)}) custom-call(bf16[64,2,2176]{2,1,0:T(2,128)(2,1)S(1)} %all_to_all.26.refs_0_, f32[8,256]{1,0:T(8,128)S(1)} %copy-done.5, bf16[256,256]{1,0:T(8,128)(2,1)S(1)} %copy-done.1, f32[96,2048]{1,0:T(8,128)S(1)} %copy-done.3), custom_call_target="tpu_custom_call" | custom-call | flops 100663296 | bytes 2416640 | tf_op jit(solution)/shard_map/pallas_call | solution.py:103
  195.1 0.8 copy.21
  195.9 0.1 all-to-all-done.4.refs_0_
  196.0 1.0 shard_map.127
  (12 shorter events, 0.1 us)
Async XLA Ops:
  0.6 21.6 %copy-start.6 = (f32[96,2048]{1,0:T(8,128)S(1)}, f32[96,2048]{1,0:T(8,128)}, u32[]{:S(2)}) copy-start(f32[96,2048]{1,0:T(8,128)} %refs_14_.1) | copy-start | bytes 2359300
  4.1 45.4 %all-to-all-start = ((bf16[64,8,384]{2,1,0:T(8,128)(2,1)}), bf16[64,8,384]{2,1,0:T(8,128)(2,1)S(1)}, u32[]{:S(2)}, u32[]{:S(2)}) async-start(bf16[64,8,384]{2,1,0:T(8,128)(2,1)} %bitcast.10), calls=%async_computation | async-start | bytes 786432 | tf_op jit(solution)/shard_map/all_to_all | solution.py:356
  22.3 0.9 copy-start.9
  22.3 15.6 %copy-start.2 = (f32[96,4,512]{2,1,0:T(4,128)S(1)}, f32[96,4,512]{2,1,0:T(4,128)}, u32[]{:S(2)}) copy-start(f32[96,4,512]{2,1,0:T(4,128)} %refs_1_.6) | copy-start | bytes 2359300
  23.2 14.7 %copy-start = (bf16[512,512]{1,0:T(8,128)(2,1)S(1)}, bf16[512,512]{1,0:T(8,128)(2,1)}, u32[]{:S(2)}) copy-start(bf16[512,512]{1,0:T(8,128)(2,1)} %refs_1_.9) | copy-start | bytes 1572868
  23.2 34.4 %collective-permute-start.3 = (bf16[96,2432]{1,0:T(8,128)(2,1)S(1)}, bf16[96,2432]{1,0:T(8,128)(2,1)}, u32[]{:S(2)}, u32[]{:S(2)}) collective-permute-start(bf16[96,2432]{1,0:T(8,128)(2,1)S(1)} %pad_maximum_fusion.refs_5_), channel_id=1, source_target_pairs={{0,6},{1,7},{2,4},{3,5},{4,2},{5,3},{6,0},{7,1},{8,14},{9,15},{10,... | collective-permute-start | bytes 1400840 | tf_op jit(solution)/shard_map/ppermute | solution.py:295
  30.3 27.3 %collective-permute-start.2 = (bf16[96,2432]{1,0:T(8,128)(2,1)S(1)}, bf16[96,2432]{1,0:T(8,128)(2,1)}, u32[]{:S(2)}, u32[]{:S(2)}) collective-permute-start(bf16[96,2432]{1,0:T(8,128)(2,1)S(1)} %pad_maximum_fusion.refs_5_), channel_id=1, source_target_pairs={{0,3},{1,0},{2,1},{3,2},{4,7},{5,4},{6,5},{7,6},{8,11},{9,8},{10,9... | collective-permute-start | bytes 1400840 | tf_op jit(solution)/shard_map/ppermute | solution.py:295
  33.1 24.6 %collective-permute-start.1 = (bf16[96,2432]{1,0:T(8,128)(2,1)S(1)}, bf16[96,2432]{1,0:T(8,128)(2,1)}, u32[]{:S(2)}, u32[]{:S(2)}) collective-permute-start(bf16[96,2432]{1,0:T(8,128)(2,1)S(1)} %pad_maximum_fusion.refs_5_), channel_id=1, source_target_pairs={{0,1},{1,2},{2,3},{3,0},{4,5},{5,6},{6,7},{7,4},{8,9},{9,10},{10,1... | collective-permute-start | bytes 1400840 | tf_op jit(solution)/shard_map/ppermute | solution.py:295
  35.6 22.0 %collective-permute-start = (bf16[96,2432]{1,0:T(8,128)(2,1)S(1)}, bf16[96,2432]{1,0:T(8,128)(2,1)S(1)}, u32[]{:S(2)}, u32[]{:S(2)}) collective-permute-start(bf16[96,2432]{1,0:T(8,128)(2,1)S(1)} %pad_maximum_fusion.refs_5_), channel_id=1, source_target_pairs={{0,4},{1,5},{2,6},{3,7},{4,0},{5,1},{6,2},{7,3},{8,12},{9,13},{10,... | collective-permute-start | bytes 1400840 | tf_op jit(solution)/shard_map/ppermute | solution.py:295
  52.1 5.4 %copy-start.10 = (bf16[384,96]{0,1:T(8,128)(2,1)S(1)}, bf16[384,96]{0,1:T(8,128)(2,1)}, u32[]{:S(2)}) copy-start(bf16[384,96]{0,1:T(8,128)(2,1)} %param.14) | copy-start | bytes 221188
  52.1 32.6 %all-to-all-start.1 = ((bf16[64,8,384]{2,1,0:T(8,128)(2,1)}), bf16[64,8,384]{2,1,0:T(8,128)(2,1)S(1)}, u32[]{:S(2)}, u32[]{:S(2)}) async-start(bf16[64,8,384]{2,1,0:T(8,128)(2,1)} %bitcast.2), calls=%async_computation.1 | async-start | bytes 786432 | tf_op jit(solution)/shard_map/all_to_all | solution.py:356
  57.6 27.1 %copy-start.1 = (bf16[256,256]{1,0:T(8,128)(2,1)S(1)}, bf16[256,256]{1,0:T(8,128)(2,1)}, u32[]{:S(2)}) copy-start(bf16[256,256]{1,0:T(8,128)(2,1)} %refs_2_.5) | copy-start | bytes 393220
  57.6 27.1 %copy-start.5 = (f32[8,256]{1,0:T(8,128)S(1)}, f32[8,256]{1,0:T(8,128)}, u32[]{:S(2)}) copy-start(f32[8,256]{1,0:T(8,128)} %refs_1_.10) | copy-start | bytes 24580
  57.7 24.2 %collective-permute-start.6 = (bf16[96,2432]{1,0:T(8,128)(2,1)S(1)}, bf16[96,2432]{1,0:T(8,128)(2,1)S(1)}, u32[]{:S(2)}, u32[]{:S(2)}) collective-permute-start(bf16[96,2432]{1,0:T(8,128)(2,1)S(1)} %collective-permute-done.refs_6_), channel_id=1, source_target_pairs={{0,3},{1,0},{2,1},{3,2},{4,7},{5,4},{6,5},{7,6},{8,11},{9,8},{10,9... | collective-permute-start | bytes 1400840 | tf_op jit(solution)/shard_map/ppermute | solution.py:298
  62.2 21.2 %collective-permute-start.5 = (bf16[96,2432]{1,0:T(8,128)(2,1)S(1)}, bf16[96,2432]{1,0:T(8,128)(2,1)}, u32[]{:S(2)}, u32[]{:S(2)}) collective-permute-start(bf16[96,2432]{1,0:T(8,128)(2,1)S(1)} %collective-permute-done.refs_6_), channel_id=1, source_target_pairs={{0,1},{1,2},{2,3},{3,0},{4,5},{5,6},{6,7},{7,4},{8,9},{9,10},{10,1... | collective-permute-start | bytes 1400840 | tf_op jit(solution)/shard_map/ppermute | solution.py:298
  64.1 17.7 %collective-permute-start.4 = (bf16[96,2432]{1,0:T(8,128)(2,1)}, bf16[96,2432]{1,0:T(8,128)(2,1)S(1)}, u32[]{:S(2)}, u32[]{:S(2)}) collective-permute-start(bf16[96,2432]{1,0:T(8,128)(2,1)} %collective-permute-done.3.refs_9_), channel_id=1, source_target_pairs={{0,4},{1,5},{2,6},{3,7},{4,0},{5,1},{6,2},{7,3},{8,12},{9,13},{10,... | collective-permute-start | bytes 1400840 | tf_op jit(solution)/shard_map/ppermute | solution.py:298
  81.8 0.8 copy-start.8
  82.6 0.8 copy-start.7
  141.6 38.9 %copy-start.4 = (bf16[96,2048]{1,0:T(8,128)(2,1)S(1)}, bf16[96,2048]{1,0:T(8,128)(2,1)}, u32[]{:S(2)}) copy-start(bf16[96,2048]{1,0:T(8,128)(2,1)} %get-tuple-element.49.refs_1_) | copy-start | bytes 1179652
  182.8 13.1 %all-to-all-start.4 = ((bf16[8,64,128]{2,1,0:T(8,128)(2,1)}), bf16[8,64,128]{2,1,0:T(8,128)(2,1)S(1)}, u32[]{:S(2)}, u32[]{:S(2)}) async-start(bf16[8,64,128]{2,1,0:T(8,128)(2,1)} %shard_map.126), calls=%async_computation.4 | async-start | bytes 262144 | tf_op jit(solution)/shard_map/all_to_all | solution.py:451
  191.2 1.4 copy-start.3
